TPU v7x, 512 devices: a whole 4x8x8 slice. The times are simulated.
512 devices in a mesh: samp: 16 (over z, x_hi), par: 32 (over x_lo, y, core).
Axes of the slice: x: 4 (x_hi: 2, x_lo: 2; x = x_hi * 2 + x_lo), y: 8, z: 8, core: 2. Of those that a mesh axis runs over, the one named last changes fastest.
Arguments:
- samples: bfloat16 [2048, 262144], P('samp', 'par'), may hold values from -1 to 1
- shift: float32 [2048], P('samp'), may hold values from 0.1 to 1
- panel_ids: int32 [16], replicated, may hold values from 0 to 15, each once
Outputs:
- factor_columns: float32 [2048, 256], P('samp')
Inputs may be any that keep to these rules, and one draw needn't show every extreme that they name: `panel_ids`: each block number once.
All inputs are finite; a program needn't handle non-finite values.
Results may differ from a plain program's by a relative error of at most 0.0003.
Values may be sent and summed in bfloat16 or wider, within the bound.
No kernel may reach another device: no remote copies, remote signals or barrier semaphores. Data moves between devices by JAX's collectives and lax.ppermute only.
A program may use at most 64 MiB of HBM per device.

v0:
```python
import jax
import jax.numpy as jnp
from jax import lax
from jax.sharding import PartitionSpec as P


def from_root(block, axis, source):
    block = jnp.where(lax.axis_index(axis) == source, block, jnp.zeros_like(block))
    return lax.psum(block, axis)


def fetch_panel(samples, owner):
    return from_root(samples, "samp", owner)


def partial_gram(samples, panel):
    return lax.dot_general(
        samples, panel, (((1,), (1,)), ((), ())), preferred_element_type=jnp.float32
    )


def summed_gram(samples, owner):
    return lax.psum(partial_gram(samples, fetch_panel(samples, owner)), "par")


def shift_term(shift, owner):
    square = jnp.eye(shift.shape[0], dtype=jnp.float32) * shift[:, None]
    return jnp.where(lax.axis_index("samp") == owner, square, jnp.zeros_like(square))


def solve_rows(block, matrix):
    factor = jnp.linalg.cholesky(block)
    return jax.scipy.linalg.solve_triangular(factor, matrix.T, lower=True).T


def outer_rows(left, right):
    return jnp.dot(
        left, right.T, precision=lax.Precision.HIGHEST, preferred_element_type=jnp.float32
    )


def per_device(samples, shift, panel_ids):
    first_owner = panel_ids[0]
    second_owner = panel_ids[1]
    gram_zero = summed_gram(samples, first_owner)
    gram_one = summed_gram(samples, second_owner)
    shifted_zero = gram_zero + shift_term(shift, first_owner)
    block_zero = from_root(shifted_zero, "samp", first_owner)
    column_zero = solve_rows(block_zero, shifted_zero)
    base_one = gram_one + shift_term(shift, second_owner)
    remote_rows = from_root(column_zero, "samp", second_owner)
    shifted_one = base_one - outer_rows(column_zero, remote_rows)
    block_one = from_root(shifted_one, "samp", second_owner)
    column_one = solve_rows(block_one, shifted_one)
    return jnp.concatenate([column_zero, column_one], axis=1)


def solution(mesh):
    placed = (P("samp", "par"), P("samp"), P())
    return jax.shard_map(
        per_device, mesh=mesh, in_specs=placed, out_specs=P("samp", None), check_vma=False
    )
```

profile of v0, /device:TPU:1, one launch (start us, length us, event | category | flops | bytes accessed | tf_op | source)
XLA Modules:
  0.0 957.2 jit_solution(14962061487131028092)
XLA Ops:
  6.5 0.0 all-reduce.16.cloned.1.call-start
  6.5 1.3 fusion.17
  9.2 3.8 broadcast_select_fusion
  13.0 0.0 copy-start
  13.0 0.0 all-reduce.16.cloned.1.call-update
  13.1 0.0 all-reduce.14.cloned.1.call-start
  13.1 217.6 %all-reduce.16.cloned.1.call-done = (bf16[128,8192]{1,0:T(8,128)(2,1)}, bf16[128,8192]{1,0:T(8,128)(2,1)}) async-done(((bf16[128,8192]{1,0:T(8,128)(2,1)}, bf16[128,8192]{1,0:T(8,128)(2,1)}), (bf16[128,8192]{1,0:T(8,128)(2,1)}, bf16[128,8192]{1,0:T(8,128)(2,1)})) %all-reduce.16.cloned.1.call-update) | async-done | bytes 4194320 | tf_op jit(solution)/shard_map/psum | solution.py:9
  230.7 0.0 copy-done
  230.7 0.0 copy-start.1
  230.8 3.1 convolution_bitcast_fusion.2
  233.8 0.0 copy-done.1
  233.8 0.0 copy-start.2
  233.8 1.3 convolution_bitcast_fusion.1
  235.2 0.0 all-reduce.14.cloned.1.call-update
  235.2 0.0 all-reduce.8.cloned.1.call-start
  235.2 205.9 %all-reduce.14.cloned.1.call-done = (f32[128,128]{0,1:T(8,128)}, f32[128,128]{0,1:T(8,128)}) async-done(((f32[128,128]{0,1:T(8,128)}, f32[128,128]{0,1:T(8,128)}), (f32[128,128]{0,1:T(8,128)}, f32[128,128]{0,1:T(8,128)})) %all-reduce.14.cloned.1.call-update) | async-done | bytes 131088 | tf_op jit(solution)/shard_map/psum | solution.py:23
  441.2 0.0 copy-done.2
  441.2 1.5 fusion.12
  442.7 0.0 all-reduce.8.cloned.1.call-update
  442.7 0.0 all-reduce.10.cloned.1.call-start
  442.7 147.3 %all-reduce.8.cloned.1.call-done = f32[128,128]{0,1:T(8,128)} async-done(((f32[128,128]{0,1:T(8,128)}), f32[128,128]{0,1:T(8,128)}) %all-reduce.8.cloned.1.call-update) | async-done | bytes 65552 | tf_op jit(solution)/shard_map/psum | solution.py:9
  590.0 0.9 copy.4
  591.0 0.9 fusion.10
  591.8 11.7 %cholesky.44 = f32[128,128]{1,0:T(8,128)S(1)} custom-call(f32[128,128]{1,0:T(8,128)S(1)} %fusion.10), custom_call_target="Cholesky" | custom-call | tf_op jit(solution)/shard_map/jit(cholesky)/cholesky | solution.py:32
  603.6 0.6 compare_reduce_fusion.1
  604.2 0.7 fusion
  604.9 9.8 %custom-call.6 = f32[1,128,128]{1,2,0:T(8,128)S(1)} custom-call(f32[1,128,128]{2,1,0:T(8,128)S(1)} %fusion), custom_call_target="InvertDiagBlocksLowerTriangular" | custom-call | tf_op jit(solution)/shard_map/jit(_solve_triangular)/triangular_solve | solution.py:33
  614.7 1.8 broadcast_select_fusion.2
  616.4 0.0 all-reduce.10.cloned.1.call-update
  616.5 0.2 all-reduce.12.cloned.1.call-start
  616.7 152.5 %all-reduce.10.cloned.1.call-done = f32[128,128]{0,1:T(8,128)} async-done(((f32[128,128]{0,1:T(8,128)}), f32[128,128]{0,1:T(8,128)}) %all-reduce.10.cloned.1.call-update) | async-done | bytes 65552 | tf_op jit(solution)/shard_map/psum | solution.py:9
  769.2 1.8 broadcast_select_fusion.3
  771.0 0.0 all-reduce.12.cloned.1.call-update
  771.1 153.9 %all-reduce.12.cloned.1.call-done = f32[128,128]{0,1:T(8,128)} async-done(((f32[128,128]{0,1:T(8,128)}), f32[128,128]{0,1:T(8,128)}) %all-reduce.12.cloned.1.call-update) | async-done | bytes 65552 | tf_op jit(solution)/shard_map/psum | solution.py:9
  924.9 0.9 copy.6
  925.9 0.9 fusion.6
  926.7 11.7 %cholesky.55 = f32[128,128]{1,0:T(8,128)S(1)} custom-call(f32[128,128]{1,0:T(8,128)S(1)} %fusion.6), custom_call_target="Cholesky" | custom-call | tf_op jit(solution)/shard_map/jit(cholesky)/cholesky | solution.py:32
  938.5 0.6 compare_reduce_fusion
  939.1 0.7 fusion.1
  939.8 9.8 %custom-call.7 = f32[1,128,128]{1,2,0:T(8,128)S(1)} custom-call(f32[1,128,128]{2,1,0:T(8,128)S(1)} %fusion.1), custom_call_target="InvertDiagBlocksLowerTriangular" | custom-call | tf_op jit(solution)/shard_map/jit(_solve_triangular)/triangular_solve | solution.py:33
  949.6 0.3 convolution_bitcast_fusion
  949.9 0.8 copy.7
  (3 shorter events, 0.1 us)
Async XLA Ops:
  6.5 224.2 %all-reduce.16.cloned.1.call-start = ((), (), s32[]{:S(2)}) async-start(), calls=%async_computation.4 | async-start | bytes 8388608 | tf_op jit(solution)/shard_map/psum | solution.py:9
  13.0 217.7 %copy-start = (bf16[128,8192]{1,0:T(8,128)(2,1)S(1)}, bf16[128,8192]{1,0:T(8,128)(2,1)}, u32[]{:S(2)}) copy-start(bf16[128,8192]{1,0:T(8,128)(2,1)} %param.6) | copy-start | bytes 6291460
  13.1 428.1 %all-reduce.14.cloned.1.call-start = ((), (), s32[]{:S(2)}) async-start(), calls=%async_computation.3 | async-start | bytes 262144 | tf_op jit(solution)/shard_map/psum | solution.py:23
  230.7 3.1 copy-start.1
  233.8 207.3 %copy-start.2 = (f32[128]{0:T(128)S(1)}, f32[128]{0:T(128)}, u32[]{:S(2)}) copy-start(f32[128]{0:T(128)} %param.7) | copy-start | bytes 1540
  235.2 354.8 %all-reduce.8.cloned.1.call-start = ((), (), s32[]{:S(2)}) async-start(), calls=%async_computation | async-start | bytes 131072 | tf_op jit(solution)/shard_map/psum | solution.py:9
  442.7 326.6 %all-reduce.10.cloned.1.call-start = ((), (), s32[]{:S(2)}) async-start(), calls=%async_computation.1 | async-start | bytes 131072 | tf_op jit(solution)/shard_map/psum | solution.py:9
  616.5 308.5 %all-reduce.12.cloned.1.call-start = ((), (), s32[]{:S(2)}) async-start(), calls=%async_computation.2 | async-start | bytes 131072 | tf_op jit(solution)/shard_map/psum | solution.py:9
Sparse Core Ops, SparseCore 0:
  13.2 217.5 all-reduce.15
  235.3 205.8 all-reduce.13
  444.3 145.6 all-reduce.7
  616.6 152.6 all-reduce.9
  772.3 152.6 all-reduce.11
where the time goes:
time: 967 us; the launch traced here: 957 us
  waiting for transfers between devices  877 us (91%)
  other arithmetic  52.7 us (5%)
  between operations  14.6 us (2%)
    psum x4, waiting for transfers between devices, from_root(): return lax.psum(block, axis)  671 us
    psum x1, waiting for transfers between devices, summed_gram(): return lax.psum(partial_gram(samples, fetch_panel(samples, owner)), 'par')  206 us
    another operation x6, other arithmetic, solve_rows(): factor = jnp.linalg.cholesky(block)  24.8 us
    another operation x4, other arithmetic, solve_rows(): return jax.scipy.linalg.solve_triangular(factor, matrix.T, lower=True).T  20.9 us
  transfers between devices with their start and end apart: 5, of which 5 were waited for; matrix products, arithmetic and copies ran while one was open for 0% of the time, Pallas kernels for 0%

commit v1 on v0

v1 whole, which is shorter than its diff:
```python
import jax
import jax.numpy as jnp
from jax import lax
from jax.sharding import PartitionSpec as P

ROWS = 128
SAMP = 16
PAR = 32
CHIPS = PAR // 2
STRIP = ROWS // CHIPS
HIGHEST = lax.Precision.HIGHEST


def swap_cores(block):
    return lax.ppermute(block, "par", [(i, i ^ 1) for i in range(PAR)])


def rows_times(left, right):
    return lax.dot_general(
        left, right, (((1,), (1,)), ((), ())), preferred_element_type=jnp.float32
    )


def exact_rows_times(left, right):
    return lax.dot_general(
        left, right, (((1,), (1,)), ((), ())),
        precision=HIGHEST, preferred_element_type=jnp.float32,
    )


def solve_rows(block, matrix):
    factor = jnp.linalg.cholesky(block)
    return jax.scipy.linalg.solve_triangular(factor, matrix.T, lower=True).T


def per_device(samples, shift, panel_ids):
    width = samples.shape[1] // SAMP
    here = lax.axis_index("samp")
    place = lax.axis_index("par")
    core = place % 2
    chip = place // 2

    pieces = samples.reshape(ROWS, SAMP, width).transpose(1, 0, 2)
    pieces = lax.all_to_all(pieces, "samp", 0, 0, tiled=True)
    every = pieces.reshape(SAMP * ROWS, width)

    def partial(k):
        panel = lax.dynamic_index_in_dim(pieces, panel_ids[k], 0, keepdims=False)
        return rows_times(every, panel)

    total = partial(core) + swap_cores(partial(1 - core))

    strips = total.reshape(SAMP, CHIPS, STRIP, ROWS).transpose(1, 0, 2, 3)
    groups = [[2 * i + c for i in range(CHIPS)] for c in range(2)]
    strips = lax.all_to_all(strips, "par", 0, 0, axis_index_groups=groups, tiled=True)
    strips = strips.sum(0)

    row = chip * STRIP + jnp.arange(STRIP)
    mine = lax.dynamic_slice_in_dim(shift, chip * STRIP, STRIP, 0)
    owner = panel_ids[core] == here
    extra = jnp.where(
        (row[:, None] == jnp.arange(ROWS)[None, :]) & owner, mine[:, None], 0.0
    )
    strips = jnp.where(
        (jnp.arange(SAMP) == here)[:, None, None], strips + extra[None], strips
    )

    def rows_of(k):
        return jnp.broadcast_to(
            lax.dynamic_index_in_dim(strips, panel_ids[k], 0, keepdims=False)[None],
            strips.shape,
        )

    three = jnp.stack([strips, rows_of(0), rows_of(1)], 1)
    three = lax.all_to_all(three, "samp", 0, 0, tiled=True).sum(0)

    copies = jnp.broadcast_to(three[None], (PAR,) + three.shape)
    gathered = lax.all_to_all(copies, "par", 0, 0, tiled=True)
    gathered = gathered.reshape(CHIPS, 2, 3, STRIP, ROWS).transpose(2, 1, 0, 3, 4)
    gathered = gathered.reshape(3, 2, ROWS, ROWS)
    own, first, second = gathered[0], gathered[1], gathered[2]

    both = jnp.concatenate([own[0], second[0]], 0)
    solved = solve_rows(first[0], both)
    column_zero, remote = solved[:ROWS], solved[ROWS:]
    both = jnp.concatenate([own[1], second[1]], 0) - exact_rows_times(solved, remote)
    column_one = solve_rows(both[ROWS:], both[:ROWS])
    return jnp.concatenate([column_zero, column_one], axis=1)


def solution(mesh):
    placed = (P("samp", "par"), P("samp"), P())
    return jax.shard_map(
        per_device, mesh=mesh, in_specs=placed, out_specs=P("samp", None), check_vma=False
    )
```

time: 967 us -> 201 us (0.21)
  waiting for transfers between devices: 877 us -> 68.5 us
  blocking collectives: 0 us -> 36.7 us
  starting transfers between devices: 0.35 us -> 25.7 us
    psum x5 -> x0, waiting for transfers between devices: 877 us -> none  [the longest x4 671 us: from_root(): return lax.psum(block, axis)]
    all_to_all x0 -> x2, waiting for transfers between devices: none -> 68 us  [the longest x1 47 us: per_device(): pieces = lax.all_to_all(pieces, 'samp', 0, 0, tiled=True)]
    all_to_all x0 -> x2, blocking collectives: none -> 36.7 us  [the longest x1 22.4 us: per_device(): gathered = lax.all_to_all(copies, 'par', 0, 0, tiled=True)]
    all_to_all x0 -> x2, starting transfers between devices: none -> 20.6 us  [the longest x1 13.6 us: per_device(): pieces = lax.all_to_all(pieces, 'samp', 0, 0, tiled=True)]
  transfers between devices with their start and end apart: 5 -> 3, of which waited for: 5 -> 3; matrix products, arithmetic and copies ran while one was open for 0% -> 0% of each run, Pallas kernels for 0% -> 0%
where the time goes in v1:
time: 201 us
  waiting for transfers between devices  68.5 us (34%)
  other arithmetic  46.1 us (23%)
  blocking collectives  36.7 us (18%)
  starting transfers between devices  25.7 us (13%)
  local copies, waits for them, and re-layouts  10.3 us (5%)
  between operations  8.65 us (4%)
  matrix products  4.77 us (2%)
    all_to_all x1, waiting for transfers between devices, per_device(): pieces = lax.all_to_all(pieces, 'samp', 0, 0, tiled=True)  47 us
    another operation x6, other arithmetic, solve_rows(): factor = jnp.linalg.cholesky(block)  24.8 us
    all_to_all x1, blocking collectives, per_device(): gathered = lax.all_to_all(copies, 'par', 0, 0, tiled=True)  22.4 us
    another operation x4, other arithmetic, solve_rows(): return jax.scipy.linalg.solve_triangular(factor, matrix.T, lower=True).T  20.9 us
    all_to_all x1, waiting for transfers between devices, per_device(): lax.all_to_all(strips, 'par', 0, 0, axis_index_groups=groups, tiled=True)  20.9 us
    all_to_all x1, blocking collectives, per_device(): three = lax.all_to_all(three, 'samp', 0, 0, tiled=True).sum(0)  14.2 us
    all_to_all x1, starting transfers between devices, per_device(): pieces = lax.all_to_all(pieces, 'samp', 0, 0, tiled=True)  13.6 us
    all_to_all x1, starting transfers between devices, per_device(): lax.all_to_all(strips, 'par', 0, 0, axis_index_groups=groups, tiled=True)  6.95 us
  transfers between devices with their start and end apart: 3, of which 3 were waited for; matrix products, arithmetic and copies ran while one was open for 0% of the time, Pallas kernels for 0%

profile of v1, /device:TPU:1, one launch (start us, length us, event | category | flops | bytes accessed | tf_op | source)
XLA Modules:
  0.0 200.7 jit_solution(8570332245685763294)
XLA Ops:
  0.0 4.1 %copy.38 = bf16[128,8192]{0,1:T(8,128)(2,1)} copy(bf16[128,8192]{1,0:T(8,128)(2,1)} %param.4) | data formatting | bytes 4194304 | tf_op args[0]
  4.1 0.0 copy-start
  4.1 13.6 %all-to-all-start = ((bf16[16,128,512]{1,2,0:T(8,128)(2,1)}), bf16[16,128,512]{1,2,0:T(8,128)(2,1)}, u32[]{:S(2)}, u32[]{:S(2)}) async-start(bf16[16,128,512]{1,2,0:T(8,128)(2,1)} %bitcast.1), calls=%async_computation | async-start | bytes 4194304 | tf_op jit(solution)/shard_map/all_to_all | solution.py:44
  17.7 0.0 copy-done
  17.7 0.7 fusion.23
  20.5 47.0 %all-to-all-done = bf16[16,128,512]{1,2,0:T(8,128)(2,1)} async-done(((bf16[16,128,512]{1,2,0:T(8,128)(2,1)}), bf16[16,128,512]{1,2,0:T(8,128)(2,1)}, u32[]{:S(2)}, u32[]{:S(2)}) %all-to-all-start) | async-done | bytes 2097184 | tf_op jit(solution)/shard_map/all_to_all | solution.py:44
  67.5 2.9 %copy.40 = bf16[16,128,512]{2,1,0:T(8,128)(2,1)S(1)} copy(bf16[16,128,512]{1,2,0:T(8,128)(2,1)} %all-to-all-done) | data formatting | bytes 4194304 | tf_op jit(solution)/shard_map/all_to_all | solution.py:44
  70.4 1.7 convolution_bitcast_fusion
  72.1 5.2 %collective-permute-start = (f32[2048,128]{0,1:T(8,128)S(1)}, f32[2048,128]{0,1:T(8,128)}, u32[]{:S(2)}, u32[]{:S(2)}) collective-permute-start(f32[2048,128]{0,1:T(8,128)S(1)} %convolution_bitcast_fusion), channel_id=1, source_target_pairs={{0,1},{1,0},{2,3},{3,2},{4,5},{5,4},{6,7},{7,6},{8,9},{9,8},{10,11... | collective-permute-start | bytes 3145736 | tf_op jit(solution)/shard_map/ppermute | solution.py:15
  79.1 0.5 collective-permute-done
  79.7 2.1 %fusion = f32[2048,128]{0,1:T(8,128)S(1)} fusion(f32[2048,128]{0,1:T(8,128)} %collective-permute-done, bf16[2048,512]{1,0:T(8,128)(2,1)S(1)} %bitcast.69, bf16[16,128,512]{1,2,0:T(8,128)(2,1)} %all-to-all-done, s32[]{:T(128)S(6)} %select_n.61), kind=kOutput, calls=%fused_computation.2 | convolution fusion | flops 268697600 | bytes 4325380 | tf_op jit(solution)/shard_map/dot_general | solution.py:19
  81.8 0.3 copy.42
  82.1 0.0 copy-start.1
  82.2 1.1 copy.43
  83.2 6.9 %all-to-all-start.1 = ((f32[16,16,8,128]{3,2,1,0:T(8,128)}), f32[16,16,8,128]{3,2,1,0:T(8,128)S(1)}, u32[]{:S(2)}, u32[]{:S(2)}) async-start(f32[16,16,8,128]{3,2,1,0:T(8,128)} %copy.43), calls=%async_computation.1 | async-start | bytes 2097152 | tf_op jit(solution)/shard_map/all_to_all | solution.py:55
  93.4 0.0 copy-done.1
  93.4 0.1 dynamic_slice.32
  94.7 0.1 fusion.19
  94.8 20.9 %all-to-all-done.1 = f32[16,16,8,128]{3,2,1,0:T(8,128)S(1)} async-done(((f32[16,16,8,128]{3,2,1,0:T(8,128)}), f32[16,16,8,128]{3,2,1,0:T(8,128)S(1)}, u32[]{:S(2)}, u32[]{:S(2)}) %all-to-all-start.1) | async-done | bytes 1048608 | tf_op jit(solution)/shard_map/all_to_all | solution.py:55
  115.7 0.1 reduce_sum.20
  115.8 0.1 add_select_fusion.1
  115.9 0.1 add_select_fusion
  116.0 14.2 %all_to_all.20 = f32[16,3,8,128]{3,2,1,0:T(8,128)S(1)} all-to-all(f32[16,3,8,128]{3,2,1,0:T(8,128)S(1)} %pad_maximum_fusion), channel_id=1, replica_groups=mesh['samp'=16,'par'=32] {'samp'}, dimensions={0} | all-to-all | bytes 393216 | tf_op jit(solution)/shard_map/all_to_all | solution.py:75
  130.3 22.4 %all_to_all.21 = f32[32,3,8,128]{3,2,1,0:T(8,128)S(1)} all-to-all(f32[32,3,8,128]{3,2,1,0:T(8,128)S(1)} %broadcast_in_dim.40), channel_id=1, replica_groups=mesh['samp'=16,'par'=32] {'par'}, dimensions={0} | all-to-all | bytes 786432 | tf_op jit(solution)/shard_map/all_to_all | solution.py:78
  152.8 0.1 copy.44
  152.9 11.7 %cholesky.44 = f32[128,128]{1,0:T(8,128)S(1)} custom-call(f32[128,128]{1,0:T(8,128)S(1)} %fusion.17), custom_call_target="Cholesky" | custom-call | tf_op jit(solution)/shard_map/jit(cholesky)/cholesky | solution.py:32
  164.7 0.6 compare_reduce_fusion.1
  165.3 0.7 fusion.9
  166.0 9.8 %custom-call.10 = f32[1,128,128]{1,2,0:T(8,128)S(1)} custom-call(f32[1,128,128]{2,1,0:T(8,128)S(1)} %fusion.9), custom_call_target="InvertDiagBlocksLowerTriangular" | custom-call | tf_op jit(solution)/shard_map/jit(_solve_triangular)/triangular_solve | solution.py:33
  175.8 0.1 copy.45
  175.9 0.1 copy.46
  176.0 0.3 fusion.1
  176.3 0.3 convolution_subtract_fusion
  176.6 0.1 copy.48
  176.8 11.7 %cholesky.55 = f32[128,128]{1,0:T(8,128)S(1)} custom-call(f32[128,128]{1,0:T(8,128)S(1)} %fusion.15), custom_call_target="Cholesky" | custom-call | tf_op jit(solution)/shard_map/jit(cholesky)/cholesky | solution.py:32
  188.5 0.6 compare_reduce_fusion
  189.2 0.7 fusion.10
  189.8 9.8 %custom-call.11 = f32[1,128,128]{1,2,0:T(8,128)S(1)} custom-call(f32[1,128,128]{2,1,0:T(8,128)S(1)} %fusion.10), custom_call_target="InvertDiagBlocksLowerTriangular" | custom-call | tf_op jit(solution)/shard_map/jit(_solve_triangular)/triangular_solve | solution.py:33
  199.6 0.3 fusion.11
  199.9 0.8 copy.49
  (16 shorter events, 0.2 us)
Async XLA Ops:
  4.1 13.6 %copy-start = (s32[16]{0:T(128)S(1)}, s32[16]{0:T(128)}, u32[]{:S(2)}) copy-start(s32[16]{0:T(128)} %param.6) | copy-start | bytes 196
  4.1 63.4 %all-to-all-start = ((bf16[16,128,512]{1,2,0:T(8,128)(2,1)}), bf16[16,128,512]{1,2,0:T(8,128)(2,1)}, u32[]{:S(2)}, u32[]{:S(2)}) async-start(bf16[16,128,512]{1,2,0:T(8,128)(2,1)} %bitcast.1), calls=%async_computation | async-start | bytes 4194304 | tf_op jit(solution)/shard_map/all_to_all | solution.py:44
  72.1 7.6 %collective-permute-start = (f32[2048,128]{0,1:T(8,128)S(1)}, f32[2048,128]{0,1:T(8,128)}, u32[]{:S(2)}, u32[]{:S(2)}) collective-permute-start(f32[2048,128]{0,1:T(8,128)S(1)} %convolution_bitcast_fusion), channel_id=1, source_target_pairs={{0,1},{1,0},{2,3},{3,2},{4,5},{5,4},{6,7},{7,6},{8,9},{9,8},{10,11... | collective-permute-start | bytes 3145736 | tf_op jit(solution)/shard_map/ppermute | solution.py:15
  82.1 11.2 %copy-start.1 = (f32[128]{0:T(128)S(1)}, f32[128]{0:T(128)}, u32[]{:S(2)}) copy-start(f32[128]{0:T(128)} %param.5) | copy-start | bytes 1540
  83.2 32.5 %all-to-all-start.1 = ((f32[16,16,8,128]{3,2,1,0:T(8,128)}), f32[16,16,8,128]{3,2,1,0:T(8,128)S(1)}, u32[]{:S(2)}, u32[]{:S(2)}) async-start(f32[16,16,8,128]{3,2,1,0:T(8,128)} %copy.43), calls=%async_computation.1 | async-start | bytes 2097152 | tf_op jit(solution)/shard_map/all_to_all | solution.py:55

commit v2 on v0

v2 whole, which is shorter than its diff:
```python
import jax
import jax.numpy as jnp
from jax import lax
from jax.experimental import pallas as pl
from jax.experimental.pallas import tpu as pltpu
from jax.sharding import PartitionSpec as P

ROWS = 128
SAMP = 16
PAR = 32
CHIPS = PAR // 2
TILE = 8
TILES = ROWS // TILE
HIGHEST = lax.Precision.HIGHEST

CHIPS_BY_CORE = [[2 * x + c for x in range(CHIPS)] for c in range(2)]


def exact(left, right, contract):
    return lax.dot_general(
        left, right, (contract, ((), ())),
        precision=HIGHEST, preferred_element_type=jnp.float32,
    )


def inverse_factor(matrix):
    lane = lax.broadcasted_iota(jnp.int32, (TILE, ROWS), 1)
    sub = lax.broadcasted_iota(jnp.int32, (TILE, ROWS), 0)
    lanes = lane[:1]
    tiles = [matrix[t * TILE:(t + 1) * TILE] for t in range(TILES)]
    for at in range(TILES):
        base = at * TILE
        rows = [tiles[at][r:r + 1] for r in range(TILE)]
        pivot = [
            [jnp.broadcast_to(rows[r][:, base + c:base + c + 1], (1, ROWS)) if c >= r else None for c in range(TILE)]
            for r in range(TILE)
        ]
        inverse = [None] * TILE
        for k in range(TILE):
            inverse[k] = 1.0 / pivot[k][k]
            scaled = jnp.where(lanes == base + k, 1.0, rows[k])
            for i in range(k + 1, TILE):
                factor = pivot[k][i] * inverse[k]
                for c in range(i, TILE):
                    pivot[i][c] = pivot[i][c] - factor * pivot[k][c]
                rows[i] = jnp.where(lanes == base + k, 0.0, rows[i]) - factor * scaled
        solved = [None] * TILE
        for k in reversed(range(TILE)):
            value = jnp.where(lanes == base + k, 1.0, rows[k])
            value = jnp.where((lanes > base + k) & (lanes < base + TILE), 0.0, value)
            for c in range(k + 1, TILE):
                value = value - pivot[k][c] * solved[c]
            solved[k] = value * inverse[k]
        wide = [jnp.broadcast_to(row, (TILE, ROWS)) for row in solved]
        inside = (lane >= base) & (lane < base + TILE)
        for t in range(at + 1, TILES):
            value = jnp.where(inside, 0.0, tiles[t])
            for k in range(TILE):
                value = value - tiles[t][:, base + k:base + k + 1] * wide[k]
            tiles[t] = value
        done = jnp.broadcast_to(rows[0], (TILE, ROWS))
        for r in range(1, TILE):
            done = jnp.where(sub == r, rows[r], done)
        tiles[at] = done
    out = []
    for t in range(TILES):
        diagonal = lane == sub + t * TILE
        square = jnp.sum(jnp.where(diagonal, tiles[t], 0.0), axis=1, keepdims=True)
        lower = jnp.where(lane < sub + t * TILE, tiles[t], jnp.where(diagonal, 1.0, 0.0))
        out.append(lower * lax.rsqrt(square))
    return jnp.concatenate(out, 0)


def cut_kernel(samples_ref, pieces_ref):
    width = pieces_ref.shape[2]
    for s in range(SAMP):
        pieces_ref[s] = samples_ref[:, s * width:(s + 1) * width]


def cut(samples):
    shape = (SAMP, ROWS, samples.shape[1] // SAMP)
    return pl.pallas_call(
        cut_kernel,
        out_shape=jax.ShapeDtypeStruct(shape, samples.dtype),
        compiler_params=pltpu.CompilerParams(vmem_limit_bytes=16 << 20),
        cost_estimate=pl.CostEstimate(flops=0, bytes_accessed=4 << 20, transcendentals=0),
    )(samples)


GROUP = 4


def gram_kernel(panel_index_ref, panel_ref, pieces_ref, *rest):
    total_ref = rest[-1]
    step = pl.program_id(0)
    for i in range(GROUP):
        product = lax.dot_general(
            panel_ref[0], pieces_ref[i], (((1,), (1,)), ((), ())), preferred_element_type=jnp.float32
        ).reshape(TILES, TILE, ROWS)
        if len(rest) == 2:
            product = product + rest[0][:, i]
        total_ref[:, i] = product


def partial_gram(panel, pieces, *received):
    width = pieces.shape[2]
    part = pl.BlockSpec((TILES, GROUP, TILE, ROWS), lambda i, panel: (0, i, 0, 0))
    return pl.pallas_call(
        gram_kernel,
        out_shape=jax.ShapeDtypeStruct((TILES, SAMP, TILE, ROWS), jnp.float32),
        grid_spec=pltpu.PrefetchScalarGridSpec(
            num_scalar_prefetch=1,
            grid=(SAMP // GROUP,),
            in_specs=[
                pl.BlockSpec((1, ROWS, width), lambda i, panel: (panel[0], 0, 0)),
                pl.BlockSpec((GROUP, ROWS, width), lambda i, panel: (i, 0, 0)),
            ] + [part] * len(received),
            out_specs=part,
        ),
        compiler_params=pltpu.CompilerParams(vmem_limit_bytes=24 << 20),
        cost_estimate=pl.CostEstimate(flops=1 << 28, bytes_accessed=4 << 20, transcendentals=0),
    )(panel[None], pieces, pieces, *received)


def factor_kernel(core_ref, mine_ref, theirs_ref, out_ref):
    even = core_ref[0] == 0

    def item(k, i):
        mine = mine_ref[:, i].reshape(ROWS, ROWS)
        theirs = theirs_ref[:, i].reshape(ROWS, ROWS)
        return jnp.where(even == (k == 0), mine, theirs)

    first = inverse_factor(item(0, 1))
    remote = exact(first, item(0, 2), ((1,), (0,)))
    second = inverse_factor(item(1, 2) - exact(remote, remote, ((0,), (0,))))
    zero = exact(first, item(0, 0), ((1,), (0,)))
    rest = item(1, 0) - exact(remote, zero, ((0,), (0,)))
    out_ref[:, :ROWS] = zero.T
    out_ref[:, ROWS:] = exact(second, rest, ((1,), (0,))).T


def factor(core, mine, theirs):
    vmem = pl.BlockSpec(memory_space=pltpu.VMEM)
    return pl.pallas_call(
        factor_kernel,
        out_shape=jax.ShapeDtypeStruct((ROWS, 2 * ROWS), jnp.float32),
        in_specs=[pl.BlockSpec(memory_space=pltpu.SMEM)] + [vmem] * 2,
        out_specs=vmem,
        compiler_params=pltpu.CompilerParams(vmem_limit_bytes=16 << 20),
        cost_estimate=pl.CostEstimate(flops=64 << 20, bytes_accessed=1 << 20, transcendentals=0),
    )(core[None], mine, theirs)


def swap_cores(block):
    return lax.ppermute(block, "par", [(i, i ^ 1) for i in range(PAR)])


def over_chips(block):
    return lax.all_to_all(block, "par", 0, 0, axis_index_groups=CHIPS_BY_CORE, tiled=True)


def per_device(samples, shift, panel_ids):
    here = lax.axis_index("samp")
    place = lax.axis_index("par")
    core = lax.rem(place, 2)
    chip = lax.div(place, 2)
    mine = jnp.where(core == 0, panel_ids[0], panel_ids[1])
    theirs = jnp.where(core == 0, panel_ids[1], panel_ids[0])

    pieces = lax.all_to_all(cut(samples), "samp", 0, 0, tiled=True)

    received = swap_cores(partial_gram(theirs, pieces))
    total = partial_gram(mine, pieces, received)

    total = over_chips(total).sum(0)
    lane = lax.broadcasted_iota(jnp.int32, (SAMP, TILE, ROWS), 2)
    sub = lax.broadcasted_iota(jnp.int32, (SAMP, TILE, ROWS), 1)
    block = lax.broadcasted_iota(jnp.int32, (SAMP, TILE, ROWS), 0)
    shifted = (lane == sub + chip * TILE) & (block == here) & (mine == here)
    total = total + jnp.where(shifted, shift[None, None, :], 0.0)

    def rows_of(k):
        rows = lax.dynamic_index_in_dim(total, panel_ids[k], 0, keepdims=True)
        return jnp.broadcast_to(rows, total.shape)

    three = jnp.stack([total, rows_of(0), rows_of(1)], 1)
    three = lax.all_to_all(three, "samp", 0, 0, tiled=True).sum(0)

    gathered = over_chips(jnp.broadcast_to(three[None], (CHIPS,) + three.shape))
    return factor(core, gathered, swap_cores(gathered))


def solution(mesh):
    placed = (P("samp", "par"), P("samp"), P())
    return jax.shard_map(
        per_device, mesh=mesh, in_specs=placed, out_specs=P("samp", None), check_vma=False
    )
```

time: 967 us -> 159 us (0.16)
  waiting for transfers between devices: 877 us -> 71.5 us
  other arithmetic: 52.7 us -> 0.28 us
  starting transfers between devices: 0.35 us -> 31.6 us
  blocking collectives: 0 us -> 27.4 us
  Pallas kernels: 0 us -> 17.4 us
    psum x5 -> x0, waiting for transfers between devices: 877 us -> none  [the longest x4 671 us: from_root(): return lax.psum(block, axis)]
    all_to_all x0 -> x2, waiting for transfers between devices: none -> 69.3 us  [the longest x1 47.8 us: per_device(): pieces = lax.all_to_all(cut(samples), 'samp', 0, 0, tiled=True)]
    another operation x10 -> x1, other arithmetic: 45.7 us -> 0.02 us  [per_device(): three = jnp.stack([total, rows_of(0), rows_of(1)], 1)]
    all_to_all x0 -> x2, blocking collectives: none -> 27.4 us  [the longest x1 14.2 us: per_device(): three = lax.all_to_all(three, 'samp', 0, 0, tiled=True).sum(0)]
    all_to_all x0 -> x2, starting transfers between devices: none -> 20.6 us  [the longest x1 13.6 us: per_device(): pieces = lax.all_to_all(cut(samples), 'samp', 0, 0, tiled=True)]
    pallas_call x0 -> x4, Pallas kernels: none -> 17.4 us  [the longest x1 12.4 us: factor(): pl.pallas_call(factor_kernel, out_shape=jax.ShapeDtypeStruct((ROWS, 2 * R...]
    ppermute x0 -> x2, starting transfers between devices: none -> 10.9 us  [swap_cores(): return lax.ppermute(block, 'par', [(i, i ^ 1) for i in range(PAR)])]
  transfers between devices with their start and end apart: 5 -> 4, of which waited for: 5 -> 4; matrix products, arithmetic and copies ran while one was open for 0% -> 0% of each run, Pallas kernels for 0% -> 0%
where the time goes in v2:
time: 159 us; the launch traced here: 158 us
  waiting for transfers between devices  71.5 us (45%)
  starting transfers between devices  31.6 us (20%)
  blocking collectives  27.4 us (17%)
  Pallas kernels  17.4 us (11%)
  between operations  6.8 us (4%)
  local copies, waits for them, and re-layouts  3.57 us (2%)
    all_to_all x1, waiting for transfers between devices, per_device(): pieces = lax.all_to_all(cut(samples), 'samp', 0, 0, tiled=True)  47.8 us
    all_to_all x1, waiting for transfers between devices, over_chips(): lax.all_to_all(block, 'par', 0, 0, axis_index_groups=CHIPS_BY_CORE, tiled...  21.5 us
    all_to_all x1, blocking collectives, per_device(): three = lax.all_to_all(three, 'samp', 0, 0, tiled=True).sum(0)  14.2 us
    all_to_all x1, starting transfers between devices, per_device(): pieces = lax.all_to_all(cut(samples), 'samp', 0, 0, tiled=True)  13.6 us
    all_to_all x1, blocking collectives, over_chips(): lax.all_to_all(block, 'par', 0, 0, axis_index_groups=CHIPS_BY_CORE, tiled...  13.2 us
    pallas_call x1, Pallas kernels, factor(): pl.pallas_call(factor_kernel, out_shape=jax.ShapeDtypeStruct((ROWS, 2 * R...  12.4 us
    ppermute x2, starting transfers between devices, swap_cores(): return lax.ppermute(block, 'par', [(i, i ^ 1) for i in range(PAR)])  10.9 us
    all_to_all x1, starting transfers between devices, over_chips(): lax.all_to_all(block, 'par', 0, 0, axis_index_groups=CHIPS_BY_CORE, tiled...  7.09 us
  transfers between devices with their start and end apart: 4, of which 4 were waited for; matrix products, arithmetic and copies ran while one was open for 0% of the time, Pallas kernels for 0%

profile of v2, /device:TPU:1, one launch (start us, length us, event | category | flops | bytes accessed | tf_op | source)
XLA Modules:
  0.0 158.5 jit_solution(13425905886080322625)
XLA Ops:
  0.0 0.0 copy-start.1
  0.0 1.6 %copy-done.1 = bf16[128,8192]{1,0:T(8,128)(2,1)S(1)} copy-done((bf16[128,8192]{1,0:T(8,128)(2,1)S(1)}, bf16[128,8192]{1,0:T(8,128)(2,1)}, u32[]{:S(2)}) %copy-start.1) | copy-done | bytes 2097176
  1.6 0.1 shard_map.37
  1.7 0.0 copy-start
  1.7 1.3 copy-done
  3.1 0.0 copy-start.3
  3.1 13.6 %all-to-all-start = ((bf16[16,128,512]{2,1,0:T(8,128)(2,1)}), bf16[16,128,512]{2,1,0:T(8,128)(2,1)S(1)}, u32[]{:S(2)}, u32[]{:S(2)}) async-start(bf16[16,128,512]{2,1,0:T(8,128)(2,1)} %copy-done), calls=%async_computation | async-start | bytes 4194304 | tf_op jit(solution)/shard_map/all_to_all | solution.py:170
  16.7 0.0 copy-done.3
  16.7 0.6 fusion.4
  18.6 47.8 %all-to-all-done.panel_ref.pieces_ref = bf16[16,128,512]{2,1,0:T(8,128)(2,1)S(1)} async-done(((bf16[16,128,512]{2,1,0:T(8,128)(2,1)}), bf16[16,128,512]{2,1,0:T(8,128)(2,1)S(1)}, u32[]{:S(2)}, u32[]{:S(2)}) %all-to-all-start) | async-done | bytes 2097184 | tf_op jit(solution)/shard_map/all_to_all | solution.py:170
  66.4 2.3 %shard_map.38 = f32[16,16,8,128]{3,2,1,0:T(8,128)} custom-call(s32[1]{0:T(128)} %bitcast.4.panel_index_ref, bf16[16,128,512]{2,1,0:T(8,128)(2,1)S(1)} %all-to-all-done.panel_ref.pieces_ref, bf16[16,128,512]{2,1,0:T(8,128)(2,1)S(1)} %all-to-all-done.panel_ref.pieces_ref), custom_call_target="tpu_custom_call" | custom-call | flops 268435456 | bytes 4194304 | tf_op jit(solution)/shard_map/pallas_call | solution.py:108
  68.8 5.1 %collective-permute-start = (f32[16,16,8,128]{3,2,1,0:T(8,128)}, f32[16,16,8,128]{3,2,1,0:T(8,128)S(1)}, u32[]{:S(2)}, u32[]{:S(2)}) collective-permute-start(f32[16,16,8,128]{3,2,1,0:T(8,128)} %shard_map.38), channel_id=1, source_target_pairs={{0,1},{1,0},{2,3},{3,2},{4,5},{5,4},{6,7},{7,6},{8,9},{9,8},{10,11... | collective-permute-start | bytes 3145736 | tf_op jit(solution)/shard_map/ppermute | solution.py:155
  75.2 1.1 collective-permute-done.rest_0_
  76.4 2.4 %shard_map.39 = f32[16,16,8,128]{3,2,1,0:T(8,128)} custom-call(s32[1]{0:T(128)} %bitcast.3.panel_index_ref, bf16[16,128,512]{2,1,0:T(8,128)(2,1)S(1)} %all-to-all-done.panel_ref.pieces_ref, bf16[16,128,512]{2,1,0:T(8,128)(2,1)S(1)} %all-to-all-done.panel_ref.pieces_ref, f32[16,16,8,128]{3,2,1,0:T(8,128)S(1)} %collective-permute-done.rest_0_), custom_call_target="tpu_custom_call" | custom-call | flops 268435456 | bytes 4194304 | tf_op jit(solution)/shard_map/pallas_call | solution.py:108
  78.8 0.0 copy-start.2
  78.8 7.1 %all-to-all-start.1 = ((f32[16,16,8,128]{3,2,1,0:T(8,128)}), f32[16,16,8,128]{3,2,1,0:T(8,128)S(1)}, u32[]{:S(2)}, u32[]{:S(2)}) async-start(f32[16,16,8,128]{3,2,1,0:T(8,128)} %shard_map.39), calls=%async_computation.1 | async-start | bytes 2097152 | tf_op jit(solution)/shard_map/all_to_all | solution.py:159
  89.9 21.5 %all-to-all-done.1 = f32[16,16,8,128]{3,2,1,0:T(8,128)S(1)} async-done(((f32[16,16,8,128]{3,2,1,0:T(8,128)}), f32[16,16,8,128]{3,2,1,0:T(8,128)S(1)}, u32[]{:S(2)}, u32[]{:S(2)}) %all-to-all-start.1) | async-done | bytes 1048608 | tf_op jit(solution)/shard_map/all_to_all | solution.py:159
  111.4 0.1 reduce_sum.20
  111.5 0.0 copy-done.2
  111.5 0.1 select_add_fusion
  111.6 0.1 bitcast_add_fusion
  111.8 14.2 %all_to_all.20 = f32[16,3,8,128]{3,2,1,0:T(8,128)S(1)} all-to-all(f32[16,3,8,128]{3,2,1,0:T(8,128)S(1)} %pad_maximum_fusion), channel_id=1, replica_groups=mesh['samp'=16,'par'=32] {'samp'}, dimensions={0} | all-to-all | bytes 393216 | tf_op jit(solution)/shard_map/all_to_all | solution.py:187
  126.1 13.2 %all_to_all.21.mine_ref = f32[16,3,8,128]{3,2,1,0:T(8,128)S(1)} all-to-all(f32[16,3,8,128]{3,2,1,0:T(8,128)S(1)} %broadcast_in_dim.39), channel_id=1, replica_groups={{0,2,4,6,8,10,12,14,16,18,20,22,24,26,28,30},{1,3,5,7,9,11,13,15,17,19,..., dimensions={0} | all-to-all | bytes 393216 | tf_op jit(solution)/shard_map/all_to_all | solution.py:159
  139.2 5.8 %collective-permute-start.1 = (f32[16,3,8,128]{3,2,1,0:T(8,128)S(1)}, f32[16,3,8,128]{3,2,1,0:T(8,128)S(1)}, u32[]{:S(2)}, u32[]{:S(2)}) collective-permute-start(f32[16,3,8,128]{3,2,1,0:T(8,128)S(1)} %all_to_all.21.mine_ref), channel_id=1, source_target_pairs={{0,1},{1,0},{2,3},{3,2},{4,5},{5,4},{6,7},{7,6},{8,9},{9,8},{10,11... | collective-permute-start | bytes 589832 | tf_op jit(solution)/shard_map/ppermute | solution.py:155
  145.0 1.0 collective-permute-done.1.theirs_ref
  146.1 12.4 %shard_map.40 = f32[128,256]{1,0:T(8,128)} custom-call(s32[1]{0:T(128)} %bitcast.core_ref, f32[16,3,8,128]{3,2,1,0:T(8,128)S(1)} %all_to_all.21.mine_ref, f32[16,3,8,128]{3,2,1,0:T(8,128)S(1)} %collective-permute-done.1.theirs_ref), custom_call_target="tpu_custom_call" | custom-call | flops 67108864 | bytes 1048576 | tf_op jit(solution)/shard_map/pallas_call | solution.py:144
  (8 shorter events, 0.1 us)
Async XLA Ops:
  0.0 1.6 %copy-start.1 = (bf16[128,8192]{1,0:T(8,128)(2,1)S(1)}, bf16[128,8192]{1,0:T(8,128)(2,1)}, u32[]{:S(2)}) copy-start(bf16[128,8192]{1,0:T(8,128)(2,1)} %samples_ref.1) | copy-start | bytes 6291460
  1.7 1.4 copy-start
  3.1 13.6 %copy-start.3 = (s32[16]{0:T(128)S(1)}, s32[16]{0:T(128)}, u32[]{:S(2)}) copy-start(s32[16]{0:T(128)} %param.5) | copy-start | bytes 196
  3.1 63.3 %all-to-all-start = ((bf16[16,128,512]{2,1,0:T(8,128)(2,1)}), bf16[16,128,512]{2,1,0:T(8,128)(2,1)S(1)}, u32[]{:S(2)}, u32[]{:S(2)}) async-start(bf16[16,128,512]{2,1,0:T(8,128)(2,1)} %copy-done), calls=%async_computation | async-start | bytes 4194304 | tf_op jit(solution)/shard_map/all_to_all | solution.py:170
  68.8 7.6 %collective-permute-start = (f32[16,16,8,128]{3,2,1,0:T(8,128)}, f32[16,16,8,128]{3,2,1,0:T(8,128)S(1)}, u32[]{:S(2)}, u32[]{:S(2)}) collective-permute-start(f32[16,16,8,128]{3,2,1,0:T(8,128)} %shard_map.38), channel_id=1, source_target_pairs={{0,1},{1,0},{2,3},{3,2},{4,5},{5,4},{6,7},{7,6},{8,9},{9,8},{10,11... | collective-permute-start | bytes 3145736 | tf_op jit(solution)/shard_map/ppermute | solution.py:155
  78.8 32.7 %copy-start.2 = (f32[128]{0:T(128)S(1)}, f32[128]{0:T(128)}, u32[]{:S(2)}) copy-start(f32[128]{0:T(128)} %param.4) | copy-start | bytes 1540
  78.8 32.6 %all-to-all-start.1 = ((f32[16,16,8,128]{3,2,1,0:T(8,128)}), f32[16,16,8,128]{3,2,1,0:T(8,128)S(1)}, u32[]{:S(2)}, u32[]{:S(2)}) async-start(f32[16,16,8,128]{3,2,1,0:T(8,128)} %shard_map.39), calls=%async_computation.1 | async-start | bytes 2097152 | tf_op jit(solution)/shard_map/all_to_all | solution.py:159
  139.2 6.8 %collective-permute-start.1 = (f32[16,3,8,128]{3,2,1,0:T(8,128)S(1)}, f32[16,3,8,128]{3,2,1,0:T(8,128)S(1)}, u32[]{:S(2)}, u32[]{:S(2)}) collective-permute-start(f32[16,3,8,128]{3,2,1,0:T(8,128)S(1)} %all_to_all.21.mine_ref), channel_id=1, source_target_pairs={{0,1},{1,0},{2,3},{3,2},{4,5},{5,4},{6,7},{7,6},{8,9},{9,8},{10,11... | collective-permute-start | bytes 589832 | tf_op jit(solution)/shard_map/ppermute | solution.py:155

commit v3 on v2

v3 whole, which is shorter than its diff:
```python
import jax
import jax.numpy as jnp
from jax import lax
from jax.experimental import pallas as pl
from jax.experimental.pallas import tpu as pltpu
from jax.sharding import PartitionSpec as P

ROWS = 128
SAMP = 16
PAR = 32
CHIPS = PAR // 2
TILE = 8
TILES = ROWS // TILE
HIGHEST = lax.Precision.HIGHEST

OVER_CHIPS = [[[s * PAR + 2 * x + c for x in range(CHIPS)] for s in range(SAMP)] for c in range(2)]
OVER_SAMP = [[[s * PAR + 2 * x + c for s in range(SAMP)] for x in range(CHIPS)] for c in range(2)]
CHIPS_THEN_SAMP = OVER_CHIPS[0] + OVER_SAMP[1]
SAMP_THEN_CHIPS = OVER_SAMP[0] + OVER_CHIPS[1]
CHIPS_BY_CORE = [[2 * x + c for x in range(CHIPS)] for c in range(2)]


def exact(left, right, contract):
    return lax.dot_general(
        left, right, (contract, ((), ())),
        precision=HIGHEST, preferred_element_type=jnp.float32,
    )


def inverse_factor(matrix):
    lane = lax.broadcasted_iota(jnp.int32, (TILE, ROWS), 1)
    sub = lax.broadcasted_iota(jnp.int32, (TILE, ROWS), 0)
    lanes = lane[:1]
    tiles = [matrix[t * TILE:(t + 1) * TILE] for t in range(TILES)]
    for at in range(TILES):
        base = at * TILE
        rows = [tiles[at][r:r + 1] for r in range(TILE)]
        pivot = [
            [jnp.broadcast_to(rows[r][:, base + c:base + c + 1], (1, ROWS)) if c >= r else None for c in range(TILE)]
            for r in range(TILE)
        ]
        inverse = [None] * TILE
        for k in range(TILE):
            inverse[k] = 1.0 / pivot[k][k]
            scaled = jnp.where(lanes == base + k, 1.0, rows[k])
            for i in range(k + 1, TILE):
                factor = pivot[k][i] * inverse[k]
                for c in range(i, TILE):
                    pivot[i][c] = pivot[i][c] - factor * pivot[k][c]
                rows[i] = jnp.where(lanes == base + k, 0.0, rows[i]) - factor * scaled
        solved = [None] * TILE
        for k in reversed(range(TILE)):
            value = jnp.where(lanes == base + k, 1.0, rows[k])
            value = jnp.where((lanes > base + k) & (lanes < base + TILE), 0.0, value)
            for c in range(k + 1, TILE):
                value = value - pivot[k][c] * solved[c]
            solved[k] = value * inverse[k]
        wide = [jnp.broadcast_to(row, (TILE, ROWS)) for row in solved]
        inside = (lane >= base) & (lane < base + TILE)
        for t in range(at + 1, TILES):
            value = jnp.where(inside, 0.0, tiles[t])
            for k in range(TILE):
                value = value - tiles[t][:, base + k:base + k + 1] * wide[k]
            tiles[t] = value
        done = jnp.broadcast_to(rows[0], (TILE, ROWS))
        for r in range(1, TILE):
            done = jnp.where(sub == r, rows[r], done)
        tiles[at] = done
    out = []
    for t in range(TILES):
        diagonal = lane == sub + t * TILE
        square = jnp.sum(jnp.where(diagonal, tiles[t], 0.0), axis=1, keepdims=True)
        lower = jnp.where(lane < sub + t * TILE, tiles[t], jnp.where(diagonal, 1.0, 0.0))
        out.append(lower * lax.rsqrt(square))
    return jnp.concatenate(out, 0)


def cut_kernel(samples_ref, pieces_ref, sems):
    width = pieces_ref.shape[2]
    copies = [
        pltpu.make_async_copy(
            samples_ref.at[:, s * width:(s + 1) * width], pieces_ref.at[s], sems.at[s]
        )
        for s in range(SAMP)
    ]
    for copy in copies:
        copy.start()
    for copy in copies:
        copy.wait()


def cut(samples):
    shape = (SAMP, ROWS, samples.shape[1] // SAMP)
    return pl.pallas_call(
        cut_kernel,
        out_shape=jax.ShapeDtypeStruct(shape, samples.dtype),
        in_specs=[pl.BlockSpec(memory_space=pl.ANY)],
        out_specs=pl.BlockSpec(memory_space=pl.ANY),
        scratch_shapes=[pltpu.SemaphoreType.DMA((SAMP,))],
        cost_estimate=pl.CostEstimate(flops=0, bytes_accessed=4 << 20, transcendentals=0),
    )(samples)


GROUP = 4


def gram_kernel(order_ref, panel_ref, pieces_ref, total_ref):
    step = pl.program_id(0)
    for i in range(GROUP):
        block = step * GROUP + i
        product = lax.dot_general(
            panel_ref[0], pieces_ref[i], (((1,), (1,)), ((), ())), preferred_element_type=jnp.float32
        ).reshape(TILES, TILE, ROWS)

        @pl.when(order_ref[1] == 0)
        def _(product=product, block=block):
            total_ref[:, block] = product

        @pl.when(order_ref[1] == 1)
        def _(product=product, block=block):
            total_ref[block] = product


def partial_gram(panel, order, pieces):
    width = pieces.shape[2]
    whole = (TILES, SAMP, TILE, ROWS)
    return pl.pallas_call(
        gram_kernel,
        out_shape=jax.ShapeDtypeStruct(whole, jnp.float32),
        grid_spec=pltpu.PrefetchScalarGridSpec(
            num_scalar_prefetch=1,
            grid=(SAMP // GROUP,),
            in_specs=[
                pl.BlockSpec((1, ROWS, width), lambda i, order: (order[0], 0, 0)),
                pl.BlockSpec((GROUP, ROWS, width), lambda i, order: (i, 0, 0)),
            ],
            out_specs=pl.BlockSpec(whole, lambda i, order: (0, 0, 0, 0)),
        ),
        compiler_params=pltpu.CompilerParams(vmem_limit_bytes=24 << 20),
        cost_estimate=pl.CostEstimate(flops=1 << 28, bytes_accessed=4 << 20, transcendentals=0),
    )(jnp.stack([panel, order]), pieces, pieces)


def inverse_kernel(block_ref, inverse_ref):
    inverse_ref[...] = inverse_factor(block_ref[...])


def first_factor(block):
    return pl.pallas_call(
        inverse_kernel,
        out_shape=jax.ShapeDtypeStruct((ROWS, ROWS), jnp.float32),
        cost_estimate=pl.CostEstimate(flops=20 << 20, bytes_accessed=1 << 20, transcendentals=0),
    )(block)


def last_kernel(flag_ref, mine_ref, theirs_ref, shift_ref, inverse_ref, other_ref, out_ref):
    row = lax.broadcasted_iota(jnp.int32, (ROWS, ROWS), 0)
    column = lax.broadcasted_iota(jnp.int32, (ROWS, ROWS), 1)
    even = flag_ref[2] == 0

    def item(k, i):
        mine = mine_ref[:, i].reshape(ROWS, ROWS)
        theirs = theirs_ref[:, i].reshape(ROWS, ROWS)
        return jnp.where(even == (k == 0), mine, theirs)

    def own(k):
        add = (row == column) & (flag_ref[k] == 1)
        return item(k, 0) + jnp.where(add, shift_ref[...], 0.0)

    inverse = inverse_ref[...]
    remote = exact(inverse, item(0, 1), ((1,), (0,)))
    second = inverse_factor(other_ref[...] - exact(remote, remote, ((0,), (0,))))
    zero = exact(inverse, own(0), ((1,), (0,)))
    rest = own(1) - exact(remote, zero, ((0,), (0,)))
    out_ref[:, :ROWS] = zero.T
    out_ref[:, ROWS:] = exact(second, rest, ((1,), (0,))).T


def last_factor(flags, mine, theirs, shift, inverse, other):
    vmem = pl.BlockSpec(memory_space=pltpu.VMEM)
    return pl.pallas_call(
        last_kernel,
        out_shape=jax.ShapeDtypeStruct((ROWS, 2 * ROWS), jnp.float32),
        in_specs=[pl.BlockSpec(memory_space=pltpu.SMEM)] + [vmem] * 5,
        out_specs=vmem,
        compiler_params=pltpu.CompilerParams(vmem_limit_bytes=16 << 20),
        cost_estimate=pl.CostEstimate(flops=64 << 20, bytes_accessed=1 << 20, transcendentals=0),
    )(flags, mine, theirs, shift, inverse, other)


def flip(block, axis, bit):
    size = SAMP if axis == "samp" else PAR
    return lax.ppermute(block, axis, [(i, i ^ bit) for i in range(size)])


def per_device(samples, shift, panel_ids):
    here = lax.axis_index("samp")
    place = lax.axis_index("par")
    core = lax.rem(place, 2)
    mine = jnp.where(core == 0, panel_ids[0], panel_ids[1])
    theirs = jnp.where(core == 0, panel_ids[1], panel_ids[0])
    axes = ("samp", "par")

    pieces = lax.all_to_all(cut(samples), "samp", 0, 0, tiled=True)

    square = lax.dot_general(
        samples, samples, (((1,), (1,)), ((), ())), preferred_element_type=jnp.float32
    )
    for bit in (1, 16, 2, 4, 8):
        square = square + flip(square, "par", bit)
    square = square + jnp.eye(ROWS, dtype=jnp.float32) * shift[:, None]
    away = here ^ mine
    for bit in (1, 2, 4):
        square = jnp.where((away & (2 * bit - 1)) < bit, square, flip(square, "samp", bit))
    pieces, square = lax.optimization_barrier((pieces, square))

    sent = flip(partial_gram(theirs, 1 - core, pieces), "par", 1)
    total = partial_gram(mine, core, pieces) + sent

    total = lax.all_to_all(total, axes, 0, 0, axis_index_groups=CHIPS_THEN_SAMP, tiled=True).sum(0)
    square = jnp.where(away < 8, square, flip(square, "samp", 8))
    swapped = flip(square, "par", 1)
    total, square, swapped = lax.optimization_barrier((total, square, swapped))
    inverse = first_factor(jnp.where(core == 0, square, swapped))
    other = jnp.where(core == 0, swapped, square)

    remote = lax.dynamic_index_in_dim(total, panel_ids[1], 0, keepdims=True)
    total = jnp.stack([total, jnp.broadcast_to(remote, total.shape)], 1)
    total = lax.all_to_all(total, axes, 0, 0, axis_index_groups=SAMP_THEN_CHIPS, tiled=True).sum(0)
    total, inverse = lax.optimization_barrier((total, inverse))

    copies = jnp.broadcast_to(total[None], (CHIPS,) + total.shape)
    gathered = lax.all_to_all(copies, "par", 0, 0, axis_index_groups=CHIPS_BY_CORE, tiled=True)
    flags = jnp.stack([panel_ids[0] == here, panel_ids[1] == here, core == 1]).astype(jnp.int32)
    return last_factor(flags, gathered, flip(gathered, "par", 1), shift[None, :], inverse, other)


def solution(mesh):
    placed = (P("samp", "par"), P("samp"), P())
    return jax.shard_map(
        per_device, mesh=mesh, in_specs=placed, out_specs=P("samp", None), check_vma=False
    )
```

time: 159 us -> 230 us (1.45)
  Pallas kernels: 17.4 us -> 87.2 us
  starting transfers between devices: 31.6 us -> 86.9 us
  waiting for transfers between devices: 71.5 us -> 27.2 us
  blocking collectives: 27.4 us -> 14.6 us
  matrix products: 0 us -> 2.96 us
  other arithmetic: 0.28 us -> 2.9 us
    pallas_call x1, Pallas kernels: 0.14 us -> 64.8 us  [cut(): pl.pallas_call(cut_kernel, out_shape=jax.ShapeDtypeStruct(shape, samples....]
    ppermute x2 -> x12, starting transfers between devices: 10.9 us -> 62 us  [flip(): return lax.ppermute(block, axis, [(i, i ^ bit) for i in range(size)])]
    all_to_all x1, waiting for transfers between devices: 47.8 us -> 0.01 us  [per_device(): pieces = lax.all_to_all(cut(samples), 'samp', 0, 0, tiled=True)]
    ppermute x2 -> x12, waiting for transfers between devices: 2.2 us -> 26.9 us  [flip(): return lax.ppermute(block, axis, [(i, i ^ bit) for i in range(size)])]
    all_to_all x1 -> x2, waiting for transfers between devices: 21.5 us -> 0.24 us  [the longest x1 0.24 us: per_device(): lax.all_to_all(total, axes, 0, 0, axis_index_groups=SAMP_THEN_CHIPS, tile...]
    all_to_all x2 -> x1, blocking collectives: 27.4 us -> 14.6 us  [per_device(): lax.all_to_all(copies, 'par', 0, 0, axis_index_groups=CHIPS_BY_CORE, tile...]
    pallas_call x3 -> x4, Pallas kernels: 17.2 us -> 22.5 us  [the longest x2 8.12 us: partial_gram(): pl.pallas_call(gram_kernel, out_shape=jax.ShapeDtypeStruct(whole, jnp.flo...]
    all_to_all x1 -> x2, starting transfers between devices: 7.09 us -> 11.5 us  [the longest x1 6.92 us: per_device(): lax.all_to_all(total, axes, 0, 0, axis_index_groups=SAMP_THEN_CHIPS, tile...]
  transfers between devices with their start and end apart: 4 -> 15, of which waited for: 4 -> 10; matrix products, arithmetic and copies ran while one was open for 0% -> 2% of each run, Pallas kernels for 0% -> 5%
where the time goes in v3:
time: 230 us; the launch traced here: 229 us
  Pallas kernels  87.2 us (38%)
  starting transfers between devices  86.9 us (38%)
  waiting for transfers between devices  27.2 us (12%)
  blocking collectives  14.6 us (6%)
  between operations  5.74 us (2%)
  matrix products  2.96 us (1%)
  other arithmetic  2.9 us (1%)
    pallas_call x1, Pallas kernels, cut(): pl.pallas_call(cut_kernel, out_shape=jax.ShapeDtypeStruct(shape, samples....  64.8 us
    ppermute x12, starting transfers between devices, flip(): return lax.ppermute(block, axis, [(i, i ^ bit) for i in range(size)])  62 us
    ppermute x12, waiting for transfers between devices, flip(): return lax.ppermute(block, axis, [(i, i ^ bit) for i in range(size)])  26.9 us
    all_to_all x1, blocking collectives, per_device(): lax.all_to_all(copies, 'par', 0, 0, axis_index_groups=CHIPS_BY_CORE, tile...  14.6 us
    all_to_all x1, starting transfers between devices, per_device(): pieces = lax.all_to_all(cut(samples), 'samp', 0, 0, tiled=True)  13.4 us
    pallas_call x2, Pallas kernels, partial_gram(): pl.pallas_call(gram_kernel, out_shape=jax.ShapeDtypeStruct(whole, jnp.flo...  8.12 us
    pallas_call x1, Pallas kernels, last_factor(): pl.pallas_call(last_kernel, out_shape=jax.ShapeDtypeStruct((ROWS, 2 * ROW...  7.5 us
    all_to_all x1, starting transfers between devices, per_device(): lax.all_to_all(total, axes, 0, 0, axis_index_groups=SAMP_THEN_CHIPS, tile...  6.92 us
  transfers between devices with their start and end apart: 15, of which 10 were waited for; matrix products, arithmetic and copies ran while one was open for 2% of the time, Pallas kernels for 5%

profile of v3, /device:TPU:1, one launch (start us, length us, event | category | flops | bytes accessed | tf_op | source)
XLA Modules:
  0.0 228.9 jit_solution(209337687116109076)
XLA Ops:
  0.0 64.8 %shard_map.37 = bf16[16,128,512]{2,1,0:T(8,128)(2,1)} custom-call(bf16[128,8192]{1,0:T(8,128)(2,1)} %samples_ref.1), custom_call_target="tpu_custom_call" | custom-call | bytes 4194304 | tf_op jit(solution)/shard_map/pallas_call | solution.py:94
  64.8 13.4 %all-to-all-start = ((bf16[16,128,512]{2,1,0:T(8,128)(2,1)}), bf16[16,128,512]{2,1,0:T(8,128)(2,1)S(1)}, u32[]{:S(2)}, u32[]{:S(2)}) async-start(bf16[16,128,512]{2,1,0:T(8,128)(2,1)} %shard_map.37), calls=%async_computation | async-start | bytes 4194304 | tf_op jit(solution)/shard_map/all_to_all | solution.py:204
  78.2 0.0 copy-start.1
  78.2 0.0 copy-start.2
  78.3 3.0 %fusion.1 = f32[128,128]{1,0:T(8,128)S(1)} fusion(bf16[128,8192]{1,0:T(8,128)(2,1)} %samples_ref.1), kind=kOutput, calls=%fused_computation.14 | convolution fusion | flops 268435456 | bytes 2162688 | tf_op jit(solution)/shard_map/dot_general | solution.py:206
  81.2 2.9 %collective-permute-start = (f32[128,128]{1,0:T(8,128)S(1)}, f32[128,128]{1,0:T(8,128)S(1)}, u32[]{:S(2)}, u32[]{:S(2)}) collective-permute-start(f32[128,128]{1,0:T(8,128)S(1)} %fusion.1), channel_id=1, source_target_pairs={{0,1},{1,0},{2,3},{3,2},{4,5},{5,4},{6,7},{7,6},{8,9},{9,8},{10,11... | collective-permute-start | bytes 196616 | tf_op jit(solution)/shard_map/ppermute | solution.py:193
  84.1 0.9 collective-permute-done
  85.0 2.2 collective-permute-start.1
  87.2 3.1 %collective-permute-done.1 = f32[128,128]{1,0:T(8,128)S(1)} collective-permute-done((f32[128,128]{1,0:T(8,128)S(1)}, f32[128,128]{1,0:T(8,128)S(1)}, u32[]{:S(2)}, u32[]{:S(2)}) %collective-permute-start.1) | collective-permute-done | bytes 65568 | tf_op jit(solution)/shard_map/ppermute | solution.py:193
  90.3 3.2 %collective-permute-start.2 = (f32[128,128]{1,0:T(8,128)S(1)}, f32[128,128]{1,0:T(8,128)S(1)}, u32[]{:S(2)}, u32[]{:S(2)}) collective-permute-start(f32[128,128]{1,0:T(8,128)S(1)} %add.26), channel_id=1, source_target_pairs={{0,2},{1,3},{2,0},{3,1},{4,6},{5,7},{6,4},{7,5},{8,10},{9,11},{10,... | collective-permute-start | bytes 196616 | tf_op jit(solution)/shard_map/ppermute | solution.py:193
  93.5 2.1 collective-permute-done.2
  95.6 4.2 %collective-permute-start.3 = (f32[128,128]{1,0:T(8,128)S(1)}, f32[128,128]{1,0:T(8,128)S(1)}, u32[]{:S(2)}, u32[]{:S(2)}) collective-permute-start(f32[128,128]{1,0:T(8,128)S(1)} %add.27), channel_id=1, source_target_pairs={{0,4},{1,5},{2,6},{3,7},{4,0},{5,1},{6,2},{7,3},{8,12},{9,13},{10,... | collective-permute-start | bytes 196616 | tf_op jit(solution)/shard_map/ppermute | solution.py:193
  99.8 2.0 collective-permute-done.3
  101.8 8.2 %collective-permute-start.4 = (f32[128,128]{1,0:T(8,128)S(1)}, f32[128,128]{1,0:T(8,128)S(1)}, u32[]{:S(2)}, u32[]{:S(2)}) collective-permute-start(f32[128,128]{1,0:T(8,128)S(1)} %add.28), channel_id=1, source_target_pairs={{0,8},{1,9},{2,10},{3,11},{4,12},{5,13},{6,14},{7,15},{8,0},{9,1},... | collective-permute-start | bytes 196616 | tf_op jit(solution)/shard_map/ppermute | solution.py:193
  110.0 1.9 collective-permute-done.4
  111.9 0.1 select_add_fusion
  112.0 5.1 %collective-permute-start.5 = (f32[128,128]{1,0:T(8,128)S(1)}, f32[128,128]{1,0:T(8,128)S(1)}, u32[]{:S(2)}, u32[]{:S(2)}) collective-permute-start(f32[128,128]{1,0:T(8,128)S(1)} %select_add_fusion), channel_id=1, source_target_pairs={{0,32},{32,0},{64,96},{96,64},{128,160},{160,128},{192,224},{224,1... | collective-permute-start | bytes 196616 | tf_op jit(solution)/shard_map/ppermute | solution.py:193
  117.1 0.6 fusion
  118.9 1.7 collective-permute-done.5
  120.7 5.7 %collective-permute-start.6 = (f32[128,128]{1,0:T(8,128)S(1)}, f32[128,128]{1,0:T(8,128)S(1)}, u32[]{:S(2)}, u32[]{:S(2)}) collective-permute-start(f32[128,128]{1,0:T(8,128)S(1)} %broadcast_select_fusion.3), channel_id=1, source_target_pairs={{0,64},{32,96},{64,0},{96,32},{128,192},{160,224},{192,128},{224,1... | collective-permute-start | bytes 196616 | tf_op jit(solution)/shard_map/ppermute | solution.py:193
  127.7 0.7 collective-permute-done.6
  128.4 7.7 %collective-permute-start.7 = (f32[128,128]{1,0:T(8,128)S(1)}, f32[128,128]{1,0:T(8,128)S(1)}, u32[]{:S(2)}, u32[]{:S(2)}) collective-permute-start(f32[128,128]{1,0:T(8,128)S(1)} %broadcast_select_fusion.4), channel_id=1, source_target_pairs={{0,128},{32,160},{64,192},{96,224},{128,0},{160,32},{192,64},{224,... | collective-permute-start | bytes 196616 | tf_op jit(solution)/shard_map/ppermute | solution.py:193
  136.1 0.1 pad_add_fusion.1.order_ref
  136.2 2.0 collective-permute-done.7
  138.2 0.0 all-to-all-done.panel_ref.pieces_ref
  138.2 4.0 %shard_map.39 = f32[16,16,8,128]{3,2,1,0:T(8,128)S(1)} custom-call(s32[2]{0:T(128)S(1)} %pad_add_fusion.1.order_ref, bf16[16,128,512]{2,1,0:T(8,128)(2,1)S(1)} %all-to-all-done.panel_ref.pieces_ref, bf16[16,128,512]{2,1,0:T(8,128)(2,1)S(1)} %all-to-all-done.panel_ref.pieces_ref), custom_call_target="tpu_custom_call" | custom-call | flops 268435456 | bytes 4194304 | tf_op jit(solution)/shard_map/pallas_call | solution.py:127
  142.3 8.3 %collective-permute-start.8 = (f32[16,16,8,128]{3,2,1,0:T(8,128)S(1)}, f32[16,16,8,128]{3,2,1,0:T(8,128)S(1)}, u32[]{:S(2)}, u32[]{:S(2)}) collective-permute-start(f32[16,16,8,128]{3,2,1,0:T(8,128)S(1)} %shard_map.39), channel_id=1, source_target_pairs={{0,1},{1,0},{2,3},{3,2},{4,5},{5,4},{6,7},{7,6},{8,9},{9,8},{10,11... | collective-permute-start | bytes 3145736 | tf_op jit(solution)/shard_map/ppermute | solution.py:193
  150.5 0.1 pad_add_fusion.order_ref
  150.6 4.1 %shard_map.38 = f32[16,16,8,128]{3,2,1,0:T(8,128)S(1)} custom-call(s32[2]{0:T(128)S(1)} %pad_add_fusion.order_ref, bf16[16,128,512]{2,1,0:T(8,128)(2,1)S(1)} %all-to-all-done.panel_ref.pieces_ref, bf16[16,128,512]{2,1,0:T(8,128)(2,1)S(1)} %all-to-all-done.panel_ref.pieces_ref), custom_call_target="tpu_custom_call" | custom-call | flops 268435456 | bytes 4194304 | tf_op jit(solution)/shard_map/pallas_call | solution.py:127
  154.7 0.0 collective-permute-done.8
  154.7 1.1 add.31
  155.8 4.6 %all-to-all-start.1 = ((f32[16,16,8,128]{3,2,1,0:T(8,128)}), f32[16,16,8,128]{3,2,1,0:T(8,128)S(1)}, u32[]{:S(2)}, u32[]{:S(2)}) async-start(f32[16,16,8,128]{3,2,1,0:T(8,128)} %add.31), calls=%async_computation.1 | async-start | bytes 2097152 | tf_op jit(solution)/shard_map/all_to_all | solution.py:220
  160.4 7.2 %collective-permute-start.9 = (f32[128,128]{1,0:T(8,128)S(1)}, f32[128,128]{1,0:T(8,128)S(1)}, u32[]{:S(2)}, u32[]{:S(2)}) collective-permute-start(f32[128,128]{1,0:T(8,128)S(1)} %broadcast_select_fusion.5), channel_id=1, source_target_pairs={{0,256},{32,288},{64,320},{96,352},{128,384},{160,416},{192,448},{... | collective-permute-start | bytes 196616 | tf_op jit(solution)/shard_map/ppermute | solution.py:193
  167.6 12.6 %collective-permute-done.9 = f32[128,128]{1,0:T(8,128)S(1)} collective-permute-done((f32[128,128]{1,0:T(8,128)S(1)}, f32[128,128]{1,0:T(8,128)S(1)}, u32[]{:S(2)}, u32[]{:S(2)}) %collective-permute-start.9) | collective-permute-done | bytes 65568 | tf_op jit(solution)/shard_map/ppermute | solution.py:193
  180.2 1.9 collective-permute-start.10
  183.8 0.0 all-to-all-done.1
  183.8 0.1 reduce_sum.18
  183.9 0.0 collective-permute-done.10
  183.9 0.7 pad_maximum_fusion
  184.6 6.9 %all-to-all-start.2 = ((f32[16,2,8,128]{3,2,1,0:T(8,128)}), f32[16,2,8,128]{3,2,1,0:T(8,128)S(1)}, u32[]{:S(2)}, u32[]{:S(2)}) async-start(f32[16,2,8,128]{3,2,1,0:T(8,128)} %pad_maximum_fusion), calls=%async_computation.2 | async-start | bytes 262144 | tf_op jit(solution)/shard_map/all_to_all | solution.py:229
  191.5 0.6 broadcast_select_fusion
  192.1 6.8 %shard_map.40.inverse_ref = f32[128,128]{1,0:T(8,128)} custom-call(f32[128,128]{1,0:T(8,128)} %get-tuple-element.20.block_ref), custom_call_target="tpu_custom_call" | custom-call | flops 20971520 | bytes 1048576 | tf_op jit(solution)/shard_map/pallas_call | solution.py:149
  199.0 0.2 all-to-all-done.2
  199.3 14.6 %all_to_all.20.mine_ref = f32[16,2,8,128]{3,2,1,0:T(8,128)S(1)} all-to-all(f32[16,2,8,128]{3,2,1,0:T(8,128)S(1)} %broadcast_in_dim.4), channel_id=1, replica_groups={{0,2,4,6,8,10,12,14,16,18,20,22,24,26,28,30},{1,3,5,7,9,11,13,15,17,19,..., dimensions={0} | all-to-all | bytes 262144 | tf_op jit(solution)/shard_map/all_to_all | solution.py:233
  213.8 5.4 %collective-permute-start.11 = (f32[16,2,8,128]{3,2,1,0:T(8,128)S(1)}, f32[16,2,8,128]{3,2,1,0:T(8,128)S(1)}, u32[]{:S(2)}, u32[]{:S(2)}) collective-permute-start(f32[16,2,8,128]{3,2,1,0:T(8,128)S(1)} %all_to_all.20.mine_ref), channel_id=1, source_target_pairs={{0,1},{1,0},{2,3},{3,2},{4,5},{5,4},{6,7},{7,6},{8,9},{9,8},{10,11... | collective-permute-start | bytes 393224 | tf_op jit(solution)/shard_map/ppermute | solution.py:193
  220.5 0.1 add_convert_fusion.flag_ref
  220.6 0.8 copy-done
  221.4 7.5 %shard_map.41 = f32[128,256]{1,0:T(8,128)} custom-call(s32[3]{0:T(128)S(1)} %add_convert_fusion.flag_ref, f32[16,2,8,128]{3,2,1,0:T(8,128)S(1)} %all_to_all.20.mine_ref, f32[16,2,8,128]{3,2,1,0:T(8,128)S(1)} %collective-permute-done.11.theirs_ref, f32[1,128]{1,0:T(1,128)S(1)} %bitcast.15, f32[128,128]{1,0:T(8,128)S(1)} %copy-done, ...), custom_call_target="tpu_custom_call" | custom-call | flops 67108864 | bytes 1048576 | tf_op jit(solution)/shard_map/pallas_call | solution.py:181
  (16 shorter events, 0.1 us)
Async XLA Ops:
  64.8 73.4 %all-to-all-start = ((bf16[16,128,512]{2,1,0:T(8,128)(2,1)}), bf16[16,128,512]{2,1,0:T(8,128)(2,1)S(1)}, u32[]{:S(2)}, u32[]{:S(2)}) async-start(bf16[16,128,512]{2,1,0:T(8,128)(2,1)} %shard_map.37), calls=%async_computation | async-start | bytes 4194304 | tf_op jit(solution)/shard_map/all_to_all | solution.py:204
  78.2 33.7 %copy-start.1 = (f32[128]{0:T(128)S(1)}, f32[128]{0:T(128)}, u32[]{:S(2)}) copy-start(f32[128]{0:T(128)} %param.4) | copy-start | bytes 1540
  78.2 38.8 %copy-start.2 = (s32[16]{0:T(128)S(1)}, s32[16]{0:T(128)}, u32[]{:S(2)}) copy-start(s32[16]{0:T(128)} %param.5) | copy-start | bytes 196
  81.2 3.7 %collective-permute-start = (f32[128,128]{1,0:T(8,128)S(1)}, f32[128,128]{1,0:T(8,128)S(1)}, u32[]{:S(2)}, u32[]{:S(2)}) collective-permute-start(f32[128,128]{1,0:T(8,128)S(1)} %fusion.1), channel_id=1, source_target_pairs={{0,1},{1,0},{2,3},{3,2},{4,5},{5,4},{6,7},{7,6},{8,9},{9,8},{10,11... | collective-permute-start | bytes 196616 | tf_op jit(solution)/shard_map/ppermute | solution.py:193
  85.0 5.3 %collective-permute-start.1 = (f32[128,128]{1,0:T(8,128)S(1)}, f32[128,128]{1,0:T(8,128)S(1)}, u32[]{:S(2)}, u32[]{:S(2)}) collective-permute-start(f32[128,128]{1,0:T(8,128)S(1)} %add.25), channel_id=1, source_target_pairs={{0,16},{1,17},{2,18},{3,19},{4,20},{5,21},{6,22},{7,23},{8,24},{9,... | collective-permute-start | bytes 196616 | tf_op jit(solution)/shard_map/ppermute | solution.py:193
  90.3 5.3 %collective-permute-start.2 = (f32[128,128]{1,0:T(8,128)S(1)}, f32[128,128]{1,0:T(8,128)S(1)}, u32[]{:S(2)}, u32[]{:S(2)}) collective-permute-start(f32[128,128]{1,0:T(8,128)S(1)} %add.26), channel_id=1, source_target_pairs={{0,2},{1,3},{2,0},{3,1},{4,6},{5,7},{6,4},{7,5},{8,10},{9,11},{10,... | collective-permute-start | bytes 196616 | tf_op jit(solution)/shard_map/ppermute | solution.py:193
  95.6 6.2 %collective-permute-start.3 = (f32[128,128]{1,0:T(8,128)S(1)}, f32[128,128]{1,0:T(8,128)S(1)}, u32[]{:S(2)}, u32[]{:S(2)}) collective-permute-start(f32[128,128]{1,0:T(8,128)S(1)} %add.27), channel_id=1, source_target_pairs={{0,4},{1,5},{2,6},{3,7},{4,0},{5,1},{6,2},{7,3},{8,12},{9,13},{10,... | collective-permute-start | bytes 196616 | tf_op jit(solution)/shard_map/ppermute | solution.py:193
  101.8 10.1 %collective-permute-start.4 = (f32[128,128]{1,0:T(8,128)S(1)}, f32[128,128]{1,0:T(8,128)S(1)}, u32[]{:S(2)}, u32[]{:S(2)}) collective-permute-start(f32[128,128]{1,0:T(8,128)S(1)} %add.28), channel_id=1, source_target_pairs={{0,8},{1,9},{2,10},{3,11},{4,12},{5,13},{6,14},{7,15},{8,0},{9,1},... | collective-permute-start | bytes 196616 | tf_op jit(solution)/shard_map/ppermute | solution.py:193
  112.0 8.7 %collective-permute-start.5 = (f32[128,128]{1,0:T(8,128)S(1)}, f32[128,128]{1,0:T(8,128)S(1)}, u32[]{:S(2)}, u32[]{:S(2)}) collective-permute-start(f32[128,128]{1,0:T(8,128)S(1)} %select_add_fusion), channel_id=1, source_target_pairs={{0,32},{32,0},{64,96},{96,64},{128,160},{160,128},{192,224},{224,1... | collective-permute-start | bytes 196616 | tf_op jit(solution)/shard_map/ppermute | solution.py:193
  120.7 7.7 %collective-permute-start.6 = (f32[128,128]{1,0:T(8,128)S(1)}, f32[128,128]{1,0:T(8,128)S(1)}, u32[]{:S(2)}, u32[]{:S(2)}) collective-permute-start(f32[128,128]{1,0:T(8,128)S(1)} %broadcast_select_fusion.3), channel_id=1, source_target_pairs={{0,64},{32,96},{64,0},{96,32},{128,192},{160,224},{192,128},{224,1... | collective-permute-start | bytes 196616 | tf_op jit(solution)/shard_map/ppermute | solution.py:193
  128.4 9.8 %collective-permute-start.7 = (f32[128,128]{1,0:T(8,128)S(1)}, f32[128,128]{1,0:T(8,128)S(1)}, u32[]{:S(2)}, u32[]{:S(2)}) collective-permute-start(f32[128,128]{1,0:T(8,128)S(1)} %broadcast_select_fusion.4), channel_id=1, source_target_pairs={{0,128},{32,160},{64,192},{96,224},{128,0},{160,32},{192,64},{224,... | collective-permute-start | bytes 196616 | tf_op jit(solution)/shard_map/ppermute | solution.py:193
  142.3 12.4 %collective-permute-start.8 = (f32[16,16,8,128]{3,2,1,0:T(8,128)S(1)}, f32[16,16,8,128]{3,2,1,0:T(8,128)S(1)}, u32[]{:S(2)}, u32[]{:S(2)}) collective-permute-start(f32[16,16,8,128]{3,2,1,0:T(8,128)S(1)} %shard_map.39), channel_id=1, source_target_pairs={{0,1},{1,0},{2,3},{3,2},{4,5},{5,4},{6,7},{7,6},{8,9},{9,8},{10,11... | collective-permute-start | bytes 3145736 | tf_op jit(solution)/shard_map/ppermute | solution.py:193
  155.8 28.0 %all-to-all-start.1 = ((f32[16,16,8,128]{3,2,1,0:T(8,128)}), f32[16,16,8,128]{3,2,1,0:T(8,128)S(1)}, u32[]{:S(2)}, u32[]{:S(2)}) async-start(f32[16,16,8,128]{3,2,1,0:T(8,128)} %add.31), calls=%async_computation.1 | async-start | bytes 2097152 | tf_op jit(solution)/shard_map/all_to_all | solution.py:220
  160.4 19.8 %collective-permute-start.9 = (f32[128,128]{1,0:T(8,128)S(1)}, f32[128,128]{1,0:T(8,128)S(1)}, u32[]{:S(2)}, u32[]{:S(2)}) collective-permute-start(f32[128,128]{1,0:T(8,128)S(1)} %broadcast_select_fusion.5), channel_id=1, source_target_pairs={{0,256},{32,288},{64,320},{96,352},{128,384},{160,416},{192,448},{... | collective-permute-start | bytes 196616 | tf_op jit(solution)/shard_map/ppermute | solution.py:193
  180.2 3.7 %collective-permute-start.10 = (f32[128,128]{1,0:T(8,128)S(1)}, f32[128,128]{1,0:T(8,128)S(1)}, u32[]{:S(2)}, u32[]{:S(2)}) collective-permute-start(f32[128,128]{1,0:T(8,128)S(1)} %broadcast_select_fusion.2), channel_id=1, source_target_pairs={{0,1},{1,0},{2,3},{3,2},{4,5},{5,4},{6,7},{7,6},{8,9},{9,8},{10,11... | collective-permute-start | bytes 196616 | tf_op jit(solution)/shard_map/ppermute | solution.py:193
  184.6 14.7 %all-to-all-start.2 = ((f32[16,2,8,128]{3,2,1,0:T(8,128)}), f32[16,2,8,128]{3,2,1,0:T(8,128)S(1)}, u32[]{:S(2)}, u32[]{:S(2)}) async-start(f32[16,2,8,128]{3,2,1,0:T(8,128)} %pad_maximum_fusion), calls=%async_computation.2 | async-start | bytes 262144 | tf_op jit(solution)/shard_map/all_to_all | solution.py:229
  213.8 6.8 %collective-permute-start.11 = (f32[16,2,8,128]{3,2,1,0:T(8,128)S(1)}, f32[16,2,8,128]{3,2,1,0:T(8,128)S(1)}, u32[]{:S(2)}, u32[]{:S(2)}) collective-permute-start(f32[16,2,8,128]{3,2,1,0:T(8,128)S(1)} %all_to_all.20.mine_ref), channel_id=1, source_target_pairs={{0,1},{1,0},{2,3},{3,2},{4,5},{5,4},{6,7},{7,6},{8,9},{9,8},{10,11... | collective-permute-start | bytes 393224 | tf_op jit(solution)/shard_map/ppermute | solution.py:193
  220.6 0.8 copy-start

commit v4 on v3

v4 whole, which is shorter than its diff:
```python
import jax
import jax.numpy as jnp
from jax import lax
from jax.experimental import pallas as pl
from jax.experimental.pallas import tpu as pltpu
from jax.sharding import PartitionSpec as P

ROWS = 128
SAMP = 16
PAR = 32
CHIPS = PAR // 2
TILE = 8
TILES = ROWS // TILE
HIGHEST = lax.Precision.HIGHEST

OVER_CHIPS = [[[s * PAR + 2 * x + c for x in range(CHIPS)] for s in range(SAMP)] for c in range(2)]
OVER_SAMP = [[[s * PAR + 2 * x + c for s in range(SAMP)] for x in range(CHIPS)] for c in range(2)]
CHIPS_THEN_SAMP = OVER_CHIPS[0] + OVER_SAMP[1]
SAMP_THEN_CHIPS = OVER_SAMP[0] + OVER_CHIPS[1]
CHIPS_BY_CORE = [[2 * x + c for x in range(CHIPS)] for c in range(2)]


def exact(left, right, contract):
    return lax.dot_general(
        left, right, (contract, ((), ())),
        precision=HIGHEST, preferred_element_type=jnp.float32,
    )


def inverse_factor(matrix):
    lane = lax.broadcasted_iota(jnp.int32, (TILE, ROWS), 1)
    sub = lax.broadcasted_iota(jnp.int32, (TILE, ROWS), 0)
    lanes = lane[:1]
    tiles = [matrix[t * TILE:(t + 1) * TILE] for t in range(TILES)]
    for at in range(TILES):
        base = at * TILE
        rows = [tiles[at][r:r + 1] for r in range(TILE)]
        pivot = [
            [jnp.broadcast_to(rows[r][:, base + c:base + c + 1], (1, ROWS)) if c >= r else None for c in range(TILE)]
            for r in range(TILE)
        ]
        inverse = [None] * TILE
        for k in range(TILE):
            inverse[k] = 1.0 / pivot[k][k]
            scaled = jnp.where(lanes == base + k, 1.0, rows[k])
            for i in range(k + 1, TILE):
                factor = pivot[k][i] * inverse[k]
                for c in range(i, TILE):
                    pivot[i][c] = pivot[i][c] - factor * pivot[k][c]
                rows[i] = jnp.where(lanes == base + k, 0.0, rows[i]) - factor * scaled
        solved = [None] * TILE
        for k in reversed(range(TILE)):
            value = jnp.where(lanes == base + k, 1.0, rows[k])
            value = jnp.where((lanes > base + k) & (lanes < base + TILE), 0.0, value)
            for c in range(k + 1, TILE):
                value = value - pivot[k][c] * solved[c]
            solved[k] = value * inverse[k]
        wide = [jnp.broadcast_to(row, (TILE, ROWS)) for row in solved]
        inside = (lane >= base) & (lane < base + TILE)
        for t in range(at + 1, TILES):
            value = jnp.where(inside, 0.0, tiles[t])
            for k in range(TILE):
                value = value - tiles[t][:, base + k:base + k + 1] * wide[k]
            tiles[t] = value
        done = jnp.broadcast_to(rows[0], (TILE, ROWS))
        for r in range(1, TILE):
            done = jnp.where(sub == r, rows[r], done)
        tiles[at] = done
    out = []
    for t in range(TILES):
        diagonal = lane == sub + t * TILE
        square = jnp.sum(jnp.where(diagonal, tiles[t], 0.0), axis=1, keepdims=True)
        lower = jnp.where(lane < sub + t * TILE, tiles[t], jnp.where(diagonal, 1.0, 0.0))
        out.append(lower * lax.rsqrt(square))
    return jnp.concatenate(out, 0)


def cut_kernel(samples_ref, pieces_ref, held, arrived, left):
    width = pieces_ref.shape[2]
    into = [
        pltpu.make_async_copy(samples_ref.at[:, s * width:(s + 1) * width], held.at[s], arrived.at[s])
        for s in range(SAMP)
    ]
    out = [pltpu.make_async_copy(held.at[s], pieces_ref.at[s], left.at[s]) for s in range(SAMP)]
    for copy in into:
        copy.start()
    for s in range(SAMP):
        into[s].wait()
        out[s].start()
    for copy in out:
        copy.wait()


def cut(samples):
    shape = (SAMP, ROWS, samples.shape[1] // SAMP)
    return pl.pallas_call(
        cut_kernel,
        out_shape=jax.ShapeDtypeStruct(shape, samples.dtype),
        in_specs=[pl.BlockSpec(memory_space=pl.ANY)],
        out_specs=pl.BlockSpec(memory_space=pl.ANY),
        scratch_shapes=[
            pltpu.VMEM(shape, samples.dtype),
            pltpu.SemaphoreType.DMA((SAMP,)),
            pltpu.SemaphoreType.DMA((SAMP,)),
        ],
        cost_estimate=pl.CostEstimate(flops=0, bytes_accessed=4 << 20, transcendentals=0),
    )(samples)


def gram_kernel(panel_ref, pieces_ref, total_ref):
    panel = pieces_ref[panel_ref[0]]
    for block in range(SAMP):
        total_ref[:, block] = lax.dot_general(
            panel, pieces_ref[block], (((1,), (1,)), ((), ())), preferred_element_type=jnp.float32
        ).reshape(TILES, TILE, ROWS)


VMEM = pl.BlockSpec(memory_space=pltpu.VMEM)
SMEM = pl.BlockSpec(memory_space=pltpu.SMEM)


def partial_gram(panel, pieces):
    return pl.pallas_call(
        gram_kernel,
        out_shape=jax.ShapeDtypeStruct((TILES, SAMP, TILE, ROWS), jnp.float32),
        in_specs=[SMEM, VMEM],
        out_specs=VMEM,
        compiler_params=pltpu.CompilerParams(vmem_limit_bytes=16 << 20),
        cost_estimate=pl.CostEstimate(flops=1 << 28, bytes_accessed=4 << 20, transcendentals=0),
    )(panel[None], pieces)


def join_kernel(core_ref, mine_ref, theirs_ref, strip_ref, out_ref):
    for block in range(SAMP):
        value = mine_ref[:, block] + theirs_ref[:, block]

        @pl.when(core_ref[0] == 0)
        def _(value=value, block=block):
            out_ref[:, block] = value

        @pl.when(core_ref[0] == 1)
        def _(value=value, block=block):
            out_ref[block, :SAMP] = value

        out_ref[block, SAMP] = strip_ref[...]


def join(core, mine, theirs, strip):
    return pl.pallas_call(
        join_kernel,
        out_shape=jax.ShapeDtypeStruct((TILES, SAMP + 1, TILE, ROWS), jnp.float32),
        in_specs=[SMEM, VMEM, VMEM, VMEM],
        out_specs=VMEM,
        compiler_params=pltpu.CompilerParams(vmem_limit_bytes=16 << 20),
        cost_estimate=pl.CostEstimate(flops=1 << 20, bytes_accessed=4 << 20, transcendentals=0),
    )(core[None], mine, theirs, strip)


def first_kernel(core_ref, mine_ref, theirs_ref, inverse_ref, other_ref):
    def item(i):
        mine = mine_ref[:, i].reshape(ROWS, ROWS)
        theirs = theirs_ref[:, i].reshape(ROWS, ROWS)
        return jnp.where(core_ref[0] == 1, mine, theirs)

    inverse_ref[...] = inverse_factor(item(0))
    other_ref[...] = item(1)


def first_factor(core, mine, theirs):
    square = jax.ShapeDtypeStruct((ROWS, ROWS), jnp.float32)
    return pl.pallas_call(
        first_kernel,
        out_shape=(square, square),
        in_specs=[SMEM, VMEM, VMEM],
        out_specs=(VMEM, VMEM),
        compiler_params=pltpu.CompilerParams(vmem_limit_bytes=16 << 20),
        cost_estimate=pl.CostEstimate(flops=20 << 20, bytes_accessed=1 << 20, transcendentals=0),
    )(core[None], mine, theirs)


def last_kernel(owns_ref, strips_ref, shift_ref, inverse_ref, other_ref, out_ref):
    row = lax.broadcasted_iota(jnp.int32, (ROWS, ROWS), 0)
    column = lax.broadcasted_iota(jnp.int32, (ROWS, ROWS), 1)

    def own(k):
        add = (row == column) & (owns_ref[k] == 1)
        return strips_ref[:, k, 0].reshape(ROWS, ROWS) + jnp.where(add, shift_ref[...], 0.0)

    inverse = inverse_ref[...]
    remote = exact(inverse, strips_ref[:, 0, 1].reshape(ROWS, ROWS), ((1,), (0,)))
    second = inverse_factor(other_ref[...] - exact(remote, remote, ((0,), (0,))))
    zero = exact(inverse, own(0), ((1,), (0,)))
    rest = own(1) - exact(remote, zero, ((0,), (0,)))
    out_ref[:, :ROWS] = zero.T
    out_ref[:, ROWS:] = exact(second, rest, ((1,), (0,))).T


def last_factor(owns, strips, shift, inverse, other):
    return pl.pallas_call(
        last_kernel,
        out_shape=jax.ShapeDtypeStruct((ROWS, 2 * ROWS), jnp.float32),
        in_specs=[SMEM] + [VMEM] * 4,
        out_specs=VMEM,
        compiler_params=pltpu.CompilerParams(vmem_limit_bytes=16 << 20),
        cost_estimate=pl.CostEstimate(flops=64 << 20, bytes_accessed=1 << 20, transcendentals=0),
    )(owns, strips, shift, inverse, other)


def flip(block, bit):
    return lax.ppermute(block, "par", [(i, i ^ bit) for i in range(PAR)])


def per_device(samples, shift, panel_ids):
    here = lax.axis_index("samp")
    place = lax.axis_index("par")
    core = lax.rem(place, 2)
    chip = lax.div(place, 2)
    mine = jnp.where(core == 0, panel_ids[0], panel_ids[1])
    theirs = jnp.where(core == 0, panel_ids[1], panel_ids[0])
    axes = ("samp", "par")

    pieces = lax.all_to_all(cut(samples), "samp", 0, 0, tiled=True)

    square = lax.dot_general(
        samples, samples, (((1,), (1,)), ((), ())), preferred_element_type=jnp.float32
    )
    for bit in (1, 16, 2, 4, 8):
        square = square + flip(square, bit)
    square = square + jnp.eye(ROWS, dtype=jnp.float32) * shift[:, None]
    strip = lax.dynamic_slice_in_dim(square, chip * TILE, TILE, 0)
    pieces, strip = lax.optimization_barrier((pieces, strip))

    sent = flip(partial_gram(theirs, pieces), 1)
    total = join(core, partial_gram(mine, pieces), sent, strip)

    total = lax.all_to_all(total, axes, 0, 0, axis_index_groups=CHIPS_THEN_SAMP, tiled=True)
    strips = total[:, SAMP]
    total = total[:, :SAMP].sum(0)

    def pick(array, k):
        return lax.dynamic_index_in_dim(array, panel_ids[k], 0, keepdims=False)

    one = jnp.where(core == 0, pick(total, 1), pick(strips, 0))
    two = pick(strips, 1)
    total = jnp.stack([total, jnp.broadcast_to(one, total.shape), jnp.broadcast_to(two, total.shape)], 1)
    total = lax.all_to_all(total, axes, 0, 0, axis_index_groups=SAMP_THEN_CHIPS, tiled=True)
    blocks = total[:, 1:]
    total = total[:, :2].sum(0)

    copies = jnp.broadcast_to(total[None], (PAR,) + total.shape)
    gathered = lax.all_to_all(copies, "par", 0, 0, tiled=True)
    inverse, other = first_factor(core, blocks, flip(blocks, 1))
    owns = jnp.stack([panel_ids[0] == here, panel_ids[1] == here]).astype(jnp.int32)
    gathered = gathered.reshape(CHIPS, 2, 2, TILE, ROWS)
    return last_factor(owns, gathered, shift[None, :], inverse, other)


def solution(mesh):
    placed = (P("samp", "par"), P("samp"), P())
    return jax.shard_map(
        per_device, mesh=mesh, in_specs=placed, out_specs=P("samp", None), check_vma=False
    )
```

time: 230 us -> 145 us (0.63)
  Pallas kernels: 87.2 us -> 19.5 us
  starting transfers between devices: 86.9 us -> 53.3 us
  waiting for transfers between devices: 27.2 us -> 43.3 us
  other arithmetic: 2.9 us -> 0.29 us
  between operations: 5.74 us -> 8.23 us
    pallas_call x1, Pallas kernels: 64.8 us -> 2.62 us  [cut(): pl.pallas_call(cut_kernel, out_shape=jax.ShapeDtypeStruct(shape, samples....]
    ppermute x12 -> x7, starting transfers between devices: 62 us -> 28 us  [flip(): return lax.ppermute(block, 'par', [(i, i ^ bit) for i in range(PAR)])]
    ppermute x12 -> x7, waiting for transfers between devices: 26.9 us -> 8.3 us  [flip(): return lax.ppermute(block, 'par', [(i, i ^ bit) for i in range(PAR)])]
    all_to_all x1, waiting for transfers between devices: 0.01 us -> 16.1 us  [per_device(): lax.all_to_all(total, axes, 0, 0, axis_index_groups=CHIPS_THEN_SAMP, tile...]
    all_to_all x1, waiting for transfers between devices: 0.01 us -> 15.9 us  [per_device(): pieces = lax.all_to_all(cut(samples), 'samp', 0, 0, tiled=True)]
    pallas_call x3 -> x4, Pallas kernels: 15 us -> 9.35 us  [the longest x1 5.38 us: first_factor(): pl.pallas_call(first_kernel, out_shape=(square, square), in_specs=[SMEM,...]
    all_to_all x1, waiting for transfers between devices: 0.24 us -> 2.96 us  [per_device(): gathered = lax.all_to_all(copies, 'par', 0, 0, tiled=True)]
  transfers between devices with their start and end apart: 15 -> 10, of which waited for: 10 -> 8; matrix products, arithmetic and copies ran while one was open for 2% -> 3% of each run, Pallas kernels for 5% -> 4%
where the time goes in v4:
time: 145 us; the launch traced here: 144 us
  starting transfers between devices  53.3 us (37%)
  waiting for transfers between devices  43.3 us (30%)
  Pallas kernels  19.5 us (13%)
  blocking collectives  14.9 us (10%)
  between operations  8.23 us (6%)
  matrix products  2.93 us (2%)
  local copies, waits for them, and re-layouts  1.49 us (1%)
    ppermute x7, starting transfers between devices, flip(): return lax.ppermute(block, 'par', [(i, i ^ bit) for i in range(PAR)])  28 us
    all_to_all x1, waiting for transfers between devices, per_device(): lax.all_to_all(total, axes, 0, 0, axis_index_groups=CHIPS_THEN_SAMP, tile...  16.1 us
    all_to_all x1, waiting for transfers between devices, per_device(): pieces = lax.all_to_all(cut(samples), 'samp', 0, 0, tiled=True)  15.9 us
    all_to_all x1, blocking collectives, per_device(): lax.all_to_all(total, axes, 0, 0, axis_index_groups=SAMP_THEN_CHIPS, tile...  14.9 us
    all_to_all x1, starting transfers between devices, per_device(): pieces = lax.all_to_all(cut(samples), 'samp', 0, 0, tiled=True)  13.4 us
    ppermute x7, waiting for transfers between devices, flip(): return lax.ppermute(block, 'par', [(i, i ^ bit) for i in range(PAR)])  8.3 us
    all_to_all x1, starting transfers between devices, per_device(): gathered = lax.all_to_all(copies, 'par', 0, 0, tiled=True)  8.18 us
    pallas_call x1, Pallas kernels, last_factor(): pl.pallas_call(last_kernel, out_shape=jax.ShapeDtypeStruct((ROWS, 2 * ROW...  7.49 us
  transfers between devices with their start and end apart: 10, of which 8 were waited for; matrix products, arithmetic and copies ran while one was open for 3% of the time, Pallas kernels for 4%

profile of v4, /device:TPU:1, one launch (start us, length us, event | category | flops | bytes accessed | tf_op | source)
XLA Modules:
  0.0 143.9 jit_solution(2343052353222819002)
XLA Ops:
  0.0 2.6 %shard_map.37 = bf16[16,128,512]{2,1,0:T(8,128)(2,1)} custom-call(bf16[128,8192]{1,0:T(8,128)(2,1)} %samples_ref.1), custom_call_target="tpu_custom_call" | custom-call | bytes 4194304 | tf_op jit(solution)/shard_map/pallas_call | solution.py:96
  2.6 13.4 %all-to-all-start = ((bf16[16,128,512]{2,1,0:T(8,128)(2,1)}), bf16[16,128,512]{2,1,0:T(8,128)(2,1)S(1)}, u32[]{:S(2)}, u32[]{:S(2)}) async-start(bf16[16,128,512]{2,1,0:T(8,128)(2,1)} %shard_map.37), calls=%async_computation | async-start | bytes 4194304 | tf_op jit(solution)/shard_map/all_to_all | solution.py:222
  16.1 0.0 copy-start
  16.1 0.0 copy-start.1
  16.1 2.9 %fusion.3 = f32[128,128]{1,0:T(8,128)S(1)} fusion(bf16[128,8192]{1,0:T(8,128)(2,1)} %samples_ref.1), kind=kOutput, calls=%fused_computation.11 | convolution fusion | flops 268435456 | bytes 2162688 | tf_op jit(solution)/shard_map/dot_general | solution.py:224
  19.0 2.9 %collective-permute-start = (f32[128,128]{1,0:T(8,128)S(1)}, f32[128,128]{1,0:T(8,128)S(1)}, u32[]{:S(2)}, u32[]{:S(2)}) collective-permute-start(f32[128,128]{1,0:T(8,128)S(1)} %fusion.3), channel_id=1, source_target_pairs={{0,1},{1,0},{2,3},{3,2},{4,5},{5,4},{6,7},{7,6},{8,9},{9,8},{10,11... | collective-permute-start | bytes 196616 | tf_op jit(solution)/shard_map/ppermute | solution.py:210
  21.9 0.9 collective-permute-done
  22.8 2.2 %collective-permute-start.1 = (f32[128,128]{1,0:T(8,128)S(1)}, f32[128,128]{1,0:T(8,128)S(1)}, u32[]{:S(2)}, u32[]{:S(2)}) collective-permute-start(f32[128,128]{1,0:T(8,128)S(1)} %add.29), channel_id=1, source_target_pairs={{0,16},{1,17},{2,18},{3,19},{4,20},{5,21},{6,22},{7,23},{8,24},{9,... | collective-permute-start | bytes 196616 | tf_op jit(solution)/shard_map/ppermute | solution.py:210
  25.0 3.1 %collective-permute-done.1 = f32[128,128]{1,0:T(8,128)S(1)} collective-permute-done((f32[128,128]{1,0:T(8,128)S(1)}, f32[128,128]{1,0:T(8,128)S(1)}, u32[]{:S(2)}, u32[]{:S(2)}) %collective-permute-start.1) | collective-permute-done | bytes 65568 | tf_op jit(solution)/shard_map/ppermute | solution.py:210
  28.1 3.2 %collective-permute-start.2 = (f32[128,128]{1,0:T(8,128)S(1)}, f32[128,128]{1,0:T(8,128)S(1)}, u32[]{:S(2)}, u32[]{:S(2)}) collective-permute-start(f32[128,128]{1,0:T(8,128)S(1)} %add.30), channel_id=1, source_target_pairs={{0,2},{1,3},{2,0},{3,1},{4,6},{5,7},{6,4},{7,5},{8,10},{9,11},{10,... | collective-permute-start | bytes 196616 | tf_op jit(solution)/shard_map/ppermute | solution.py:210
  31.3 2.1 %collective-permute-done.2 = f32[128,128]{1,0:T(8,128)S(1)} collective-permute-done((f32[128,128]{1,0:T(8,128)S(1)}, f32[128,128]{1,0:T(8,128)S(1)}, u32[]{:S(2)}, u32[]{:S(2)}) %collective-permute-start.2) | collective-permute-done | bytes 65568 | tf_op jit(solution)/shard_map/ppermute | solution.py:210
  33.5 4.2 %collective-permute-start.3 = (f32[128,128]{1,0:T(8,128)S(1)}, f32[128,128]{1,0:T(8,128)S(1)}, u32[]{:S(2)}, u32[]{:S(2)}) collective-permute-start(f32[128,128]{1,0:T(8,128)S(1)} %add.31), channel_id=1, source_target_pairs={{0,4},{1,5},{2,6},{3,7},{4,0},{5,1},{6,2},{7,3},{8,12},{9,13},{10,... | collective-permute-start | bytes 196616 | tf_op jit(solution)/shard_map/ppermute | solution.py:210
  37.7 0.0 copy-done
  37.7 0.1 dynamic-slice.2
  37.8 1.9 %collective-permute-done.3 = f32[128,128]{1,0:T(8,128)S(1)} collective-permute-done((f32[128,128]{1,0:T(8,128)S(1)}, f32[128,128]{1,0:T(8,128)S(1)}, u32[]{:S(2)}, u32[]{:S(2)}) %collective-permute-start.3) | collective-permute-done | bytes 65568 | tf_op jit(solution)/shard_map/ppermute | solution.py:210
  39.7 8.2 %collective-permute-start.4 = (f32[128,128]{1,0:T(8,128)S(1)}, f32[128,128]{1,0:T(8,128)S(1)}, u32[]{:S(2)}, u32[]{:S(2)}) collective-permute-start(f32[128,128]{1,0:T(8,128)S(1)} %add.32), channel_id=1, source_target_pairs={{0,8},{1,9},{2,10},{3,11},{4,12},{5,13},{6,14},{7,15},{8,0},{9,1},... | collective-permute-start | bytes 196616 | tf_op jit(solution)/shard_map/ppermute | solution.py:210
  47.8 0.0 copy-done.1
  47.8 0.7 fusion.2
  49.8 0.0 collective-permute-done.4
  49.8 0.1 fusion.strip_ref
  49.9 15.9 %all-to-all-done.pieces_ref = bf16[16,128,512]{2,1,0:T(8,128)(2,1)S(1)} async-done(((bf16[16,128,512]{2,1,0:T(8,128)(2,1)}), bf16[16,128,512]{2,1,0:T(8,128)(2,1)S(1)}, u32[]{:S(2)}, u32[]{:S(2)}) %all-to-all-start) | async-done | bytes 2097184 | tf_op jit(solution)/shard_map/all_to_all | solution.py:222
  65.8 0.7 shard_map.39
  66.6 5.2 %collective-permute-start.5 = (f32[16,16,8,128]{3,2,1,0:T(8,128)S(1)}, f32[16,16,8,128]{3,2,1,0:T(8,128)}, u32[]{:S(2)}, u32[]{:S(2)}) collective-permute-start(f32[16,16,8,128]{3,2,1,0:T(8,128)S(1)} %shard_map.39), channel_id=1, source_target_pairs={{0,1},{1,0},{2,3},{3,2},{4,5},{5,4},{6,7},{7,6},{8,9},{9,8},{10,11... | collective-permute-start | bytes 3145736 | tf_op jit(solution)/shard_map/ppermute | solution.py:210
  73.1 0.7 shard_map.38.mine_ref
  73.8 0.4 collective-permute-done.5.theirs_ref
  74.1 2.6 %shard_map.40 = f32[16,17,8,128]{3,2,1,0:T(8,128)} custom-call(s32[1]{0:T(128)} %bitcast.4.core_ref, f32[16,16,8,128]{3,2,1,0:T(8,128)S(1)} %shard_map.38.mine_ref, f32[16,16,8,128]{3,2,1,0:T(8,128)} %collective-permute-done.5.theirs_ref, f32[8,128]{1,0:T(8,128)S(1)} %fusion.strip_ref), custom_call_target="tpu_custom_call" | custom-call | flops 1048576 | bytes 4194304 | tf_op jit(solution)/shard_map/pallas_call | solution.py:149
  76.7 3.7 %all-to-all-start.1 = ((f32[16,17,8,128]{3,2,1,0:T(8,128)}), f32[16,17,8,128]{3,2,1,0:T(8,128)S(1)}, u32[]{:S(2)}, u32[]{:S(2)}) async-start(f32[16,17,8,128]{3,2,1,0:T(8,128)} %shard_map.40), calls=%async_computation.1 | async-start | bytes 2228224 | tf_op jit(solution)/shard_map/all_to_all | solution.py:236
  84.4 16.1 %all-to-all-done.1 = f32[16,17,8,128]{3,2,1,0:T(8,128)S(1)} async-done(((f32[16,17,8,128]{3,2,1,0:T(8,128)}), f32[16,17,8,128]{3,2,1,0:T(8,128)S(1)}, u32[]{:S(2)}, u32[]{:S(2)}) %all-to-all-start.1) | async-done | bytes 1114144 | tf_op jit(solution)/shard_map/all_to_all | solution.py:236
  100.5 0.1 slice_reduce_fusion
  100.6 14.9 %all_to_all.20 = f32[16,3,8,128]{3,2,1,0:T(8,128)S(1)} all-to-all(f32[16,3,8,128]{3,2,1,0:T(8,128)S(1)} %pad_maximum_fusion), channel_id=1, replica_groups={{0,32,64,96,128,160,192,224,256,288,320,352,384,416,448,480},{2,34,66,9..., dimensions={0} | all-to-all | bytes 393216 | tf_op jit(solution)/shard_map/all_to_all | solution.py:246
  115.5 0.7 broadcast_in_dim.23
  116.3 8.2 %all-to-all-start.3 = ((f32[32,2,8,128]{3,2,1,0:T(8,128)}), f32[32,2,8,128]{3,2,1,0:T(8,128)S(1)}, u32[]{:S(2)}, u32[]{:S(2)}) async-start(f32[32,2,8,128]{3,2,1,0:T(8,128)} %broadcast_in_dim.23), calls=%async_computation.3 | async-start | bytes 524288 | tf_op jit(solution)/shard_map/all_to_all | solution.py:251
  124.4 2.1 %collective-permute-start.6 = (f32[16,2,8,128]{3,2,1,0:T(8,128)S(1)}, f32[16,2,8,128]{3,2,1,0:T(8,128)S(1)}, u32[]{:S(2)}, u32[]{:S(2)}) collective-permute-start(f32[16,2,8,128]{3,2,1,0:T(8,128)S(1)} %get-tuple-element.13.mine_ref), channel_id=1, source_target_pairs={{0,1},{1,0},{2,3},{3,2},{4,5},{5,4},{6,7},{7,6},{8,9},{9,8},{10,11... | collective-permute-start | bytes 393224 | tf_op jit(solution)/shard_map/ppermute | solution.py:210
  127.9 0.1 add_convert_fusion.owns_ref
  128.0 0.0 collective-permute-done.6.theirs_ref
  128.0 5.4 %shard_map.41 = (f32[128,128]{1,0:T(8,128)S(1)}, f32[128,128]{1,0:T(8,128)S(1)}) custom-call(s32[1]{0:T(128)} %bitcast.4.core_ref, f32[16,2,8,128]{3,2,1,0:T(8,128)S(1)} %get-tuple-element.13.mine_ref, f32[16,2,8,128]{3,2,1,0:T(8,128)S(1)} %collective-permute-done.6.theirs_ref), custom_call_target="tpu_custom_call" | custom-call | flops 20971520 | bytes 1048576 | tf_op jit(solution)/shard_map/pallas_call | solution.py:171
  133.4 3.0 %all-to-all-done.3 = f32[32,2,8,128]{3,2,1,0:T(8,128)S(1)} async-done(((f32[32,2,8,128]{3,2,1,0:T(8,128)}), f32[32,2,8,128]{3,2,1,0:T(8,128)S(1)}, u32[]{:S(2)}, u32[]{:S(2)}) %all-to-all-start.3) | async-done | bytes 262176 | tf_op jit(solution)/shard_map/all_to_all | solution.py:251
  136.4 7.5 %shard_map.42 = f32[128,256]{1,0:T(8,128)} custom-call(s32[2]{0:T(128)S(1)} %add_convert_fusion.owns_ref, f32[16,2,2,8,128]{4,3,2,1,0:T(8,128)S(1)} %bitcast.18, f32[1,128]{1,0:T(1,128)S(1)} %bitcast.19, f32[128,128]{1,0:T(8,128)S(1)} %get-tuple-element.11.inverse_ref, f32[128,128]{1,0:T(8,128)S(1)} %get-tuple-element.12.other_ref), custom_call_target="tpu_custom_call" | custom-call | flops 67108864 | bytes 1048576 | tf_op jit(solution)/shard_map/pallas_call | solution.py:199
  (11 shorter events, 0.1 us)
Async XLA Ops:
  2.6 63.2 %all-to-all-start = ((bf16[16,128,512]{2,1,0:T(8,128)(2,1)}), bf16[16,128,512]{2,1,0:T(8,128)(2,1)S(1)}, u32[]{:S(2)}, u32[]{:S(2)}) async-start(bf16[16,128,512]{2,1,0:T(8,128)(2,1)} %shard_map.37), calls=%async_computation | async-start | bytes 4194304 | tf_op jit(solution)/shard_map/all_to_all | solution.py:222
  16.1 21.6 %copy-start = (f32[128]{0:T(128)S(1)}, f32[128]{0:T(128)}, u32[]{:S(2)}) copy-start(f32[128]{0:T(128)} %param.4) | copy-start | bytes 1540
  16.1 31.7 %copy-start.1 = (s32[16]{0:T(128)S(1)}, s32[16]{0:T(128)}, u32[]{:S(2)}) copy-start(s32[16]{0:T(128)} %param.5) | copy-start | bytes 196
  19.0 3.8 %collective-permute-start = (f32[128,128]{1,0:T(8,128)S(1)}, f32[128,128]{1,0:T(8,128)S(1)}, u32[]{:S(2)}, u32[]{:S(2)}) collective-permute-start(f32[128,128]{1,0:T(8,128)S(1)} %fusion.3), channel_id=1, source_target_pairs={{0,1},{1,0},{2,3},{3,2},{4,5},{5,4},{6,7},{7,6},{8,9},{9,8},{10,11... | collective-permute-start | bytes 196616 | tf_op jit(solution)/shard_map/ppermute | solution.py:210
  22.8 5.3 %collective-permute-start.1 = (f32[128,128]{1,0:T(8,128)S(1)}, f32[128,128]{1,0:T(8,128)S(1)}, u32[]{:S(2)}, u32[]{:S(2)}) collective-permute-start(f32[128,128]{1,0:T(8,128)S(1)} %add.29), channel_id=1, source_target_pairs={{0,16},{1,17},{2,18},{3,19},{4,20},{5,21},{6,22},{7,23},{8,24},{9,... | collective-permute-start | bytes 196616 | tf_op jit(solution)/shard_map/ppermute | solution.py:210
  28.1 5.3 %collective-permute-start.2 = (f32[128,128]{1,0:T(8,128)S(1)}, f32[128,128]{1,0:T(8,128)S(1)}, u32[]{:S(2)}, u32[]{:S(2)}) collective-permute-start(f32[128,128]{1,0:T(8,128)S(1)} %add.30), channel_id=1, source_target_pairs={{0,2},{1,3},{2,0},{3,1},{4,6},{5,7},{6,4},{7,5},{8,10},{9,11},{10,... | collective-permute-start | bytes 196616 | tf_op jit(solution)/shard_map/ppermute | solution.py:210
  33.5 6.2 %collective-permute-start.3 = (f32[128,128]{1,0:T(8,128)S(1)}, f32[128,128]{1,0:T(8,128)S(1)}, u32[]{:S(2)}, u32[]{:S(2)}) collective-permute-start(f32[128,128]{1,0:T(8,128)S(1)} %add.31), channel_id=1, source_target_pairs={{0,4},{1,5},{2,6},{3,7},{4,0},{5,1},{6,2},{7,3},{8,12},{9,13},{10,... | collective-permute-start | bytes 196616 | tf_op jit(solution)/shard_map/ppermute | solution.py:210
  39.7 10.2 %collective-permute-start.4 = (f32[128,128]{1,0:T(8,128)S(1)}, f32[128,128]{1,0:T(8,128)S(1)}, u32[]{:S(2)}, u32[]{:S(2)}) collective-permute-start(f32[128,128]{1,0:T(8,128)S(1)} %add.32), channel_id=1, source_target_pairs={{0,8},{1,9},{2,10},{3,11},{4,12},{5,13},{6,14},{7,15},{8,0},{9,1},... | collective-permute-start | bytes 196616 | tf_op jit(solution)/shard_map/ppermute | solution.py:210
  66.6 7.6 %collective-permute-start.5 = (f32[16,16,8,128]{3,2,1,0:T(8,128)S(1)}, f32[16,16,8,128]{3,2,1,0:T(8,128)}, u32[]{:S(2)}, u32[]{:S(2)}) collective-permute-start(f32[16,16,8,128]{3,2,1,0:T(8,128)S(1)} %shard_map.39), channel_id=1, source_target_pairs={{0,1},{1,0},{2,3},{3,2},{4,5},{5,4},{6,7},{7,6},{8,9},{9,8},{10,11... | collective-permute-start | bytes 3145736 | tf_op jit(solution)/shard_map/ppermute | solution.py:210
  76.7 23.8 %all-to-all-start.1 = ((f32[16,17,8,128]{3,2,1,0:T(8,128)}), f32[16,17,8,128]{3,2,1,0:T(8,128)S(1)}, u32[]{:S(2)}, u32[]{:S(2)}) async-start(f32[16,17,8,128]{3,2,1,0:T(8,128)} %shard_map.40), calls=%async_computation.1 | async-start | bytes 2228224 | tf_op jit(solution)/shard_map/all_to_all | solution.py:236
  116.3 20.1 %all-to-all-start.3 = ((f32[32,2,8,128]{3,2,1,0:T(8,128)}), f32[32,2,8,128]{3,2,1,0:T(8,128)S(1)}, u32[]{:S(2)}, u32[]{:S(2)}) async-start(f32[32,2,8,128]{3,2,1,0:T(8,128)} %broadcast_in_dim.23), calls=%async_computation.3 | async-start | bytes 524288 | tf_op jit(solution)/shard_map/all_to_all | solution.py:251
  124.4 3.6 %collective-permute-start.6 = (f32[16,2,8,128]{3,2,1,0:T(8,128)S(1)}, f32[16,2,8,128]{3,2,1,0:T(8,128)S(1)}, u32[]{:S(2)}, u32[]{:S(2)}) collective-permute-start(f32[16,2,8,128]{3,2,1,0:T(8,128)S(1)} %get-tuple-element.13.mine_ref), channel_id=1, source_target_pairs={{0,1},{1,0},{2,3},{3,2},{4,5},{5,4},{6,7},{7,6},{8,9},{9,8},{10,11... | collective-permute-start | bytes 393224 | tf_op jit(solution)/shard_map/ppermute | solution.py:210

commit v5 on v4

--- a/solution.py
+++ b/solution.py
@@ -52,27 +52,23 @@
         for k in reversed(range(TILE)):
             value = jnp.where(lanes == base + k, 1.0, rows[k])
             value = jnp.where((lanes > base + k) & (lanes < base + TILE), 0.0, value)
-            for c in range(k + 1, TILE):
+            for c in range(TILE - 1, k, -1):
                 value = value - pivot[k][c] * solved[c]
             solved[k] = value * inverse[k]
         wide = [jnp.broadcast_to(row, (TILE, ROWS)) for row in solved]
         inside = (lane >= base) & (lane < base + TILE)
         for t in range(at + 1, TILES):
             value = jnp.where(inside, 0.0, tiles[t])
-            for k in range(TILE):
+            for k in reversed(range(TILE)):
                 value = value - tiles[t][:, base + k:base + k + 1] * wide[k]
             tiles[t] = value
-        done = jnp.broadcast_to(rows[0], (TILE, ROWS))
-        for r in range(1, TILE):
-            done = jnp.where(sub == r, rows[r], done)
+        done = None
+        for r in range(TILE):
+            row = jnp.where(lanes < base + r, rows[r], jnp.where(lanes == base + r, 1.0, 0.0))
+            row = jnp.broadcast_to(row * lax.rsqrt(pivot[r][r]), (TILE, ROWS))
+            done = row if done is None else jnp.where(sub == r, row, done)
         tiles[at] = done
-    out = []
-    for t in range(TILES):
-        diagonal = lane == sub + t * TILE
-        square = jnp.sum(jnp.where(diagonal, tiles[t], 0.0), axis=1, keepdims=True)
-        lower = jnp.where(lane < sub + t * TILE, tiles[t], jnp.where(diagonal, 1.0, 0.0))
-        out.append(lower * lax.rsqrt(square))
-    return jnp.concatenate(out, 0)
+    return jnp.concatenate(tiles, 0)
 
 
 def cut_kernel(samples_ref, pieces_ref, held, arrived, left):
@@ -130,27 +126,56 @@
     )(panel[None], pieces)
 
 
-def join_kernel(core_ref, mine_ref, theirs_ref, strip_ref, out_ref):
-    for block in range(SAMP):
-        value = mine_ref[:, block] + theirs_ref[:, block]
-
-        @pl.when(core_ref[0] == 0)
-        def _(value=value, block=block):
-            out_ref[:, block] = value
-
-        @pl.when(core_ref[0] == 1)
-        def _(value=value, block=block):
-            out_ref[block, :SAMP] = value
-
-        out_ref[block, SAMP] = strip_ref[...]
+PART = 4
+
+
+def join_kernel(core_ref, mine_ref, theirs_ref, strip_ref, out_ref, theirs_held, held, arrived, left):
+    def arrival(part):
+        tiles = pl.ds(part * PART, PART)
+        return pltpu.make_async_copy(theirs_ref.at[tiles], theirs_held.at[tiles], arrived.at[part])
+
+    def departure(tile, core):
+        place = out_ref.at[tile, pl.ds(0, SAMP)] if core == 0 else out_ref.at[:, tile]
+        return pltpu.make_async_copy(held.at[tile], place, left.at[tile])
+
+    def strips():
+        return pltpu.make_async_copy(held.at[TILES], out_ref.at[:, SAMP], left.at[TILES])
+
+    def on_core(core, tiles, act):
+        @pl.when(core_ref[0] == core)
+        def _():
+            for tile in tiles:
+                act(departure(tile, core))
+
+    for part in range(TILES // PART):
+        arrival(part).start()
+    held[TILES] = jnp.broadcast_to(strip_ref[...][None], (SAMP, TILE, ROWS))
+    strips().start()
+    for part in range(TILES // PART):
+        arrival(part).wait()
+        tiles = range(part * PART, part * PART + PART)
+        for tile in tiles:
+            held[tile] = mine_ref[tile] + theirs_held[tile]
+        for core in range(2):
+            on_core(core, tiles, lambda copy: copy.start())
+    for core in range(2):
+        on_core(core, range(TILES), lambda copy: copy.wait())
+    strips().wait()
 
 
 def join(core, mine, theirs, strip):
+    anywhere = pl.BlockSpec(memory_space=pl.ANY)
     return pl.pallas_call(
         join_kernel,
         out_shape=jax.ShapeDtypeStruct((TILES, SAMP + 1, TILE, ROWS), jnp.float32),
-        in_specs=[SMEM, VMEM, VMEM, VMEM],
-        out_specs=VMEM,
+        in_specs=[SMEM, VMEM, anywhere, VMEM],
+        out_specs=anywhere,
+        scratch_shapes=[
+            pltpu.VMEM((TILES, SAMP, TILE, ROWS), jnp.float32),
+            pltpu.VMEM((TILES + 1, SAMP, TILE, ROWS), jnp.float32),
+            pltpu.SemaphoreType.DMA((TILES // PART,)),
+            pltpu.SemaphoreType.DMA((TILES + 1,)),
+        ],
         compiler_params=pltpu.CompilerParams(vmem_limit_bytes=16 << 20),
         cost_estimate=pl.CostEstimate(flops=1 << 20, bytes_accessed=4 << 20, transcendentals=0),
     )(core[None], mine, theirs, strip)
@@ -178,16 +203,21 @@
     )(core[None], mine, theirs)
 
 
-def last_kernel(owns_ref, strips_ref, shift_ref, inverse_ref, other_ref, out_ref):
+def last_kernel(flags_ref, mine_ref, theirs_ref, shift_ref, inverse_ref, other_ref, out_ref):
     row = lax.broadcasted_iota(jnp.int32, (ROWS, ROWS), 0)
     column = lax.broadcasted_iota(jnp.int32, (ROWS, ROWS), 1)
 
+    def item(k, i):
+        mine = mine_ref[:, i].reshape(ROWS, ROWS)
+        theirs = theirs_ref[:, i].reshape(ROWS, ROWS)
+        return jnp.where(flags_ref[2] == k, mine, theirs)
+
     def own(k):
-        add = (row == column) & (owns_ref[k] == 1)
-        return strips_ref[:, k, 0].reshape(ROWS, ROWS) + jnp.where(add, shift_ref[...], 0.0)
+        add = (row == column) & (flags_ref[k] == 1)
+        return item(k, 0) + jnp.where(add, shift_ref[...], 0.0)
 
     inverse = inverse_ref[...]
-    remote = exact(inverse, strips_ref[:, 0, 1].reshape(ROWS, ROWS), ((1,), (0,)))
+    remote = exact(inverse, item(0, 1), ((1,), (0,)))
     second = inverse_factor(other_ref[...] - exact(remote, remote, ((0,), (0,))))
     zero = exact(inverse, own(0), ((1,), (0,)))
     rest = own(1) - exact(remote, zero, ((0,), (0,)))
@@ -195,15 +225,15 @@
     out_ref[:, ROWS:] = exact(second, rest, ((1,), (0,))).T
 
 
-def last_factor(owns, strips, shift, inverse, other):
+def last_factor(flags, mine, theirs, shift, inverse, other):
     return pl.pallas_call(
         last_kernel,
         out_shape=jax.ShapeDtypeStruct((ROWS, 2 * ROWS), jnp.float32),
-        in_specs=[SMEM] + [VMEM] * 4,
+        in_specs=[SMEM] + [VMEM] * 5,
         out_specs=VMEM,
         compiler_params=pltpu.CompilerParams(vmem_limit_bytes=16 << 20),
         cost_estimate=pl.CostEstimate(flops=64 << 20, bytes_accessed=1 << 20, transcendentals=0),
-    )(owns, strips, shift, inverse, other)
+    )(flags, mine, theirs, shift, inverse, other)
 
 
 def flip(block, bit):
@@ -247,12 +277,14 @@
     blocks = total[:, 1:]
     total = total[:, :2].sum(0)
 
-    copies = jnp.broadcast_to(total[None], (PAR,) + total.shape)
-    gathered = lax.all_to_all(copies, "par", 0, 0, tiled=True)
+    copies = jnp.broadcast_to(total[None], (CHIPS,) + total.shape)
+    gathered = lax.all_to_all(copies, "par", 0, 0, axis_index_groups=CHIPS_BY_CORE, tiled=True)
     inverse, other = first_factor(core, blocks, flip(blocks, 1))
-    owns = jnp.stack([panel_ids[0] == here, panel_ids[1] == here]).astype(jnp.int32)
-    gathered = gathered.reshape(CHIPS, 2, 2, TILE, ROWS)
-    return last_factor(owns, gathered, shift[None, :], inverse, other)
+    gathered, inverse = lax.optimization_barrier((gathered, inverse))
+    flags = jnp.stack([
+        (panel_ids[0] == here).astype(jnp.int32), (panel_ids[1] == here).astype(jnp.int32), core
+    ])
+    return last_factor(flags, gathered, flip(gathered, 1), shift[None, :], inverse, other)
 
 
 def solution(mesh):

time: 145 us -> 142 us (0.979)
  Pallas kernels: 19.5 us -> 16 us
  starting transfers between devices: 53.3 us -> 56.8 us
  waiting for transfers between devices: 43.3 us -> 41.8 us
    ppermute x7 -> x8, starting transfers between devices: 28 us -> 36 us  [flip(): return lax.ppermute(block, 'par', [(i, i ^ bit) for i in range(PAR)])]
    all_to_all x1, starting transfers between devices: 8.18 us -> 3.63 us  [per_device(): lax.all_to_all(copies, 'par', 0, 0, axis_index_groups=CHIPS_BY_CORE, tile...]
    all_to_all x1, waiting for transfers between devices: 2.96 us -> 0.01 us  [per_device(): lax.all_to_all(copies, 'par', 0, 0, axis_index_groups=CHIPS_BY_CORE, tile...]
    pallas_call x1, Pallas kernels: 7.49 us -> 5.92 us  [last_factor(): pl.pallas_call(last_kernel, out_shape=jax.ShapeDtypeStruct((ROWS, 2 * ROW...]
    pallas_call x1, Pallas kernels: 5.38 us -> 3.85 us  [first_factor(): pl.pallas_call(first_kernel, out_shape=(square, square), in_specs=[SMEM,...]
    ppermute x7 -> x8, waiting for transfers between devices: 8.3 us -> 9.38 us  [flip(): return lax.ppermute(block, 'par', [(i, i ^ bit) for i in range(PAR)])]
  transfers between devices with their start and end apart: 10 -> 11, of which waited for: 8 -> 8; matrix products, arithmetic and copies ran while one was open for 3% -> 3% of each run, Pallas kernels for 4% -> 3%
where the time goes in v5:
time: 142 us
  starting transfers between devices  56.8 us (40%)
  waiting for transfers between devices  41.8 us (29%)
  Pallas kernels  16 us (11%)
  blocking collectives  14.9 us (10%)
  between operations  7.66 us (5%)
  matrix products  2.94 us (2%)
  local copies, waits for them, and re-layouts  1.43 us (1%)
    ppermute x8, starting transfers between devices, flip(): return lax.ppermute(block, 'par', [(i, i ^ bit) for i in range(PAR)])  36 us
    all_to_all x1, waiting for transfers between devices, per_device(): lax.all_to_all(total, axes, 0, 0, axis_index_groups=CHIPS_THEN_SAMP, tile...  16.4 us
    all_to_all x1, waiting for transfers between devices, per_device(): pieces = lax.all_to_all(cut(samples), 'samp', 0, 0, tiled=True)  16 us
    all_to_all x1, blocking collectives, per_device(): lax.all_to_all(total, axes, 0, 0, axis_index_groups=SAMP_THEN_CHIPS, tile...  14.9 us
    all_to_all x1, starting transfers between devices, per_device(): pieces = lax.all_to_all(cut(samples), 'samp', 0, 0, tiled=True)  13.4 us
    ppermute x8, waiting for transfers between devices, flip(): return lax.ppermute(block, 'par', [(i, i ^ bit) for i in range(PAR)])  9.38 us
    pallas_call x1, Pallas kernels, last_factor(): pl.pallas_call(last_kernel, out_shape=jax.ShapeDtypeStruct((ROWS, 2 * ROW...  5.92 us
    pallas_call x1, Pallas kernels, first_factor(): pl.pallas_call(first_kernel, out_shape=(square, square), in_specs=[SMEM,...  3.85 us
  transfers between devices with their start and end apart: 11, of which 8 were waited for; matrix products, arithmetic and copies ran while one was open for 3% of the time, Pallas kernels for 3%

profile of v5, /device:TPU:1, one launch (start us, length us, event | category | flops | bytes accessed | tf_op | source)
XLA Modules:
  0.0 141.8 jit_solution(17834637595513229358)
XLA Ops:
  0.0 2.6 %shard_map.37 = bf16[16,128,512]{2,1,0:T(8,128)(2,1)} custom-call(bf16[128,8192]{1,0:T(8,128)(2,1)} %samples_ref.1), custom_call_target="tpu_custom_call" | custom-call | bytes 4194304 | tf_op jit(solution)/shard_map/pallas_call | solution.py:92
  2.6 13.4 %all-to-all-start = ((bf16[16,128,512]{2,1,0:T(8,128)(2,1)}), bf16[16,128,512]{2,1,0:T(8,128)(2,1)S(1)}, u32[]{:S(2)}, u32[]{:S(2)}) async-start(bf16[16,128,512]{2,1,0:T(8,128)(2,1)} %shard_map.37), calls=%async_computation | async-start | bytes 4194304 | tf_op jit(solution)/shard_map/all_to_all | solution.py:252
  16.1 0.0 copy-start
  16.1 0.0 copy-start.1
  16.1 2.9 %fusion.3 = f32[128,128]{1,0:T(8,128)S(1)} fusion(bf16[128,8192]{1,0:T(8,128)(2,1)} %samples_ref.1), kind=kOutput, calls=%fused_computation.11 | convolution fusion | flops 268435456 | bytes 2162688 | tf_op jit(solution)/shard_map/dot_general | solution.py:254
  19.0 2.9 %collective-permute-start = (f32[128,128]{1,0:T(8,128)S(1)}, f32[128,128]{1,0:T(8,128)S(1)}, u32[]{:S(2)}, u32[]{:S(2)}) collective-permute-start(f32[128,128]{1,0:T(8,128)S(1)} %fusion.3), channel_id=1, source_target_pairs={{0,1},{1,0},{2,3},{3,2},{4,5},{5,4},{6,7},{7,6},{8,9},{9,8},{10,11... | collective-permute-start | bytes 196616 | tf_op jit(solution)/shard_map/ppermute | solution.py:240
  21.9 0.9 collective-permute-done
  22.8 2.2 %collective-permute-start.1 = (f32[128,128]{1,0:T(8,128)S(1)}, f32[128,128]{1,0:T(8,128)S(1)}, u32[]{:S(2)}, u32[]{:S(2)}) collective-permute-start(f32[128,128]{1,0:T(8,128)S(1)} %add.29), channel_id=1, source_target_pairs={{0,16},{1,17},{2,18},{3,19},{4,20},{5,21},{6,22},{7,23},{8,24},{9,... | collective-permute-start | bytes 196616 | tf_op jit(solution)/shard_map/ppermute | solution.py:240
  25.0 3.1 %collective-permute-done.1 = f32[128,128]{1,0:T(8,128)S(1)} collective-permute-done((f32[128,128]{1,0:T(8,128)S(1)}, f32[128,128]{1,0:T(8,128)S(1)}, u32[]{:S(2)}, u32[]{:S(2)}) %collective-permute-start.1) | collective-permute-done | bytes 65568 | tf_op jit(solution)/shard_map/ppermute | solution.py:240
  28.1 3.2 %collective-permute-start.2 = (f32[128,128]{1,0:T(8,128)S(1)}, f32[128,128]{1,0:T(8,128)S(1)}, u32[]{:S(2)}, u32[]{:S(2)}) collective-permute-start(f32[128,128]{1,0:T(8,128)S(1)} %add.30), channel_id=1, source_target_pairs={{0,2},{1,3},{2,0},{3,1},{4,6},{5,7},{6,4},{7,5},{8,10},{9,11},{10,... | collective-permute-start | bytes 196616 | tf_op jit(solution)/shard_map/ppermute | solution.py:240
  31.3 2.1 %collective-permute-done.2 = f32[128,128]{1,0:T(8,128)S(1)} collective-permute-done((f32[128,128]{1,0:T(8,128)S(1)}, f32[128,128]{1,0:T(8,128)S(1)}, u32[]{:S(2)}, u32[]{:S(2)}) %collective-permute-start.2) | collective-permute-done | bytes 65568 | tf_op jit(solution)/shard_map/ppermute | solution.py:240
  33.4 4.2 %collective-permute-start.3 = (f32[128,128]{1,0:T(8,128)S(1)}, f32[128,128]{1,0:T(8,128)S(1)}, u32[]{:S(2)}, u32[]{:S(2)}) collective-permute-start(f32[128,128]{1,0:T(8,128)S(1)} %add.31), channel_id=1, source_target_pairs={{0,4},{1,5},{2,6},{3,7},{4,0},{5,1},{6,2},{7,3},{8,12},{9,13},{10,... | collective-permute-start | bytes 196616 | tf_op jit(solution)/shard_map/ppermute | solution.py:240
  37.7 0.0 copy-done
  37.7 0.1 dynamic-slice.2
  37.8 1.9 %collective-permute-done.3 = f32[128,128]{1,0:T(8,128)S(1)} collective-permute-done((f32[128,128]{1,0:T(8,128)S(1)}, f32[128,128]{1,0:T(8,128)S(1)}, u32[]{:S(2)}, u32[]{:S(2)}) %collective-permute-start.3) | collective-permute-done | bytes 65568 | tf_op jit(solution)/shard_map/ppermute | solution.py:240
  39.7 8.2 %collective-permute-start.4 = (f32[128,128]{1,0:T(8,128)S(1)}, f32[128,128]{1,0:T(8,128)S(1)}, u32[]{:S(2)}, u32[]{:S(2)}) collective-permute-start(f32[128,128]{1,0:T(8,128)S(1)} %add.32), channel_id=1, source_target_pairs={{0,8},{1,9},{2,10},{3,11},{4,12},{5,13},{6,14},{7,15},{8,0},{9,1},... | collective-permute-start | bytes 196616 | tf_op jit(solution)/shard_map/ppermute | solution.py:240
  47.8 0.0 copy-done.1
  47.8 0.7 fusion.2
  49.7 0.0 collective-permute-done.4
  49.8 0.1 fusion.strip_ref
  49.8 16.0 %all-to-all-done.pieces_ref = bf16[16,128,512]{2,1,0:T(8,128)(2,1)S(1)} async-done(((bf16[16,128,512]{2,1,0:T(8,128)(2,1)}), bf16[16,128,512]{2,1,0:T(8,128)(2,1)S(1)}, u32[]{:S(2)}, u32[]{:S(2)}) %all-to-all-start) | async-done | bytes 2097184 | tf_op jit(solution)/shard_map/all_to_all | solution.py:252
  65.8 0.7 shard_map.39
  66.6 5.2 %collective-permute-start.5 = (f32[16,16,8,128]{3,2,1,0:T(8,128)S(1)}, f32[16,16,8,128]{3,2,1,0:T(8,128)}, u32[]{:S(2)}, u32[]{:S(2)}) collective-permute-start(f32[16,16,8,128]{3,2,1,0:T(8,128)S(1)} %shard_map.39), channel_id=1, source_target_pairs={{0,1},{1,0},{2,3},{3,2},{4,5},{5,4},{6,7},{7,6},{8,9},{9,8},{10,11... | collective-permute-start | bytes 3145736 | tf_op jit(solution)/shard_map/ppermute | solution.py:240
  72.9 0.7 shard_map.38.mine_ref
  73.7 0.5 collective-permute-done.5.theirs_ref
  74.1 2.2 %shard_map.40 = f32[16,17,8,128]{3,2,1,0:T(8,128)} custom-call(s32[1]{0:T(128)} %bitcast.4.core_ref, f32[16,16,8,128]{3,2,1,0:T(8,128)S(1)} %shard_map.38.mine_ref, f32[16,16,8,128]{3,2,1,0:T(8,128)} %collective-permute-done.5.theirs_ref, f32[8,128]{1,0:T(8,128)S(1)} %fusion.strip_ref), custom_call_target="tpu_custom_call" | custom-call | flops 1048576 | bytes 4194304 | tf_op jit(solution)/shard_map/pallas_call | solution.py:168
  76.3 3.7 %all-to-all-start.1 = ((f32[16,17,8,128]{3,2,1,0:T(8,128)}), f32[16,17,8,128]{3,2,1,0:T(8,128)S(1)}, u32[]{:S(2)}, u32[]{:S(2)}) async-start(f32[16,17,8,128]{3,2,1,0:T(8,128)} %shard_map.40), calls=%async_computation.1 | async-start | bytes 2228224 | tf_op jit(solution)/shard_map/all_to_all | solution.py:266
  83.8 16.4 %all-to-all-done.1 = f32[16,17,8,128]{3,2,1,0:T(8,128)S(1)} async-done(((f32[16,17,8,128]{3,2,1,0:T(8,128)}), f32[16,17,8,128]{3,2,1,0:T(8,128)S(1)}, u32[]{:S(2)}, u32[]{:S(2)}) %all-to-all-start.1) | async-done | bytes 1114144 | tf_op jit(solution)/shard_map/all_to_all | solution.py:266
  100.2 0.1 slice_reduce_fusion
  100.3 14.9 %all_to_all.20 = f32[16,3,8,128]{3,2,1,0:T(8,128)S(1)} all-to-all(f32[16,3,8,128]{3,2,1,0:T(8,128)S(1)} %pad_maximum_fusion), channel_id=1, replica_groups={{0,32,64,96,128,160,192,224,256,288,320,352,384,416,448,480},{2,34,66,9..., dimensions={0} | all-to-all | bytes 393216 | tf_op jit(solution)/shard_map/all_to_all | solution.py:276
  115.2 0.7 broadcast_in_dim.20
  115.9 3.6 %all-to-all-start.3 = ((f32[16,2,8,128]{3,2,1,0:T(8,128)}), f32[16,2,8,128]{3,2,1,0:T(8,128)S(1)}, u32[]{:S(2)}, u32[]{:S(2)}) async-start(f32[16,2,8,128]{3,2,1,0:T(8,128)} %broadcast_in_dim.20), calls=%async_computation.3 | async-start | bytes 262144 | tf_op jit(solution)/shard_map/all_to_all | solution.py:281
  119.5 6.5 %collective-permute-start.6 = (f32[16,2,8,128]{3,2,1,0:T(8,128)S(1)}, f32[16,2,8,128]{3,2,1,0:T(8,128)S(1)}, u32[]{:S(2)}, u32[]{:S(2)}) collective-permute-start(f32[16,2,8,128]{3,2,1,0:T(8,128)S(1)} %get-tuple-element.17.mine_ref), channel_id=1, source_target_pairs={{0,1},{1,0},{2,3},{3,2},{4,5},{5,4},{6,7},{7,6},{8,9},{9,8},{10,11... | collective-permute-start | bytes 393224 | tf_op jit(solution)/shard_map/ppermute | solution.py:240
  126.0 1.0 collective-permute-done.6.theirs_ref
  126.9 3.9 %shard_map.41 = (f32[128,128]{1,0:T(8,128)S(1)}, f32[128,128]{1,0:T(8,128)S(1)}) custom-call(s32[1]{0:T(128)} %bitcast.4.core_ref, f32[16,2,8,128]{3,2,1,0:T(8,128)S(1)} %get-tuple-element.17.mine_ref, f32[16,2,8,128]{3,2,1,0:T(8,128)S(1)} %collective-permute-done.6.theirs_ref), custom_call_target="tpu_custom_call" | custom-call | flops 20971520 | bytes 1048576 | tf_op jit(solution)/shard_map/pallas_call | solution.py:196
  130.8 0.0 all-to-all-done.3.mine_ref
  130.8 3.7 %collective-permute-start.7 = (f32[16,2,8,128]{3,2,1,0:T(8,128)S(1)}, f32[16,2,8,128]{3,2,1,0:T(8,128)S(1)}, u32[]{:S(2)}, u32[]{:S(2)}) collective-permute-start(f32[16,2,8,128]{3,2,1,0:T(8,128)S(1)} %all-to-all-done.3.mine_ref), channel_id=1, source_target_pairs={{0,1},{1,0},{2,3},{3,2},{4,5},{5,4},{6,7},{7,6},{8,9},{9,8},{10,11... | collective-permute-start | bytes 393224 | tf_op jit(solution)/shard_map/ppermute | solution.py:240
  135.8 0.1 pad_add_fusion.flags_ref
  135.8 0.0 collective-permute-done.7.theirs_ref
  135.8 5.9 %shard_map.42 = f32[128,256]{1,0:T(8,128)} custom-call(s32[3]{0:T(128)S(1)} %pad_add_fusion.flags_ref, f32[16,2,8,128]{3,2,1,0:T(8,128)S(1)} %all-to-all-done.3.mine_ref, f32[16,2,8,128]{3,2,1,0:T(8,128)S(1)} %collective-permute-done.7.theirs_ref, f32[1,128]{1,0:T(1,128)S(1)} %bitcast.17, f32[128,128]{1,0:T(8,128)S(1)} %get-tuple-element.15.inverse_ref, ...), custom_call_target="tpu_custom_call" | custom-call | flops 67108864 | bytes 1048576 | tf_op jit(solution)/shard_map/pallas_call | solution.py:229
  (11 shorter events, 0.1 us)
Async XLA Ops:
  2.6 63.2 %all-to-all-start = ((bf16[16,128,512]{2,1,0:T(8,128)(2,1)}), bf16[16,128,512]{2,1,0:T(8,128)(2,1)S(1)}, u32[]{:S(2)}, u32[]{:S(2)}) async-start(bf16[16,128,512]{2,1,0:T(8,128)(2,1)} %shard_map.37), calls=%async_computation | async-start | bytes 4194304 | tf_op jit(solution)/shard_map/all_to_all | solution.py:252
  16.1 21.6 %copy-start = (f32[128]{0:T(128)S(1)}, f32[128]{0:T(128)}, u32[]{:S(2)}) copy-start(f32[128]{0:T(128)} %param.4) | copy-start | bytes 1540
  16.1 31.7 %copy-start.1 = (s32[16]{0:T(128)S(1)}, s32[16]{0:T(128)}, u32[]{:S(2)}) copy-start(s32[16]{0:T(128)} %param.5) | copy-start | bytes 196
  19.0 3.7 %collective-permute-start = (f32[128,128]{1,0:T(8,128)S(1)}, f32[128,128]{1,0:T(8,128)S(1)}, u32[]{:S(2)}, u32[]{:S(2)}) collective-permute-start(f32[128,128]{1,0:T(8,128)S(1)} %fusion.3), channel_id=1, source_target_pairs={{0,1},{1,0},{2,3},{3,2},{4,5},{5,4},{6,7},{7,6},{8,9},{9,8},{10,11... | collective-permute-start | bytes 196616 | tf_op jit(solution)/shard_map/ppermute | solution.py:240
  22.8 5.3 %collective-permute-start.1 = (f32[128,128]{1,0:T(8,128)S(1)}, f32[128,128]{1,0:T(8,128)S(1)}, u32[]{:S(2)}, u32[]{:S(2)}) collective-permute-start(f32[128,128]{1,0:T(8,128)S(1)} %add.29), channel_id=1, source_target_pairs={{0,16},{1,17},{2,18},{3,19},{4,20},{5,21},{6,22},{7,23},{8,24},{9,... | collective-permute-start | bytes 196616 | tf_op jit(solution)/shard_map/ppermute | solution.py:240
  28.1 5.3 %collective-permute-start.2 = (f32[128,128]{1,0:T(8,128)S(1)}, f32[128,128]{1,0:T(8,128)S(1)}, u32[]{:S(2)}, u32[]{:S(2)}) collective-permute-start(f32[128,128]{1,0:T(8,128)S(1)} %add.30), channel_id=1, source_target_pairs={{0,2},{1,3},{2,0},{3,1},{4,6},{5,7},{6,4},{7,5},{8,10},{9,11},{10,... | collective-permute-start | bytes 196616 | tf_op jit(solution)/shard_map/ppermute | solution.py:240
  33.4 6.2 %collective-permute-start.3 = (f32[128,128]{1,0:T(8,128)S(1)}, f32[128,128]{1,0:T(8,128)S(1)}, u32[]{:S(2)}, u32[]{:S(2)}) collective-permute-start(f32[128,128]{1,0:T(8,128)S(1)} %add.31), channel_id=1, source_target_pairs={{0,4},{1,5},{2,6},{3,7},{4,0},{5,1},{6,2},{7,3},{8,12},{9,13},{10,... | collective-permute-start | bytes 196616 | tf_op jit(solution)/shard_map/ppermute | solution.py:240
  39.7 10.1 %collective-permute-start.4 = (f32[128,128]{1,0:T(8,128)S(1)}, f32[128,128]{1,0:T(8,128)S(1)}, u32[]{:S(2)}, u32[]{:S(2)}) collective-permute-start(f32[128,128]{1,0:T(8,128)S(1)} %add.32), channel_id=1, source_target_pairs={{0,8},{1,9},{2,10},{3,11},{4,12},{5,13},{6,14},{7,15},{8,0},{9,1},... | collective-permute-start | bytes 196616 | tf_op jit(solution)/shard_map/ppermute | solution.py:240
  66.6 7.6 %collective-permute-start.5 = (f32[16,16,8,128]{3,2,1,0:T(8,128)S(1)}, f32[16,16,8,128]{3,2,1,0:T(8,128)}, u32[]{:S(2)}, u32[]{:S(2)}) collective-permute-start(f32[16,16,8,128]{3,2,1,0:T(8,128)S(1)} %shard_map.39), channel_id=1, source_target_pairs={{0,1},{1,0},{2,3},{3,2},{4,5},{5,4},{6,7},{7,6},{8,9},{9,8},{10,11... | collective-permute-start | bytes 3145736 | tf_op jit(solution)/shard_map/ppermute | solution.py:240
  76.3 23.8 %all-to-all-start.1 = ((f32[16,17,8,128]{3,2,1,0:T(8,128)}), f32[16,17,8,128]{3,2,1,0:T(8,128)S(1)}, u32[]{:S(2)}, u32[]{:S(2)}) async-start(f32[16,17,8,128]{3,2,1,0:T(8,128)} %shard_map.40), calls=%async_computation.1 | async-start | bytes 2228224 | tf_op jit(solution)/shard_map/all_to_all | solution.py:266
  115.9 14.9 %all-to-all-start.3 = ((f32[16,2,8,128]{3,2,1,0:T(8,128)}), f32[16,2,8,128]{3,2,1,0:T(8,128)S(1)}, u32[]{:S(2)}, u32[]{:S(2)}) async-start(f32[16,2,8,128]{3,2,1,0:T(8,128)} %broadcast_in_dim.20), calls=%async_computation.3 | async-start | bytes 262144 | tf_op jit(solution)/shard_map/all_to_all | solution.py:281
  119.5 7.4 %collective-permute-start.6 = (f32[16,2,8,128]{3,2,1,0:T(8,128)S(1)}, f32[16,2,8,128]{3,2,1,0:T(8,128)S(1)}, u32[]{:S(2)}, u32[]{:S(2)}) collective-permute-start(f32[16,2,8,128]{3,2,1,0:T(8,128)S(1)} %get-tuple-element.17.mine_ref), channel_id=1, source_target_pairs={{0,1},{1,0},{2,3},{3,2},{4,5},{5,4},{6,7},{7,6},{8,9},{9,8},{10,11... | collective-permute-start | bytes 393224 | tf_op jit(solution)/shard_map/ppermute | solution.py:240
  130.8 5.1 %collective-permute-start.7 = (f32[16,2,8,128]{3,2,1,0:T(8,128)S(1)}, f32[16,2,8,128]{3,2,1,0:T(8,128)S(1)}, u32[]{:S(2)}, u32[]{:S(2)}) collective-permute-start(f32[16,2,8,128]{3,2,1,0:T(8,128)S(1)} %all-to-all-done.3.mine_ref), channel_id=1, source_target_pairs={{0,1},{1,0},{2,3},{3,2},{4,5},{5,4},{6,7},{7,6},{8,9},{9,8},{10,11... | collective-permute-start | bytes 393224 | tf_op jit(solution)/shard_map/ppermute | solution.py:240

commit v6 on v5

--- a/solution.py
+++ b/solution.py
@@ -203,21 +203,19 @@
     )(core[None], mine, theirs)
 
 
-def last_kernel(flags_ref, mine_ref, theirs_ref, shift_ref, inverse_ref, other_ref, out_ref):
+def last_kernel(owns_ref, strips_ref, shift_ref, inverse_ref, other_ref, out_ref):
     row = lax.broadcasted_iota(jnp.int32, (ROWS, ROWS), 0)
     column = lax.broadcasted_iota(jnp.int32, (ROWS, ROWS), 1)
 
-    def item(k, i):
-        mine = mine_ref[:, i].reshape(ROWS, ROWS)
-        theirs = theirs_ref[:, i].reshape(ROWS, ROWS)
-        return jnp.where(flags_ref[2] == k, mine, theirs)
+    def item(i):
+        return strips_ref[:, i].reshape(ROWS, ROWS)
 
     def own(k):
-        add = (row == column) & (flags_ref[k] == 1)
-        return item(k, 0) + jnp.where(add, shift_ref[...], 0.0)
+        add = (row == column) & (owns_ref[k] == 1)
+        return item(k) + jnp.where(add, shift_ref[...], 0.0)
 
     inverse = inverse_ref[...]
-    remote = exact(inverse, item(0, 1), ((1,), (0,)))
+    remote = exact(inverse, item(2), ((1,), (0,)))
     second = inverse_factor(other_ref[...] - exact(remote, remote, ((0,), (0,))))
     zero = exact(inverse, own(0), ((1,), (0,)))
     rest = own(1) - exact(remote, zero, ((0,), (0,)))
@@ -225,15 +223,15 @@
     out_ref[:, ROWS:] = exact(second, rest, ((1,), (0,))).T
 
 
-def last_factor(flags, mine, theirs, shift, inverse, other):
+def last_factor(owns, strips, shift, inverse, other):
     return pl.pallas_call(
         last_kernel,
         out_shape=jax.ShapeDtypeStruct((ROWS, 2 * ROWS), jnp.float32),
-        in_specs=[SMEM] + [VMEM] * 5,
+        in_specs=[SMEM] + [VMEM] * 4,
         out_specs=VMEM,
         compiler_params=pltpu.CompilerParams(vmem_limit_bytes=16 << 20),
         cost_estimate=pl.CostEstimate(flops=64 << 20, bytes_accessed=1 << 20, transcendentals=0),
-    )(flags, mine, theirs, shift, inverse, other)
+    )(owns, strips, shift, inverse, other)
 
 
 def flip(block, bit):
@@ -276,15 +274,19 @@
     total = lax.all_to_all(total, axes, 0, 0, axis_index_groups=SAMP_THEN_CHIPS, tiled=True)
     blocks = total[:, 1:]
     total = total[:, :2].sum(0)
-
-    copies = jnp.broadcast_to(total[None], (CHIPS,) + total.shape)
-    gathered = lax.all_to_all(copies, "par", 0, 0, axis_index_groups=CHIPS_BY_CORE, tiled=True)
+    across = flip(total, 1)
+    three = jnp.stack([
+        jnp.where(core == 0, total[0], across[0]),
+        jnp.where(core == 0, across[0], total[0]),
+        jnp.where(core == 0, total[1], across[1]),
+    ])
+    three, blocks = lax.optimization_barrier((three, blocks))
+
+    copies = jnp.broadcast_to(three[None], (CHIPS,) + three.shape)
+    strips = lax.all_to_all(copies, "par", 0, 0, axis_index_groups=CHIPS_BY_CORE, tiled=True)
     inverse, other = first_factor(core, blocks, flip(blocks, 1))
-    gathered, inverse = lax.optimization_barrier((gathered, inverse))
-    flags = jnp.stack([
-        (panel_ids[0] == here).astype(jnp.int32), (panel_ids[1] == here).astype(jnp.int32), core
-    ])
-    return last_factor(flags, gathered, flip(gathered, 1), shift[None, :], inverse, other)
+    owns = jnp.stack([panel_ids[0] == here, panel_ids[1] == here]).astype(jnp.int32)
+    return last_factor(owns, strips, shift[None, :], inverse, other)
 
 
 def solution(mesh):

time: 142 us -> 142 us (level); the launches traced: 142 us -> 140 us
    ppermute x8, starting transfers between devices: 36 us -> 33.1 us  [flip(): return lax.ppermute(block, 'par', [(i, i ^ bit) for i in range(PAR)])]
    all_to_all x1, starting transfers between devices: 3.63 us -> 5.18 us  [per_device(): lax.all_to_all(copies, 'par', 0, 0, axis_index_groups=CHIPS_BY_CORE, tile...]
where the time goes in v6:
time: 142 us; the launch traced here: 140 us
  starting transfers between devices  55.4 us (39%)
  waiting for transfers between devices  41.2 us (29%)
  Pallas kernels  16 us (11%)
  blocking collectives  14.8 us (10%)
  between operations  8.19 us (6%)
  matrix products  2.93 us (2%)
  local copies, waits for them, and re-layouts  1.47 us (1%)
    ppermute x8, starting transfers between devices, flip(): return lax.ppermute(block, 'par', [(i, i ^ bit) for i in range(PAR)])  33.1 us
    all_to_all x1, waiting for transfers between devices, per_device(): lax.all_to_all(total, axes, 0, 0, axis_index_groups=CHIPS_THEN_SAMP, tile...  16.2 us
    all_to_all x1, waiting for transfers between devices, per_device(): pieces = lax.all_to_all(cut(samples), 'samp', 0, 0, tiled=True)  15.9 us
    all_to_all x1, blocking collectives, per_device(): lax.all_to_all(total, axes, 0, 0, axis_index_groups=SAMP_THEN_CHIPS, tile...  14.8 us
    all_to_all x1, starting transfers between devices, per_device(): pieces = lax.all_to_all(cut(samples), 'samp', 0, 0, tiled=True)  13.4 us
    ppermute x8, waiting for transfers between devices, flip(): return lax.ppermute(block, 'par', [(i, i ^ bit) for i in range(PAR)])  9.12 us
    pallas_call x1, Pallas kernels, last_factor(): pl.pallas_call(last_kernel, out_shape=jax.ShapeDtypeStruct((ROWS, 2 * ROW...  5.91 us
    all_to_all x1, starting transfers between devices, per_device(): lax.all_to_all(copies, 'par', 0, 0, axis_index_groups=CHIPS_BY_CORE, tile...  5.18 us
  transfers between devices with their start and end apart: 11, of which 8 were waited for; matrix products, arithmetic and copies ran while one was open for 3% of the time, Pallas kernels for 3%

profile of v6, /device:TPU:1, one launch (start us, length us, event | category | flops | bytes accessed | tf_op | source)
XLA Modules:
  0.0 140.3 jit_solution(4886992019474082329)
XLA Ops:
  0.0 2.6 %shard_map.37 = bf16[16,128,512]{2,1,0:T(8,128)(2,1)} custom-call(bf16[128,8192]{1,0:T(8,128)(2,1)} %samples_ref.1), custom_call_target="tpu_custom_call" | custom-call | bytes 4194304 | tf_op jit(solution)/shard_map/pallas_call | solution.py:92
  2.6 13.4 %all-to-all-start = ((bf16[16,128,512]{2,1,0:T(8,128)(2,1)}), bf16[16,128,512]{2,1,0:T(8,128)(2,1)S(1)}, u32[]{:S(2)}, u32[]{:S(2)}) async-start(bf16[16,128,512]{2,1,0:T(8,128)(2,1)} %shard_map.37), calls=%async_computation | async-start | bytes 4194304 | tf_op jit(solution)/shard_map/all_to_all | solution.py:250
  16.1 0.0 copy-start
  16.1 0.0 copy-start.1
  16.1 2.9 %fusion.3 = f32[128,128]{1,0:T(8,128)S(1)} fusion(bf16[128,8192]{1,0:T(8,128)(2,1)} %samples_ref.1), kind=kOutput, calls=%fused_computation.15 | convolution fusion | flops 268435456 | bytes 2162688 | tf_op jit(solution)/shard_map/dot_general | solution.py:252
  19.1 2.9 %collective-permute-start = (f32[128,128]{1,0:T(8,128)S(1)}, f32[128,128]{1,0:T(8,128)S(1)}, u32[]{:S(2)}, u32[]{:S(2)}) collective-permute-start(f32[128,128]{1,0:T(8,128)S(1)} %fusion.3), channel_id=1, source_target_pairs={{0,1},{1,0},{2,3},{3,2},{4,5},{5,4},{6,7},{7,6},{8,9},{9,8},{10,11... | collective-permute-start | bytes 196616 | tf_op jit(solution)/shard_map/ppermute | solution.py:238
  21.9 0.9 collective-permute-done
  22.8 2.2 %collective-permute-start.1 = (f32[128,128]{1,0:T(8,128)S(1)}, f32[128,128]{1,0:T(8,128)S(1)}, u32[]{:S(2)}, u32[]{:S(2)}) collective-permute-start(f32[128,128]{1,0:T(8,128)S(1)} %add.29), channel_id=1, source_target_pairs={{0,16},{1,17},{2,18},{3,19},{4,20},{5,21},{6,22},{7,23},{8,24},{9,... | collective-permute-start | bytes 196616 | tf_op jit(solution)/shard_map/ppermute | solution.py:238
  25.0 3.1 %collective-permute-done.1 = f32[128,128]{1,0:T(8,128)S(1)} collective-permute-done((f32[128,128]{1,0:T(8,128)S(1)}, f32[128,128]{1,0:T(8,128)S(1)}, u32[]{:S(2)}, u32[]{:S(2)}) %collective-permute-start.1) | collective-permute-done | bytes 65568 | tf_op jit(solution)/shard_map/ppermute | solution.py:238
  28.1 3.2 %collective-permute-start.2 = (f32[128,128]{1,0:T(8,128)S(1)}, f32[128,128]{1,0:T(8,128)S(1)}, u32[]{:S(2)}, u32[]{:S(2)}) collective-permute-start(f32[128,128]{1,0:T(8,128)S(1)} %add.30), channel_id=1, source_target_pairs={{0,2},{1,3},{2,0},{3,1},{4,6},{5,7},{6,4},{7,5},{8,10},{9,11},{10,... | collective-permute-start | bytes 196616 | tf_op jit(solution)/shard_map/ppermute | solution.py:238
  31.3 2.1 %collective-permute-done.2 = f32[128,128]{1,0:T(8,128)S(1)} collective-permute-done((f32[128,128]{1,0:T(8,128)S(1)}, f32[128,128]{1,0:T(8,128)S(1)}, u32[]{:S(2)}, u32[]{:S(2)}) %collective-permute-start.2) | collective-permute-done | bytes 65568 | tf_op jit(solution)/shard_map/ppermute | solution.py:238
  33.5 4.2 %collective-permute-start.3 = (f32[128,128]{1,0:T(8,128)S(1)}, f32[128,128]{1,0:T(8,128)S(1)}, u32[]{:S(2)}, u32[]{:S(2)}) collective-permute-start(f32[128,128]{1,0:T(8,128)S(1)} %add.31), channel_id=1, source_target_pairs={{0,4},{1,5},{2,6},{3,7},{4,0},{5,1},{6,2},{7,3},{8,12},{9,13},{10,... | collective-permute-start | bytes 196616 | tf_op jit(solution)/shard_map/ppermute | solution.py:238
  37.7 0.0 copy-done
  37.7 0.1 dynamic-slice.2
  37.8 1.9 %collective-permute-done.3 = f32[128,128]{1,0:T(8,128)S(1)} collective-permute-done((f32[128,128]{1,0:T(8,128)S(1)}, f32[128,128]{1,0:T(8,128)S(1)}, u32[]{:S(2)}, u32[]{:S(2)}) %collective-permute-start.3) | collective-permute-done | bytes 65568 | tf_op jit(solution)/shard_map/ppermute | solution.py:238
  39.7 8.2 %collective-permute-start.4 = (f32[128,128]{1,0:T(8,128)S(1)}, f32[128,128]{1,0:T(8,128)S(1)}, u32[]{:S(2)}, u32[]{:S(2)}) collective-permute-start(f32[128,128]{1,0:T(8,128)S(1)} %add.32), channel_id=1, source_target_pairs={{0,8},{1,9},{2,10},{3,11},{4,12},{5,13},{6,14},{7,15},{8,0},{9,1},... | collective-permute-start | bytes 196616 | tf_op jit(solution)/shard_map/ppermute | solution.py:238
  47.8 0.0 copy-done.1
  47.8 0.7 fusion.2
  49.8 0.0 collective-permute-done.4
  49.8 0.1 fusion.strip_ref
  49.9 15.9 %all-to-all-done.pieces_ref = bf16[16,128,512]{2,1,0:T(8,128)(2,1)S(1)} async-done(((bf16[16,128,512]{2,1,0:T(8,128)(2,1)}), bf16[16,128,512]{2,1,0:T(8,128)(2,1)S(1)}, u32[]{:S(2)}, u32[]{:S(2)}) %all-to-all-start) | async-done | bytes 2097184 | tf_op jit(solution)/shard_map/all_to_all | solution.py:250
  65.9 0.7 shard_map.39
  66.6 5.2 %collective-permute-start.5 = (f32[16,16,8,128]{3,2,1,0:T(8,128)S(1)}, f32[16,16,8,128]{3,2,1,0:T(8,128)}, u32[]{:S(2)}, u32[]{:S(2)}) collective-permute-start(f32[16,16,8,128]{3,2,1,0:T(8,128)S(1)} %shard_map.39), channel_id=1, source_target_pairs={{0,1},{1,0},{2,3},{3,2},{4,5},{5,4},{6,7},{7,6},{8,9},{9,8},{10,11... | collective-permute-start | bytes 3145736 | tf_op jit(solution)/shard_map/ppermute | solution.py:238
  73.0 0.7 shard_map.38.mine_ref
  73.8 0.4 collective-permute-done.5.theirs_ref
  74.1 2.2 %shard_map.40 = f32[16,17,8,128]{3,2,1,0:T(8,128)} custom-call(s32[1]{0:T(128)} %bitcast.4.core_ref, f32[16,16,8,128]{3,2,1,0:T(8,128)S(1)} %shard_map.38.mine_ref, f32[16,16,8,128]{3,2,1,0:T(8,128)} %collective-permute-done.5.theirs_ref, f32[8,128]{1,0:T(8,128)S(1)} %fusion.strip_ref), custom_call_target="tpu_custom_call" | custom-call | flops 1048576 | bytes 4194304 | tf_op jit(solution)/shard_map/pallas_call | solution.py:168
  76.3 3.7 %all-to-all-start.1 = ((f32[16,17,8,128]{3,2,1,0:T(8,128)}), f32[16,17,8,128]{3,2,1,0:T(8,128)S(1)}, u32[]{:S(2)}, u32[]{:S(2)}) async-start(f32[16,17,8,128]{3,2,1,0:T(8,128)} %shard_map.40), calls=%async_computation.1 | async-start | bytes 2228224 | tf_op jit(solution)/shard_map/all_to_all | solution.py:264
  84.0 16.2 %all-to-all-done.1 = f32[16,17,8,128]{3,2,1,0:T(8,128)S(1)} async-done(((f32[16,17,8,128]{3,2,1,0:T(8,128)}), f32[16,17,8,128]{3,2,1,0:T(8,128)S(1)}, u32[]{:S(2)}, u32[]{:S(2)}) %all-to-all-start.1) | async-done | bytes 1114144 | tf_op jit(solution)/shard_map/all_to_all | solution.py:264
  100.2 0.1 slice_reduce_fusion
  100.3 14.8 %all_to_all.20 = f32[16,3,8,128]{3,2,1,0:T(8,128)S(1)} all-to-all(f32[16,3,8,128]{3,2,1,0:T(8,128)S(1)} %pad_maximum_fusion), channel_id=1, replica_groups={{0,32,64,96,128,160,192,224,256,288,320,352,384,416,448,480},{2,34,66,9..., dimensions={0} | all-to-all | bytes 393216 | tf_op jit(solution)/shard_map/all_to_all | solution.py:274
  115.2 4.7 %collective-permute-start.6 = (f32[2,8,128]{2,1,0:T(8,128)S(1)}, f32[2,8,128]{2,1,0:T(8,128)S(1)}, u32[]{:S(2)}, u32[]{:S(2)}) collective-permute-start(f32[2,8,128]{2,1,0:T(8,128)S(1)} %get-tuple-element.18), channel_id=1, source_target_pairs={{0,1},{1,0},{2,3},{3,2},{4,5},{5,4},{6,7},{7,6},{8,9},{9,8},{10,11... | collective-permute-start | bytes 24584 | tf_op jit(solution)/shard_map/ppermute | solution.py:238
  119.9 0.8 collective-permute-done.6
  120.7 0.7 broadcast_in_dim.23
  121.4 5.2 %all-to-all-start.3 = ((f32[16,3,8,128]{3,2,1,0:T(8,128)}), f32[16,3,8,128]{3,2,1,0:T(8,128)S(1)}, u32[]{:S(2)}, u32[]{:S(2)}) async-start(f32[16,3,8,128]{3,2,1,0:T(8,128)} %broadcast_in_dim.23), calls=%async_computation.3 | async-start | bytes 393216 | tf_op jit(solution)/shard_map/all_to_all | solution.py:286
  126.6 2.5 %collective-permute-start.7 = (f32[16,2,8,128]{3,2,1,0:T(8,128)S(1)}, f32[16,2,8,128]{3,2,1,0:T(8,128)S(1)}, u32[]{:S(2)}, u32[]{:S(2)}) collective-permute-start(f32[16,2,8,128]{3,2,1,0:T(8,128)S(1)} %get-tuple-element.14.mine_ref), channel_id=1, source_target_pairs={{0,1},{1,0},{2,3},{3,2},{4,5},{5,4},{6,7},{7,6},{8,9},{9,8},{10,11... | collective-permute-start | bytes 393224 | tf_op jit(solution)/shard_map/ppermute | solution.py:238
  130.5 0.1 add_convert_fusion.owns_ref
  130.5 0.0 collective-permute-done.7.theirs_ref
  130.5 3.9 %shard_map.41 = (f32[128,128]{1,0:T(8,128)S(1)}, f32[128,128]{1,0:T(8,128)S(1)}) custom-call(s32[1]{0:T(128)} %bitcast.4.core_ref, f32[16,2,8,128]{3,2,1,0:T(8,128)S(1)} %get-tuple-element.14.mine_ref, f32[16,2,8,128]{3,2,1,0:T(8,128)S(1)} %collective-permute-done.7.theirs_ref), custom_call_target="tpu_custom_call" | custom-call | flops 20971520 | bytes 1048576 | tf_op jit(solution)/shard_map/pallas_call | solution.py:196
  134.4 0.0 all-to-all-done.3.strips_ref
  134.4 5.9 %shard_map.42 = f32[128,256]{1,0:T(8,128)} custom-call(s32[2]{0:T(128)S(1)} %add_convert_fusion.owns_ref, f32[16,3,8,128]{3,2,1,0:T(8,128)S(1)} %all-to-all-done.3.strips_ref, f32[1,128]{1,0:T(1,128)S(1)} %bitcast.17, f32[128,128]{1,0:T(8,128)S(1)} %get-tuple-element.15.inverse_ref, f32[128,128]{1,0:T(8,128)S(1)} %get-tuple-element.16.other_ref), custom_call_target="tpu_custom_call" | custom-call | flops 67108864 | bytes 1048576 | tf_op jit(solution)/shard_map/pallas_call | solution.py:227
  (13 shorter events, 0.1 us)
Async XLA Ops:
  2.6 63.2 %all-to-all-start = ((bf16[16,128,512]{2,1,0:T(8,128)(2,1)}), bf16[16,128,512]{2,1,0:T(8,128)(2,1)S(1)}, u32[]{:S(2)}, u32[]{:S(2)}) async-start(bf16[16,128,512]{2,1,0:T(8,128)(2,1)} %shard_map.37), calls=%async_computation | async-start | bytes 4194304 | tf_op jit(solution)/shard_map/all_to_all | solution.py:250
  16.1 21.6 %copy-start = (f32[128]{0:T(128)S(1)}, f32[128]{0:T(128)}, u32[]{:S(2)}) copy-start(f32[128]{0:T(128)} %param.4) | copy-start | bytes 1540
  16.1 31.7 %copy-start.1 = (s32[16]{0:T(128)S(1)}, s32[16]{0:T(128)}, u32[]{:S(2)}) copy-start(s32[16]{0:T(128)} %param.5) | copy-start | bytes 196
  19.1 3.8 %collective-permute-start = (f32[128,128]{1,0:T(8,128)S(1)}, f32[128,128]{1,0:T(8,128)S(1)}, u32[]{:S(2)}, u32[]{:S(2)}) collective-permute-start(f32[128,128]{1,0:T(8,128)S(1)} %fusion.3), channel_id=1, source_target_pairs={{0,1},{1,0},{2,3},{3,2},{4,5},{5,4},{6,7},{7,6},{8,9},{9,8},{10,11... | collective-permute-start | bytes 196616 | tf_op jit(solution)/shard_map/ppermute | solution.py:238
  22.8 5.3 %collective-permute-start.1 = (f32[128,128]{1,0:T(8,128)S(1)}, f32[128,128]{1,0:T(8,128)S(1)}, u32[]{:S(2)}, u32[]{:S(2)}) collective-permute-start(f32[128,128]{1,0:T(8,128)S(1)} %add.29), channel_id=1, source_target_pairs={{0,16},{1,17},{2,18},{3,19},{4,20},{5,21},{6,22},{7,23},{8,24},{9,... | collective-permute-start | bytes 196616 | tf_op jit(solution)/shard_map/ppermute | solution.py:238
  28.1 5.3 %collective-permute-start.2 = (f32[128,128]{1,0:T(8,128)S(1)}, f32[128,128]{1,0:T(8,128)S(1)}, u32[]{:S(2)}, u32[]{:S(2)}) collective-permute-start(f32[128,128]{1,0:T(8,128)S(1)} %add.30), channel_id=1, source_target_pairs={{0,2},{1,3},{2,0},{3,1},{4,6},{5,7},{6,4},{7,5},{8,10},{9,11},{10,... | collective-permute-start | bytes 196616 | tf_op jit(solution)/shard_map/ppermute | solution.py:238
  33.5 6.2 %collective-permute-start.3 = (f32[128,128]{1,0:T(8,128)S(1)}, f32[128,128]{1,0:T(8,128)S(1)}, u32[]{:S(2)}, u32[]{:S(2)}) collective-permute-start(f32[128,128]{1,0:T(8,128)S(1)} %add.31), channel_id=1, source_target_pairs={{0,4},{1,5},{2,6},{3,7},{4,0},{5,1},{6,2},{7,3},{8,12},{9,13},{10,... | collective-permute-start | bytes 196616 | tf_op jit(solution)/shard_map/ppermute | solution.py:238
  39.7 10.2 %collective-permute-start.4 = (f32[128,128]{1,0:T(8,128)S(1)}, f32[128,128]{1,0:T(8,128)S(1)}, u32[]{:S(2)}, u32[]{:S(2)}) collective-permute-start(f32[128,128]{1,0:T(8,128)S(1)} %add.32), channel_id=1, source_target_pairs={{0,8},{1,9},{2,10},{3,11},{4,12},{5,13},{6,14},{7,15},{8,0},{9,1},... | collective-permute-start | bytes 196616 | tf_op jit(solution)/shard_map/ppermute | solution.py:238
  66.6 7.6 %collective-permute-start.5 = (f32[16,16,8,128]{3,2,1,0:T(8,128)S(1)}, f32[16,16,8,128]{3,2,1,0:T(8,128)}, u32[]{:S(2)}, u32[]{:S(2)}) collective-permute-start(f32[16,16,8,128]{3,2,1,0:T(8,128)S(1)} %shard_map.39), channel_id=1, source_target_pairs={{0,1},{1,0},{2,3},{3,2},{4,5},{5,4},{6,7},{7,6},{8,9},{9,8},{10,11... | collective-permute-start | bytes 3145736 | tf_op jit(solution)/shard_map/ppermute | solution.py:238
  76.3 23.9 %all-to-all-start.1 = ((f32[16,17,8,128]{3,2,1,0:T(8,128)}), f32[16,17,8,128]{3,2,1,0:T(8,128)S(1)}, u32[]{:S(2)}, u32[]{:S(2)}) async-start(f32[16,17,8,128]{3,2,1,0:T(8,128)} %shard_map.40), calls=%async_computation.1 | async-start | bytes 2228224 | tf_op jit(solution)/shard_map/all_to_all | solution.py:264
  115.2 5.5 %collective-permute-start.6 = (f32[2,8,128]{2,1,0:T(8,128)S(1)}, f32[2,8,128]{2,1,0:T(8,128)S(1)}, u32[]{:S(2)}, u32[]{:S(2)}) collective-permute-start(f32[2,8,128]{2,1,0:T(8,128)S(1)} %get-tuple-element.18), channel_id=1, source_target_pairs={{0,1},{1,0},{2,3},{3,2},{4,5},{5,4},{6,7},{7,6},{8,9},{9,8},{10,11... | collective-permute-start | bytes 24584 | tf_op jit(solution)/shard_map/ppermute | solution.py:238
  121.4 13.0 %all-to-all-start.3 = ((f32[16,3,8,128]{3,2,1,0:T(8,128)}), f32[16,3,8,128]{3,2,1,0:T(8,128)S(1)}, u32[]{:S(2)}, u32[]{:S(2)}) async-start(f32[16,3,8,128]{3,2,1,0:T(8,128)} %broadcast_in_dim.23), calls=%async_computation.3 | async-start | bytes 393216 | tf_op jit(solution)/shard_map/all_to_all | solution.py:286
  126.6 3.9 %collective-permute-start.7 = (f32[16,2,8,128]{3,2,1,0:T(8,128)S(1)}, f32[16,2,8,128]{3,2,1,0:T(8,128)S(1)}, u32[]{:S(2)}, u32[]{:S(2)}) collective-permute-start(f32[16,2,8,128]{3,2,1,0:T(8,128)S(1)} %get-tuple-element.14.mine_ref), channel_id=1, source_target_pairs={{0,1},{1,0},{2,3},{3,2},{4,5},{5,4},{6,7},{7,6},{8,9},{9,8},{10,11... | collective-permute-start | bytes 393224 | tf_op jit(solution)/shard_map/ppermute | solution.py:238

commit v7 on v5

--- a/solution.py
+++ b/solution.py
@@ -181,29 +181,23 @@
     )(core[None], mine, theirs, strip)
 
 
-def first_kernel(core_ref, mine_ref, theirs_ref, inverse_ref, other_ref):
-    def item(i):
-        mine = mine_ref[:, i].reshape(ROWS, ROWS)
-        theirs = theirs_ref[:, i].reshape(ROWS, ROWS)
-        return jnp.where(core_ref[0] == 1, mine, theirs)
-
-    inverse_ref[...] = inverse_factor(item(0))
-    other_ref[...] = item(1)
-
-
-def first_factor(core, mine, theirs):
-    square = jax.ShapeDtypeStruct((ROWS, ROWS), jnp.float32)
+def first_kernel(blocks_ref, pair_ref):
+    pair_ref[0] = inverse_factor(blocks_ref[:, 0].reshape(ROWS, ROWS))
+    pair_ref[1] = blocks_ref[:, 1].reshape(ROWS, ROWS)
+
+
+def first_factor(blocks):
     return pl.pallas_call(
         first_kernel,
-        out_shape=(square, square),
-        in_specs=[SMEM, VMEM, VMEM],
-        out_specs=(VMEM, VMEM),
+        out_shape=jax.ShapeDtypeStruct((2, ROWS, ROWS), jnp.float32),
+        in_specs=[VMEM],
+        out_specs=VMEM,
         compiler_params=pltpu.CompilerParams(vmem_limit_bytes=16 << 20),
         cost_estimate=pl.CostEstimate(flops=20 << 20, bytes_accessed=1 << 20, transcendentals=0),
-    )(core[None], mine, theirs)
-
-
-def last_kernel(flags_ref, mine_ref, theirs_ref, shift_ref, inverse_ref, other_ref, out_ref):
+    )(blocks)
+
+
+def last_kernel(flags_ref, mine_ref, theirs_ref, shift_ref, pair_ref, their_pair_ref, out_ref):
     row = lax.broadcasted_iota(jnp.int32, (ROWS, ROWS), 0)
     column = lax.broadcasted_iota(jnp.int32, (ROWS, ROWS), 1)
 
@@ -216,16 +210,19 @@
         add = (row == column) & (flags_ref[k] == 1)
         return item(k, 0) + jnp.where(add, shift_ref[...], 0.0)
 
-    inverse = inverse_ref[...]
+    def first(i):
+        return jnp.where(flags_ref[2] == 1, pair_ref[i], their_pair_ref[i])
+
+    inverse = first(0)
     remote = exact(inverse, item(0, 1), ((1,), (0,)))
-    second = inverse_factor(other_ref[...] - exact(remote, remote, ((0,), (0,))))
+    second = inverse_factor(first(1) - exact(remote, remote, ((0,), (0,))))
     zero = exact(inverse, own(0), ((1,), (0,)))
     rest = own(1) - exact(remote, zero, ((0,), (0,)))
     out_ref[:, :ROWS] = zero.T
     out_ref[:, ROWS:] = exact(second, rest, ((1,), (0,))).T
 
 
-def last_factor(flags, mine, theirs, shift, inverse, other):
+def last_factor(flags, mine, theirs, shift, pair, their_pair):
     return pl.pallas_call(
         last_kernel,
         out_shape=jax.ShapeDtypeStruct((ROWS, 2 * ROWS), jnp.float32),
@@ -233,7 +230,7 @@
         out_specs=VMEM,
         compiler_params=pltpu.CompilerParams(vmem_limit_bytes=16 << 20),
         cost_estimate=pl.CostEstimate(flops=64 << 20, bytes_accessed=1 << 20, transcendentals=0),
-    )(flags, mine, theirs, shift, inverse, other)
+    )(flags, mine, theirs, shift, pair, their_pair)
 
 
 def flip(block, bit):
@@ -279,12 +276,13 @@
 
     copies = jnp.broadcast_to(total[None], (CHIPS,) + total.shape)
     gathered = lax.all_to_all(copies, "par", 0, 0, axis_index_groups=CHIPS_BY_CORE, tiled=True)
-    inverse, other = first_factor(core, blocks, flip(blocks, 1))
-    gathered, inverse = lax.optimization_barrier((gathered, inverse))
+    pair = first_factor(blocks)
+    their_pair = flip(pair, 1)
+    gathered, pair, their_pair = lax.optimization_barrier((gathered, pair, their_pair))
     flags = jnp.stack([
         (panel_ids[0] == here).astype(jnp.int32), (panel_ids[1] == here).astype(jnp.int32), core
     ])
-    return last_factor(flags, gathered, flip(gathered, 1), shift[None, :], inverse, other)
+    return last_factor(flags, gathered, flip(gathered, 1), shift[None, :], pair, their_pair)
 
 
 def solution(mesh):

time: 142 us -> 143 us (level)
  transfers between devices with their start and end apart: 11 -> 11, of which waited for: 8 -> 9; matrix products, arithmetic and copies ran while one was open for 3% -> 3% of each run, Pallas kernels for 3% -> 3%
where the time goes in v7:
time: 143 us; the launch traced here: 142 us
  starting transfers between devices  56.8 us (40%)
  waiting for transfers between devices  41.8 us (29%)
  Pallas kernels  16 us (11%)
  blocking collectives  14.9 us (10%)
  between operations  7.72 us (5%)
  matrix products  2.93 us (2%)
    ppermute x8, starting transfers between devices, flip(): return lax.ppermute(block, 'par', [(i, i ^ bit) for i in range(PAR)])  36 us
    all_to_all x1, waiting for transfers between devices, per_device(): lax.all_to_all(total, axes, 0, 0, axis_index_groups=CHIPS_THEN_SAMP, tile...  16.4 us
    all_to_all x1, waiting for transfers between devices, per_device(): pieces = lax.all_to_all(cut(samples), 'samp', 0, 0, tiled=True)  16 us
    all_to_all x1, blocking collectives, per_device(): lax.all_to_all(total, axes, 0, 0, axis_index_groups=SAMP_THEN_CHIPS, tile...  14.9 us
    all_to_all x1, starting transfers between devices, per_device(): pieces = lax.all_to_all(cut(samples), 'samp', 0, 0, tiled=True)  13.4 us
    ppermute x8, waiting for transfers between devices, flip(): return lax.ppermute(block, 'par', [(i, i ^ bit) for i in range(PAR)])  9.43 us
    pallas_call x1, Pallas kernels, last_factor(): pl.pallas_call(last_kernel, out_shape=jax.ShapeDtypeStruct((ROWS, 2 * ROW...  5.92 us
    pallas_call x1, Pallas kernels, first_factor(): pl.pallas_call(first_kernel, out_shape=jax.ShapeDtypeStruct((2, ROWS, ROW...  3.85 us
  transfers between devices with their start and end apart: 11, of which 9 were waited for; matrix products, arithmetic and copies ran while one was open for 3% of the time, Pallas kernels for 3%

profile of v7, /device:TPU:1, one launch (start us, length us, event | category | flops | bytes accessed | tf_op | source)
XLA Modules:
  0.0 141.8 jit_solution(13032859878256295490)
XLA Ops:
  0.0 2.6 %shard_map.37 = bf16[16,128,512]{2,1,0:T(8,128)(2,1)} custom-call(bf16[128,8192]{1,0:T(8,128)(2,1)} %samples_ref.1), custom_call_target="tpu_custom_call" | custom-call | bytes 4194304 | tf_op jit(solution)/shard_map/pallas_call | solution.py:92
  2.6 13.4 %all-to-all-start = ((bf16[16,128,512]{2,1,0:T(8,128)(2,1)}), bf16[16,128,512]{2,1,0:T(8,128)(2,1)S(1)}, u32[]{:S(2)}, u32[]{:S(2)}) async-start(bf16[16,128,512]{2,1,0:T(8,128)(2,1)} %shard_map.37), calls=%async_computation | async-start | bytes 4194304 | tf_op jit(solution)/shard_map/all_to_all | solution.py:249
  16.1 0.0 copy-start
  16.1 0.0 copy-start.1
  16.1 2.9 %fusion.3 = f32[128,128]{1,0:T(8,128)S(1)} fusion(bf16[128,8192]{1,0:T(8,128)(2,1)} %samples_ref.1), kind=kOutput, calls=%fused_computation.11 | convolution fusion | flops 268435456 | bytes 2162688 | tf_op jit(solution)/shard_map/dot_general | solution.py:251
  19.0 2.9 %collective-permute-start = (f32[128,128]{1,0:T(8,128)S(1)}, f32[128,128]{1,0:T(8,128)S(1)}, u32[]{:S(2)}, u32[]{:S(2)}) collective-permute-start(f32[128,128]{1,0:T(8,128)S(1)} %fusion.3), channel_id=1, source_target_pairs={{0,1},{1,0},{2,3},{3,2},{4,5},{5,4},{6,7},{7,6},{8,9},{9,8},{10,11... | collective-permute-start | bytes 196616 | tf_op jit(solution)/shard_map/ppermute | solution.py:237
  21.9 0.9 collective-permute-done
  22.8 2.2 %collective-permute-start.1 = (f32[128,128]{1,0:T(8,128)S(1)}, f32[128,128]{1,0:T(8,128)S(1)}, u32[]{:S(2)}, u32[]{:S(2)}) collective-permute-start(f32[128,128]{1,0:T(8,128)S(1)} %add.29), channel_id=1, source_target_pairs={{0,16},{1,17},{2,18},{3,19},{4,20},{5,21},{6,22},{7,23},{8,24},{9,... | collective-permute-start | bytes 196616 | tf_op jit(solution)/shard_map/ppermute | solution.py:237
  25.0 3.1 %collective-permute-done.1 = f32[128,128]{1,0:T(8,128)S(1)} collective-permute-done((f32[128,128]{1,0:T(8,128)S(1)}, f32[128,128]{1,0:T(8,128)S(1)}, u32[]{:S(2)}, u32[]{:S(2)}) %collective-permute-start.1) | collective-permute-done | bytes 65568 | tf_op jit(solution)/shard_map/ppermute | solution.py:237
  28.1 3.2 %collective-permute-start.2 = (f32[128,128]{1,0:T(8,128)S(1)}, f32[128,128]{1,0:T(8,128)S(1)}, u32[]{:S(2)}, u32[]{:S(2)}) collective-permute-start(f32[128,128]{1,0:T(8,128)S(1)} %add.30), channel_id=1, source_target_pairs={{0,2},{1,3},{2,0},{3,1},{4,6},{5,7},{6,4},{7,5},{8,10},{9,11},{10,... | collective-permute-start | bytes 196616 | tf_op jit(solution)/shard_map/ppermute | solution.py:237
  31.3 2.1 %collective-permute-done.2 = f32[128,128]{1,0:T(8,128)S(1)} collective-permute-done((f32[128,128]{1,0:T(8,128)S(1)}, f32[128,128]{1,0:T(8,128)S(1)}, u32[]{:S(2)}, u32[]{:S(2)}) %collective-permute-start.2) | collective-permute-done | bytes 65568 | tf_op jit(solution)/shard_map/ppermute | solution.py:237
  33.5 4.2 %collective-permute-start.3 = (f32[128,128]{1,0:T(8,128)S(1)}, f32[128,128]{1,0:T(8,128)S(1)}, u32[]{:S(2)}, u32[]{:S(2)}) collective-permute-start(f32[128,128]{1,0:T(8,128)S(1)} %add.31), channel_id=1, source_target_pairs={{0,4},{1,5},{2,6},{3,7},{4,0},{5,1},{6,2},{7,3},{8,12},{9,13},{10,... | collective-permute-start | bytes 196616 | tf_op jit(solution)/shard_map/ppermute | solution.py:237
  37.7 0.0 copy-done
  37.7 0.1 dynamic-slice.2
  37.8 1.9 %collective-permute-done.3 = f32[128,128]{1,0:T(8,128)S(1)} collective-permute-done((f32[128,128]{1,0:T(8,128)S(1)}, f32[128,128]{1,0:T(8,128)S(1)}, u32[]{:S(2)}, u32[]{:S(2)}) %collective-permute-start.3) | collective-permute-done | bytes 65568 | tf_op jit(solution)/shard_map/ppermute | solution.py:237
  39.7 8.2 %collective-permute-start.4 = (f32[128,128]{1,0:T(8,128)S(1)}, f32[128,128]{1,0:T(8,128)S(1)}, u32[]{:S(2)}, u32[]{:S(2)}) collective-permute-start(f32[128,128]{1,0:T(8,128)S(1)} %add.32), channel_id=1, source_target_pairs={{0,8},{1,9},{2,10},{3,11},{4,12},{5,13},{6,14},{7,15},{8,0},{9,1},... | collective-permute-start | bytes 196616 | tf_op jit(solution)/shard_map/ppermute | solution.py:237
  47.8 0.0 copy-done.1
  47.8 0.6 fusion.2
  49.7 0.1 collective-permute-done.4
  49.8 0.1 fusion.strip_ref
  49.8 16.0 %all-to-all-done.pieces_ref = bf16[16,128,512]{2,1,0:T(8,128)(2,1)S(1)} async-done(((bf16[16,128,512]{2,1,0:T(8,128)(2,1)}), bf16[16,128,512]{2,1,0:T(8,128)(2,1)S(1)}, u32[]{:S(2)}, u32[]{:S(2)}) %all-to-all-start) | async-done | bytes 2097184 | tf_op jit(solution)/shard_map/all_to_all | solution.py:249
  65.8 0.7 shard_map.39
  66.6 5.2 %collective-permute-start.5 = (f32[16,16,8,128]{3,2,1,0:T(8,128)S(1)}, f32[16,16,8,128]{3,2,1,0:T(8,128)}, u32[]{:S(2)}, u32[]{:S(2)}) collective-permute-start(f32[16,16,8,128]{3,2,1,0:T(8,128)S(1)} %shard_map.39), channel_id=1, source_target_pairs={{0,1},{1,0},{2,3},{3,2},{4,5},{5,4},{6,7},{7,6},{8,9},{9,8},{10,11... | collective-permute-start | bytes 3145736 | tf_op jit(solution)/shard_map/ppermute | solution.py:237
  73.0 0.7 shard_map.38.mine_ref
  73.7 0.4 collective-permute-done.5.theirs_ref
  74.1 2.2 %shard_map.40 = f32[16,17,8,128]{3,2,1,0:T(8,128)} custom-call(s32[1]{0:T(128)} %bitcast.4.core_ref, f32[16,16,8,128]{3,2,1,0:T(8,128)S(1)} %shard_map.38.mine_ref, f32[16,16,8,128]{3,2,1,0:T(8,128)} %collective-permute-done.5.theirs_ref, f32[8,128]{1,0:T(8,128)S(1)} %fusion.strip_ref), custom_call_target="tpu_custom_call" | custom-call | flops 1048576 | bytes 4194304 | tf_op jit(solution)/shard_map/pallas_call | solution.py:168
  76.3 3.7 %all-to-all-start.1 = ((f32[16,17,8,128]{3,2,1,0:T(8,128)}), f32[16,17,8,128]{3,2,1,0:T(8,128)S(1)}, u32[]{:S(2)}, u32[]{:S(2)}) async-start(f32[16,17,8,128]{3,2,1,0:T(8,128)} %shard_map.40), calls=%async_computation.1 | async-start | bytes 2228224 | tf_op jit(solution)/shard_map/all_to_all | solution.py:263
  83.8 16.4 %all-to-all-done.1 = f32[16,17,8,128]{3,2,1,0:T(8,128)S(1)} async-done(((f32[16,17,8,128]{3,2,1,0:T(8,128)}), f32[16,17,8,128]{3,2,1,0:T(8,128)S(1)}, u32[]{:S(2)}, u32[]{:S(2)}) %all-to-all-start.1) | async-done | bytes 1114144 | tf_op jit(solution)/shard_map/all_to_all | solution.py:263
  100.2 0.1 slice_reduce_fusion
  100.3 14.9 %all_to_all.20 = f32[16,3,8,128]{3,2,1,0:T(8,128)S(1)} all-to-all(f32[16,3,8,128]{3,2,1,0:T(8,128)S(1)} %pad_maximum_fusion), channel_id=1, replica_groups={{0,32,64,96,128,160,192,224,256,288,320,352,384,416,448,480},{2,34,66,9..., dimensions={0} | all-to-all | bytes 393216 | tf_op jit(solution)/shard_map/all_to_all | solution.py:273
  115.2 0.7 broadcast_in_dim.19
  115.9 3.6 %all-to-all-start.3 = ((f32[16,2,8,128]{3,2,1,0:T(8,128)}), f32[16,2,8,128]{3,2,1,0:T(8,128)S(1)}, u32[]{:S(2)}, u32[]{:S(2)}) async-start(f32[16,2,8,128]{3,2,1,0:T(8,128)} %broadcast_in_dim.19), calls=%async_computation.3 | async-start | bytes 262144 | tf_op jit(solution)/shard_map/all_to_all | solution.py:278
  119.5 3.8 %shard_map.41.pair_ref = f32[2,128,128]{2,1,0:T(8,128)S(1)} custom-call(f32[16,2,8,128]{3,2,1,0:T(8,128)S(1)} %get-tuple-element.15.blocks_ref), custom_call_target="tpu_custom_call" | custom-call | flops 20971520 | bytes 1048576 | tf_op jit(solution)/shard_map/pallas_call | solution.py:190
  123.4 6.5 %collective-permute-start.6 = (f32[2,128,128]{2,1,0:T(8,128)S(1)}, f32[2,128,128]{2,1,0:T(8,128)S(1)}, u32[]{:S(2)}, u32[]{:S(2)}) collective-permute-start(f32[2,128,128]{2,1,0:T(8,128)S(1)} %shard_map.41.pair_ref), channel_id=1, source_target_pairs={{0,1},{1,0},{2,3},{3,2},{4,5},{5,4},{6,7},{7,6},{8,9},{9,8},{10,11... | collective-permute-start | bytes 393224 | tf_op jit(solution)/shard_map/ppermute | solution.py:237
  129.8 1.0 collective-permute-done.6.their_pair_ref
  130.8 0.0 all-to-all-done.3.mine_ref
  130.8 3.7 %collective-permute-start.7 = (f32[16,2,8,128]{3,2,1,0:T(8,128)S(1)}, f32[16,2,8,128]{3,2,1,0:T(8,128)S(1)}, u32[]{:S(2)}, u32[]{:S(2)}) collective-permute-start(f32[16,2,8,128]{3,2,1,0:T(8,128)S(1)} %all-to-all-done.3.mine_ref), channel_id=1, source_target_pairs={{0,1},{1,0},{2,3},{3,2},{4,5},{5,4},{6,7},{7,6},{8,9},{9,8},{10,11... | collective-permute-start | bytes 393224 | tf_op jit(solution)/shard_map/ppermute | solution.py:237
  135.8 0.1 pad_add_fusion.flags_ref
  135.9 0.0 collective-permute-done.7.theirs_ref
  135.9 5.9 %shard_map.42 = f32[128,256]{1,0:T(8,128)} custom-call(s32[3]{0:T(128)S(1)} %pad_add_fusion.flags_ref, f32[16,2,8,128]{3,2,1,0:T(8,128)S(1)} %all-to-all-done.3.mine_ref, f32[16,2,8,128]{3,2,1,0:T(8,128)S(1)} %collective-permute-done.7.theirs_ref, f32[1,128]{1,0:T(1,128)S(1)} %bitcast.17, f32[2,128,128]{2,1,0:T(8,128)S(1)} %shard_map.41.pair_ref, ...), custom_call_target="tpu_custom_call" | custom-call | flops 67108864 | bytes 1048576 | tf_op jit(solution)/shard_map/pallas_call | solution.py:226
  (11 shorter events, 0.1 us)
Async XLA Ops:
  2.6 63.2 %all-to-all-start = ((bf16[16,128,512]{2,1,0:T(8,128)(2,1)}), bf16[16,128,512]{2,1,0:T(8,128)(2,1)S(1)}, u32[]{:S(2)}, u32[]{:S(2)}) async-start(bf16[16,128,512]{2,1,0:T(8,128)(2,1)} %shard_map.37), calls=%async_computation | async-start | bytes 4194304 | tf_op jit(solution)/shard_map/all_to_all | solution.py:249
  16.1 21.6 %copy-start = (f32[128]{0:T(128)S(1)}, f32[128]{0:T(128)}, u32[]{:S(2)}) copy-start(f32[128]{0:T(128)} %param.4) | copy-start | bytes 1540
  16.1 31.7 %copy-start.1 = (s32[16]{0:T(128)S(1)}, s32[16]{0:T(128)}, u32[]{:S(2)}) copy-start(s32[16]{0:T(128)} %param.5) | copy-start | bytes 196
  19.0 3.8 %collective-permute-start = (f32[128,128]{1,0:T(8,128)S(1)}, f32[128,128]{1,0:T(8,128)S(1)}, u32[]{:S(2)}, u32[]{:S(2)}) collective-permute-start(f32[128,128]{1,0:T(8,128)S(1)} %fusion.3), channel_id=1, source_target_pairs={{0,1},{1,0},{2,3},{3,2},{4,5},{5,4},{6,7},{7,6},{8,9},{9,8},{10,11... | collective-permute-start | bytes 196616 | tf_op jit(solution)/shard_map/ppermute | solution.py:237
  22.8 5.3 %collective-permute-start.1 = (f32[128,128]{1,0:T(8,128)S(1)}, f32[128,128]{1,0:T(8,128)S(1)}, u32[]{:S(2)}, u32[]{:S(2)}) collective-permute-start(f32[128,128]{1,0:T(8,128)S(1)} %add.29), channel_id=1, source_target_pairs={{0,16},{1,17},{2,18},{3,19},{4,20},{5,21},{6,22},{7,23},{8,24},{9,... | collective-permute-start | bytes 196616 | tf_op jit(solution)/shard_map/ppermute | solution.py:237
  28.1 5.3 %collective-permute-start.2 = (f32[128,128]{1,0:T(8,128)S(1)}, f32[128,128]{1,0:T(8,128)S(1)}, u32[]{:S(2)}, u32[]{:S(2)}) collective-permute-start(f32[128,128]{1,0:T(8,128)S(1)} %add.30), channel_id=1, source_target_pairs={{0,2},{1,3},{2,0},{3,1},{4,6},{5,7},{6,4},{7,5},{8,10},{9,11},{10,... | collective-permute-start | bytes 196616 | tf_op jit(solution)/shard_map/ppermute | solution.py:237
  33.5 6.2 %collective-permute-start.3 = (f32[128,128]{1,0:T(8,128)S(1)}, f32[128,128]{1,0:T(8,128)S(1)}, u32[]{:S(2)}, u32[]{:S(2)}) collective-permute-start(f32[128,128]{1,0:T(8,128)S(1)} %add.31), channel_id=1, source_target_pairs={{0,4},{1,5},{2,6},{3,7},{4,0},{5,1},{6,2},{7,3},{8,12},{9,13},{10,... | collective-permute-start | bytes 196616 | tf_op jit(solution)/shard_map/ppermute | solution.py:237
  39.7 10.1 %collective-permute-start.4 = (f32[128,128]{1,0:T(8,128)S(1)}, f32[128,128]{1,0:T(8,128)S(1)}, u32[]{:S(2)}, u32[]{:S(2)}) collective-permute-start(f32[128,128]{1,0:T(8,128)S(1)} %add.32), channel_id=1, source_target_pairs={{0,8},{1,9},{2,10},{3,11},{4,12},{5,13},{6,14},{7,15},{8,0},{9,1},... | collective-permute-start | bytes 196616 | tf_op jit(solution)/shard_map/ppermute | solution.py:237
  66.6 7.6 %collective-permute-start.5 = (f32[16,16,8,128]{3,2,1,0:T(8,128)S(1)}, f32[16,16,8,128]{3,2,1,0:T(8,128)}, u32[]{:S(2)}, u32[]{:S(2)}) collective-permute-start(f32[16,16,8,128]{3,2,1,0:T(8,128)S(1)} %shard_map.39), channel_id=1, source_target_pairs={{0,1},{1,0},{2,3},{3,2},{4,5},{5,4},{6,7},{7,6},{8,9},{9,8},{10,11... | collective-permute-start | bytes 3145736 | tf_op jit(solution)/shard_map/ppermute | solution.py:237
  76.3 23.8 %all-to-all-start.1 = ((f32[16,17,8,128]{3,2,1,0:T(8,128)}), f32[16,17,8,128]{3,2,1,0:T(8,128)S(1)}, u32[]{:S(2)}, u32[]{:S(2)}) async-start(f32[16,17,8,128]{3,2,1,0:T(8,128)} %shard_map.40), calls=%async_computation.1 | async-start | bytes 2228224 | tf_op jit(solution)/shard_map/all_to_all | solution.py:263
  115.9 14.9 %all-to-all-start.3 = ((f32[16,2,8,128]{3,2,1,0:T(8,128)}), f32[16,2,8,128]{3,2,1,0:T(8,128)S(1)}, u32[]{:S(2)}, u32[]{:S(2)}) async-start(f32[16,2,8,128]{3,2,1,0:T(8,128)} %broadcast_in_dim.19), calls=%async_computation.3 | async-start | bytes 262144 | tf_op jit(solution)/shard_map/all_to_all | solution.py:278
  123.4 7.4 %collective-permute-start.6 = (f32[2,128,128]{2,1,0:T(8,128)S(1)}, f32[2,128,128]{2,1,0:T(8,128)S(1)}, u32[]{:S(2)}, u32[]{:S(2)}) collective-permute-start(f32[2,128,128]{2,1,0:T(8,128)S(1)} %shard_map.41.pair_ref), channel_id=1, source_target_pairs={{0,1},{1,0},{2,3},{3,2},{4,5},{5,4},{6,7},{7,6},{8,9},{9,8},{10,11... | collective-permute-start | bytes 393224 | tf_op jit(solution)/shard_map/ppermute | solution.py:237
  130.8 5.1 %collective-permute-start.7 = (f32[16,2,8,128]{3,2,1,0:T(8,128)S(1)}, f32[16,2,8,128]{3,2,1,0:T(8,128)S(1)}, u32[]{:S(2)}, u32[]{:S(2)}) collective-permute-start(f32[16,2,8,128]{3,2,1,0:T(8,128)S(1)} %all-to-all-done.3.mine_ref), channel_id=1, source_target_pairs={{0,1},{1,0},{2,3},{3,2},{4,5},{5,4},{6,7},{7,6},{8,9},{9,8},{10,11... | collective-permute-start | bytes 393224 | tf_op jit(solution)/shard_map/ppermute | solution.py:237

commit v8 on v7

--- a/solution.py
+++ b/solution.py
@@ -181,23 +181,28 @@
     )(core[None], mine, theirs, strip)
 
 
-def first_kernel(blocks_ref, pair_ref):
-    pair_ref[0] = inverse_factor(blocks_ref[:, 0].reshape(ROWS, ROWS))
-    pair_ref[1] = blocks_ref[:, 1].reshape(ROWS, ROWS)
-
-
-def first_factor(blocks):
+def first_kernel(core_ref, block_ref, inverse_ref):
+    @pl.when(core_ref[0] == 0)
+    def _():
+        inverse_ref[...] = jnp.zeros_like(inverse_ref)
+
+    @pl.when(core_ref[0] == 1)
+    def _():
+        inverse_ref[...] = inverse_factor(block_ref[...].reshape(ROWS, ROWS))
+
+
+def first_factor(core, block):
     return pl.pallas_call(
         first_kernel,
-        out_shape=jax.ShapeDtypeStruct((2, ROWS, ROWS), jnp.float32),
-        in_specs=[VMEM],
+        out_shape=jax.ShapeDtypeStruct((ROWS, ROWS), jnp.float32),
+        in_specs=[SMEM, VMEM],
         out_specs=VMEM,
         compiler_params=pltpu.CompilerParams(vmem_limit_bytes=16 << 20),
         cost_estimate=pl.CostEstimate(flops=20 << 20, bytes_accessed=1 << 20, transcendentals=0),
-    )(blocks)
-
-
-def last_kernel(flags_ref, mine_ref, theirs_ref, shift_ref, pair_ref, their_pair_ref, out_ref):
+    )(core[None], block)
+
+
+def last_kernel(flags_ref, mine_ref, theirs_ref, shift_ref, inverse_ref, their_inverse_ref, out_ref):
     row = lax.broadcasted_iota(jnp.int32, (ROWS, ROWS), 0)
     column = lax.broadcasted_iota(jnp.int32, (ROWS, ROWS), 1)
 
@@ -210,19 +215,16 @@
         add = (row == column) & (flags_ref[k] == 1)
         return item(k, 0) + jnp.where(add, shift_ref[...], 0.0)
 
-    def first(i):
-        return jnp.where(flags_ref[2] == 1, pair_ref[i], their_pair_ref[i])
-
-    inverse = first(0)
+    inverse = jnp.where(flags_ref[2] == 1, inverse_ref[...], their_inverse_ref[...])
     remote = exact(inverse, item(0, 1), ((1,), (0,)))
-    second = inverse_factor(first(1) - exact(remote, remote, ((0,), (0,))))
+    second = inverse_factor(item(1, 1) - exact(remote, remote, ((0,), (0,))))
     zero = exact(inverse, own(0), ((1,), (0,)))
     rest = own(1) - exact(remote, zero, ((0,), (0,)))
     out_ref[:, :ROWS] = zero.T
     out_ref[:, ROWS:] = exact(second, rest, ((1,), (0,))).T
 
 
-def last_factor(flags, mine, theirs, shift, pair, their_pair):
+def last_factor(flags, mine, theirs, shift, inverse, their_inverse):
     return pl.pallas_call(
         last_kernel,
         out_shape=jax.ShapeDtypeStruct((ROWS, 2 * ROWS), jnp.float32),
@@ -230,7 +232,7 @@
         out_specs=VMEM,
         compiler_params=pltpu.CompilerParams(vmem_limit_bytes=16 << 20),
         cost_estimate=pl.CostEstimate(flops=64 << 20, bytes_accessed=1 << 20, transcendentals=0),
-    )(flags, mine, theirs, shift, pair, their_pair)
+    )(flags, mine, theirs, shift, inverse, their_inverse)
 
 
 def flip(block, bit):
@@ -267,22 +269,23 @@
     def pick(array, k):
         return lax.dynamic_index_in_dim(array, panel_ids[k], 0, keepdims=False)
 
-    one = jnp.where(core == 0, pick(total, 1), pick(strips, 0))
-    two = pick(strips, 1)
-    total = jnp.stack([total, jnp.broadcast_to(one, total.shape), jnp.broadcast_to(two, total.shape)], 1)
+    second = jnp.where(core == 0, pick(total, 1), pick(strips, 0))
+    diagonal = pick(strips, 1)
+    total = jnp.stack([total, jnp.broadcast_to(second, total.shape)], 1)
     total = lax.all_to_all(total, axes, 0, 0, axis_index_groups=SAMP_THEN_CHIPS, tiled=True)
-    blocks = total[:, 1:]
-    total = total[:, :2].sum(0)
+    block = total[:, 1]
+    total = total.sum(0)
+    total = jnp.stack([total[0], jnp.where(core == 0, total[1], diagonal)])
 
     copies = jnp.broadcast_to(total[None], (CHIPS,) + total.shape)
     gathered = lax.all_to_all(copies, "par", 0, 0, axis_index_groups=CHIPS_BY_CORE, tiled=True)
-    pair = first_factor(blocks)
-    their_pair = flip(pair, 1)
-    gathered, pair, their_pair = lax.optimization_barrier((gathered, pair, their_pair))
+    inverse = first_factor(core, block)
+    their_inverse = flip(inverse, 1)
+    gathered, inverse, their_inverse = lax.optimization_barrier((gathered, inverse, their_inverse))
     flags = jnp.stack([
         (panel_ids[0] == here).astype(jnp.int32), (panel_ids[1] == here).astype(jnp.int32), core
     ])
-    return last_factor(flags, gathered, flip(gathered, 1), shift[None, :], pair, their_pair)
+    return last_factor(flags, gathered, flip(gathered, 1), shift[None, :], inverse, their_inverse)
 
 
 def solution(mesh):

time: 143 us -> 142 us (level)
  transfers between devices with their start and end apart: 11 -> 11, of which waited for: 9 -> 10; matrix products, arithmetic and copies ran while one was open for 3% -> 3% of each run, Pallas kernels for 3% -> 3%
where the time goes in v8:
time: 142 us; the launch traced here: 141 us
  starting transfers between devices  55.9 us (39%)
  waiting for transfers between devices  42.1 us (30%)
  Pallas kernels  16 us (11%)
  blocking collectives  14.8 us (10%)
  between operations  7.74 us (5%)
  matrix products  2.93 us (2%)
    ppermute x8, starting transfers between devices, flip(): return lax.ppermute(block, 'par', [(i, i ^ bit) for i in range(PAR)])  35.2 us
    all_to_all x1, waiting for transfers between devices, per_device(): lax.all_to_all(total, axes, 0, 0, axis_index_groups=CHIPS_THEN_SAMP, tile...  16.4 us
    all_to_all x1, waiting for transfers between devices, per_device(): pieces = lax.all_to_all(cut(samples), 'samp', 0, 0, tiled=True)  16 us
    all_to_all x1, blocking collectives, per_device(): lax.all_to_all(total, axes, 0, 0, axis_index_groups=SAMP_THEN_CHIPS, tile...  14.8 us
    all_to_all x1, starting transfers between devices, per_device(): pieces = lax.all_to_all(cut(samples), 'samp', 0, 0, tiled=True)  13.4 us
    ppermute x8, waiting for transfers between devices, flip(): return lax.ppermute(block, 'par', [(i, i ^ bit) for i in range(PAR)])  9.4 us
    pallas_call x1, Pallas kernels, last_factor(): pl.pallas_call(last_kernel, out_shape=jax.ShapeDtypeStruct((ROWS, 2 * ROW...  5.92 us
    pallas_call x1, Pallas kernels, first_factor(): pl.pallas_call(first_kernel, out_shape=jax.ShapeDtypeStruct((ROWS, ROWS),...  3.86 us
  transfers between devices with their start and end apart: 11, of which 10 were waited for; matrix products, arithmetic and copies ran while one was open for 3% of the time, Pallas kernels for 3%

profile of v8, /device:TPU:1, one launch (start us, length us, event | category | flops | bytes accessed | tf_op | source)
XLA Modules:
  0.0 141.2 jit_solution(12919770466105542053)
XLA Ops:
  0.0 2.6 %shard_map.37 = bf16[16,128,512]{2,1,0:T(8,128)(2,1)} custom-call(bf16[128,8192]{1,0:T(8,128)(2,1)} %samples_ref.1), custom_call_target="tpu_custom_call" | custom-call | bytes 4194304 | tf_op jit(solution)/shard_map/pallas_call | solution.py:92
  2.6 13.4 %all-to-all-start = ((bf16[16,128,512]{2,1,0:T(8,128)(2,1)}), bf16[16,128,512]{2,1,0:T(8,128)(2,1)S(1)}, u32[]{:S(2)}, u32[]{:S(2)}) async-start(bf16[16,128,512]{2,1,0:T(8,128)(2,1)} %shard_map.37), calls=%async_computation | async-start | bytes 4194304 | tf_op jit(solution)/shard_map/all_to_all | solution.py:251
  16.1 0.0 copy-start
  16.1 0.0 copy-start.1
  16.1 2.9 %fusion.3 = f32[128,128]{1,0:T(8,128)S(1)} fusion(bf16[128,8192]{1,0:T(8,128)(2,1)} %samples_ref.1), kind=kOutput, calls=%fused_computation.12 | convolution fusion | flops 268435456 | bytes 2162688 | tf_op jit(solution)/shard_map/dot_general | solution.py:253
  19.0 2.9 %collective-permute-start = (f32[128,128]{1,0:T(8,128)S(1)}, f32[128,128]{1,0:T(8,128)S(1)}, u32[]{:S(2)}, u32[]{:S(2)}) collective-permute-start(f32[128,128]{1,0:T(8,128)S(1)} %fusion.3), channel_id=1, source_target_pairs={{0,1},{1,0},{2,3},{3,2},{4,5},{5,4},{6,7},{7,6},{8,9},{9,8},{10,11... | collective-permute-start | bytes 196616 | tf_op jit(solution)/shard_map/ppermute | solution.py:239
  21.9 0.9 collective-permute-done
  22.8 2.2 %collective-permute-start.1 = (f32[128,128]{1,0:T(8,128)S(1)}, f32[128,128]{1,0:T(8,128)S(1)}, u32[]{:S(2)}, u32[]{:S(2)}) collective-permute-start(f32[128,128]{1,0:T(8,128)S(1)} %add.29), channel_id=1, source_target_pairs={{0,16},{1,17},{2,18},{3,19},{4,20},{5,21},{6,22},{7,23},{8,24},{9,... | collective-permute-start | bytes 196616 | tf_op jit(solution)/shard_map/ppermute | solution.py:239
  25.0 3.1 %collective-permute-done.1 = f32[128,128]{1,0:T(8,128)S(1)} collective-permute-done((f32[128,128]{1,0:T(8,128)S(1)}, f32[128,128]{1,0:T(8,128)S(1)}, u32[]{:S(2)}, u32[]{:S(2)}) %collective-permute-start.1) | collective-permute-done | bytes 65568 | tf_op jit(solution)/shard_map/ppermute | solution.py:239
  28.1 3.2 %collective-permute-start.2 = (f32[128,128]{1,0:T(8,128)S(1)}, f32[128,128]{1,0:T(8,128)S(1)}, u32[]{:S(2)}, u32[]{:S(2)}) collective-permute-start(f32[128,128]{1,0:T(8,128)S(1)} %add.30), channel_id=1, source_target_pairs={{0,2},{1,3},{2,0},{3,1},{4,6},{5,7},{6,4},{7,5},{8,10},{9,11},{10,... | collective-permute-start | bytes 196616 | tf_op jit(solution)/shard_map/ppermute | solution.py:239
  31.3 2.1 %collective-permute-done.2 = f32[128,128]{1,0:T(8,128)S(1)} collective-permute-done((f32[128,128]{1,0:T(8,128)S(1)}, f32[128,128]{1,0:T(8,128)S(1)}, u32[]{:S(2)}, u32[]{:S(2)}) %collective-permute-start.2) | collective-permute-done | bytes 65568 | tf_op jit(solution)/shard_map/ppermute | solution.py:239
  33.5 4.2 %collective-permute-start.3 = (f32[128,128]{1,0:T(8,128)S(1)}, f32[128,128]{1,0:T(8,128)S(1)}, u32[]{:S(2)}, u32[]{:S(2)}) collective-permute-start(f32[128,128]{1,0:T(8,128)S(1)} %add.31), channel_id=1, source_target_pairs={{0,4},{1,5},{2,6},{3,7},{4,0},{5,1},{6,2},{7,3},{8,12},{9,13},{10,... | collective-permute-start | bytes 196616 | tf_op jit(solution)/shard_map/ppermute | solution.py:239
  37.7 0.0 copy-done
  37.7 0.1 dynamic-slice.2
  37.8 1.9 %collective-permute-done.3 = f32[128,128]{1,0:T(8,128)S(1)} collective-permute-done((f32[128,128]{1,0:T(8,128)S(1)}, f32[128,128]{1,0:T(8,128)S(1)}, u32[]{:S(2)}, u32[]{:S(2)}) %collective-permute-start.3) | collective-permute-done | bytes 65568 | tf_op jit(solution)/shard_map/ppermute | solution.py:239
  39.7 8.2 %collective-permute-start.4 = (f32[128,128]{1,0:T(8,128)S(1)}, f32[128,128]{1,0:T(8,128)S(1)}, u32[]{:S(2)}, u32[]{:S(2)}) collective-permute-start(f32[128,128]{1,0:T(8,128)S(1)} %add.32), channel_id=1, source_target_pairs={{0,8},{1,9},{2,10},{3,11},{4,12},{5,13},{6,14},{7,15},{8,0},{9,1},... | collective-permute-start | bytes 196616 | tf_op jit(solution)/shard_map/ppermute | solution.py:239
  47.8 0.0 copy-done.1
  47.8 0.6 fusion.2
  49.7 0.1 collective-permute-done.4
  49.8 0.1 fusion.strip_ref
  49.8 16.0 %all-to-all-done.pieces_ref = bf16[16,128,512]{2,1,0:T(8,128)(2,1)S(1)} async-done(((bf16[16,128,512]{2,1,0:T(8,128)(2,1)}), bf16[16,128,512]{2,1,0:T(8,128)(2,1)S(1)}, u32[]{:S(2)}, u32[]{:S(2)}) %all-to-all-start) | async-done | bytes 2097184 | tf_op jit(solution)/shard_map/all_to_all | solution.py:251
  65.8 0.7 shard_map.39
  66.6 5.2 %collective-permute-start.5 = (f32[16,16,8,128]{3,2,1,0:T(8,128)S(1)}, f32[16,16,8,128]{3,2,1,0:T(8,128)}, u32[]{:S(2)}, u32[]{:S(2)}) collective-permute-start(f32[16,16,8,128]{3,2,1,0:T(8,128)S(1)} %shard_map.39), channel_id=1, source_target_pairs={{0,1},{1,0},{2,3},{3,2},{4,5},{5,4},{6,7},{7,6},{8,9},{9,8},{10,11... | collective-permute-start | bytes 3145736 | tf_op jit(solution)/shard_map/ppermute | solution.py:239
  73.0 0.7 shard_map.38.mine_ref
  73.7 0.4 collective-permute-done.5.theirs_ref
  74.1 2.2 %shard_map.40 = f32[16,17,8,128]{3,2,1,0:T(8,128)} custom-call(s32[1]{0:T(128)} %bitcast.4.core_ref, f32[16,16,8,128]{3,2,1,0:T(8,128)S(1)} %shard_map.38.mine_ref, f32[16,16,8,128]{3,2,1,0:T(8,128)} %collective-permute-done.5.theirs_ref, f32[8,128]{1,0:T(8,128)S(1)} %fusion.strip_ref), custom_call_target="tpu_custom_call" | custom-call | flops 1048576 | bytes 4194304 | tf_op jit(solution)/shard_map/pallas_call | solution.py:168
  76.3 3.7 %all-to-all-start.1 = ((f32[16,17,8,128]{3,2,1,0:T(8,128)}), f32[16,17,8,128]{3,2,1,0:T(8,128)S(1)}, u32[]{:S(2)}, u32[]{:S(2)}) async-start(f32[16,17,8,128]{3,2,1,0:T(8,128)} %shard_map.40), calls=%async_computation.1 | async-start | bytes 2228224 | tf_op jit(solution)/shard_map/all_to_all | solution.py:265
  83.8 16.4 %all-to-all-done.1 = f32[16,17,8,128]{3,2,1,0:T(8,128)S(1)} async-done(((f32[16,17,8,128]{3,2,1,0:T(8,128)}), f32[16,17,8,128]{3,2,1,0:T(8,128)S(1)}, u32[]{:S(2)}, u32[]{:S(2)}) %all-to-all-start.1) | async-done | bytes 1114144 | tf_op jit(solution)/shard_map/all_to_all | solution.py:265
  100.2 0.1 slice_reduce_fusion
  100.3 14.8 %all_to_all.20 = f32[16,2,8,128]{3,2,1,0:T(8,128)S(1)} all-to-all(f32[16,2,8,128]{3,2,1,0:T(8,128)S(1)} %pad_maximum_fusion), channel_id=1, replica_groups={{0,32,64,96,128,160,192,224,256,288,320,352,384,416,448,480},{2,34,66,9..., dimensions={0} | all-to-all | bytes 262144 | tf_op jit(solution)/shard_map/all_to_all | solution.py:275
  115.2 0.7 broadcast_in_dim.20
  115.8 3.5 %all-to-all-start.3 = ((f32[16,2,8,128]{3,2,1,0:T(8,128)}), f32[16,2,8,128]{3,2,1,0:T(8,128)S(1)}, u32[]{:S(2)}, u32[]{:S(2)}) async-start(f32[16,2,8,128]{3,2,1,0:T(8,128)} %broadcast_in_dim.20), calls=%async_computation.3 | async-start | bytes 262144 | tf_op jit(solution)/shard_map/all_to_all | solution.py:281
  119.4 3.9 %shard_map.41.inverse_ref = f32[128,128]{1,0:T(8,128)S(1)} custom-call(s32[1]{0:T(128)} %bitcast.4.core_ref, f32[16,8,128]{2,1,0:T(8,128)S(1)} %slice_bitcast_fusion.block_ref), custom_call_target="tpu_custom_call" | custom-call | flops 20971520 | bytes 1048576 | tf_op jit(solution)/shard_map/pallas_call | solution.py:195
  123.2 2.2 %collective-permute-start.6 = (f32[128,128]{1,0:T(8,128)S(1)}, f32[128,128]{1,0:T(8,128)S(1)}, u32[]{:S(2)}, u32[]{:S(2)}) collective-permute-start(f32[128,128]{1,0:T(8,128)S(1)} %shard_map.41.inverse_ref), channel_id=1, source_target_pairs={{0,1},{1,0},{2,3},{3,2},{4,5},{5,4},{6,7},{7,6},{8,9},{9,8},{10,11... | collective-permute-start | bytes 196616 | tf_op jit(solution)/shard_map/ppermute | solution.py:239
  125.4 0.9 collective-permute-done.6.their_inverse_ref
  126.4 0.3 all-to-all-done.3.mine_ref
  126.7 7.2 %collective-permute-start.7 = (f32[16,2,8,128]{3,2,1,0:T(8,128)S(1)}, f32[16,2,8,128]{3,2,1,0:T(8,128)S(1)}, u32[]{:S(2)}, u32[]{:S(2)}) collective-permute-start(f32[16,2,8,128]{3,2,1,0:T(8,128)S(1)} %all-to-all-done.3.mine_ref), channel_id=1, source_target_pairs={{0,1},{1,0},{2,3},{3,2},{4,5},{5,4},{6,7},{7,6},{8,9},{9,8},{10,11... | collective-permute-start | bytes 393224 | tf_op jit(solution)/shard_map/ppermute | solution.py:239
  135.2 0.1 pad_add_fusion.flags_ref
  135.3 0.0 collective-permute-done.7.theirs_ref
  135.3 5.9 %shard_map.42 = f32[128,256]{1,0:T(8,128)} custom-call(s32[3]{0:T(128)S(1)} %pad_add_fusion.flags_ref, f32[16,2,8,128]{3,2,1,0:T(8,128)S(1)} %all-to-all-done.3.mine_ref, f32[16,2,8,128]{3,2,1,0:T(8,128)S(1)} %collective-permute-done.7.theirs_ref, f32[1,128]{1,0:T(1,128)S(1)} %bitcast.21, f32[128,128]{1,0:T(8,128)S(1)} %shard_map.41.inverse_ref, ...), custom_call_target="tpu_custom_call" | custom-call | flops 67108864 | bytes 1048576 | tf_op jit(solution)/shard_map/pallas_call | solution.py:228
  (12 shorter events, 0.1 us)
Async XLA Ops:
  2.6 63.2 %all-to-all-start = ((bf16[16,128,512]{2,1,0:T(8,128)(2,1)}), bf16[16,128,512]{2,1,0:T(8,128)(2,1)S(1)}, u32[]{:S(2)}, u32[]{:S(2)}) async-start(bf16[16,128,512]{2,1,0:T(8,128)(2,1)} %shard_map.37), calls=%async_computation | async-start | bytes 4194304 | tf_op jit(solution)/shard_map/all_to_all | solution.py:251
  16.1 21.6 %copy-start = (f32[128]{0:T(128)S(1)}, f32[128]{0:T(128)}, u32[]{:S(2)}) copy-start(f32[128]{0:T(128)} %param.4) | copy-start | bytes 1540
  16.1 31.7 %copy-start.1 = (s32[16]{0:T(128)S(1)}, s32[16]{0:T(128)}, u32[]{:S(2)}) copy-start(s32[16]{0:T(128)} %param.5) | copy-start | bytes 196
  19.0 3.8 %collective-permute-start = (f32[128,128]{1,0:T(8,128)S(1)}, f32[128,128]{1,0:T(8,128)S(1)}, u32[]{:S(2)}, u32[]{:S(2)}) collective-permute-start(f32[128,128]{1,0:T(8,128)S(1)} %fusion.3), channel_id=1, source_target_pairs={{0,1},{1,0},{2,3},{3,2},{4,5},{5,4},{6,7},{7,6},{8,9},{9,8},{10,11... | collective-permute-start | bytes 196616 | tf_op jit(solution)/shard_map/ppermute | solution.py:239
  22.8 5.3 %collective-permute-start.1 = (f32[128,128]{1,0:T(8,128)S(1)}, f32[128,128]{1,0:T(8,128)S(1)}, u32[]{:S(2)}, u32[]{:S(2)}) collective-permute-start(f32[128,128]{1,0:T(8,128)S(1)} %add.29), channel_id=1, source_target_pairs={{0,16},{1,17},{2,18},{3,19},{4,20},{5,21},{6,22},{7,23},{8,24},{9,... | collective-permute-start | bytes 196616 | tf_op jit(solution)/shard_map/ppermute | solution.py:239
  28.1 5.3 %collective-permute-start.2 = (f32[128,128]{1,0:T(8,128)S(1)}, f32[128,128]{1,0:T(8,128)S(1)}, u32[]{:S(2)}, u32[]{:S(2)}) collective-permute-start(f32[128,128]{1,0:T(8,128)S(1)} %add.30), channel_id=1, source_target_pairs={{0,2},{1,3},{2,0},{3,1},{4,6},{5,7},{6,4},{7,5},{8,10},{9,11},{10,... | collective-permute-start | bytes 196616 | tf_op jit(solution)/shard_map/ppermute | solution.py:239
  33.5 6.2 %collective-permute-start.3 = (f32[128,128]{1,0:T(8,128)S(1)}, f32[128,128]{1,0:T(8,128)S(1)}, u32[]{:S(2)}, u32[]{:S(2)}) collective-permute-start(f32[128,128]{1,0:T(8,128)S(1)} %add.31), channel_id=1, source_target_pairs={{0,4},{1,5},{2,6},{3,7},{4,0},{5,1},{6,2},{7,3},{8,12},{9,13},{10,... | collective-permute-start | bytes 196616 | tf_op jit(solution)/shard_map/ppermute | solution.py:239
  39.7 10.1 %collective-permute-start.4 = (f32[128,128]{1,0:T(8,128)S(1)}, f32[128,128]{1,0:T(8,128)S(1)}, u32[]{:S(2)}, u32[]{:S(2)}) collective-permute-start(f32[128,128]{1,0:T(8,128)S(1)} %add.32), channel_id=1, source_target_pairs={{0,8},{1,9},{2,10},{3,11},{4,12},{5,13},{6,14},{7,15},{8,0},{9,1},... | collective-permute-start | bytes 196616 | tf_op jit(solution)/shard_map/ppermute | solution.py:239
  66.6 7.6 %collective-permute-start.5 = (f32[16,16,8,128]{3,2,1,0:T(8,128)S(1)}, f32[16,16,8,128]{3,2,1,0:T(8,128)}, u32[]{:S(2)}, u32[]{:S(2)}) collective-permute-start(f32[16,16,8,128]{3,2,1,0:T(8,128)S(1)} %shard_map.39), channel_id=1, source_target_pairs={{0,1},{1,0},{2,3},{3,2},{4,5},{5,4},{6,7},{7,6},{8,9},{9,8},{10,11... | collective-permute-start | bytes 3145736 | tf_op jit(solution)/shard_map/ppermute | solution.py:239
  76.3 23.8 %all-to-all-start.1 = ((f32[16,17,8,128]{3,2,1,0:T(8,128)}), f32[16,17,8,128]{3,2,1,0:T(8,128)S(1)}, u32[]{:S(2)}, u32[]{:S(2)}) async-start(f32[16,17,8,128]{3,2,1,0:T(8,128)} %shard_map.40), calls=%async_computation.1 | async-start | bytes 2228224 | tf_op jit(solution)/shard_map/all_to_all | solution.py:265
  115.8 10.9 %all-to-all-start.3 = ((f32[16,2,8,128]{3,2,1,0:T(8,128)}), f32[16,2,8,128]{3,2,1,0:T(8,128)S(1)}, u32[]{:S(2)}, u32[]{:S(2)}) async-start(f32[16,2,8,128]{3,2,1,0:T(8,128)} %broadcast_in_dim.20), calls=%async_computation.3 | async-start | bytes 262144 | tf_op jit(solution)/shard_map/all_to_all | solution.py:281
  123.2 3.1 %collective-permute-start.6 = (f32[128,128]{1,0:T(8,128)S(1)}, f32[128,128]{1,0:T(8,128)S(1)}, u32[]{:S(2)}, u32[]{:S(2)}) collective-permute-start(f32[128,128]{1,0:T(8,128)S(1)} %shard_map.41.inverse_ref), channel_id=1, source_target_pairs={{0,1},{1,0},{2,3},{3,2},{4,5},{5,4},{6,7},{7,6},{8,9},{9,8},{10,11... | collective-permute-start | bytes 196616 | tf_op jit(solution)/shard_map/ppermute | solution.py:239
  126.7 8.6 %collective-permute-start.7 = (f32[16,2,8,128]{3,2,1,0:T(8,128)S(1)}, f32[16,2,8,128]{3,2,1,0:T(8,128)S(1)}, u32[]{:S(2)}, u32[]{:S(2)}) collective-permute-start(f32[16,2,8,128]{3,2,1,0:T(8,128)S(1)} %all-to-all-done.3.mine_ref), channel_id=1, source_target_pairs={{0,1},{1,0},{2,3},{3,2},{4,5},{5,4},{6,7},{7,6},{8,9},{9,8},{10,11... | collective-permute-start | bytes 393224 | tf_op jit(solution)/shard_map/ppermute | solution.py:239

commit v9 on v8

--- a/solution.py
+++ b/solution.py
@@ -15,8 +15,8 @@
 
 OVER_CHIPS = [[[s * PAR + 2 * x + c for x in range(CHIPS)] for s in range(SAMP)] for c in range(2)]
 OVER_SAMP = [[[s * PAR + 2 * x + c for s in range(SAMP)] for x in range(CHIPS)] for c in range(2)]
-CHIPS_THEN_SAMP = OVER_CHIPS[0] + OVER_SAMP[1]
-SAMP_THEN_CHIPS = OVER_SAMP[0] + OVER_CHIPS[1]
+CHIPS_THEN_SAMP = OVER_CHIPS[1] + OVER_SAMP[0]
+SAMP_THEN_CHIPS = OVER_SAMP[1] + OVER_CHIPS[0]
 CHIPS_BY_CORE = [[2 * x + c for x in range(CHIPS)] for c in range(2)]
 
 
@@ -39,29 +39,44 @@
             [jnp.broadcast_to(rows[r][:, base + c:base + c + 1], (1, ROWS)) if c >= r else None for c in range(TILE)]
             for r in range(TILE)
         ]
+        inside = (lane >= base) & (lane < base + TILE)
+        near = at + 1 < TILES
+        if near:
+            after = jnp.where(inside, 0.0, tiles[at + 1])
+            columns = [
+                jnp.broadcast_to(tiles[at + 1][:, base + k:base + k + 1], (TILE, ROWS)) for k in range(TILE)
+            ]
         inverse = [None] * TILE
         for k in range(TILE):
             inverse[k] = 1.0 / pivot[k][k]
             scaled = jnp.where(lanes == base + k, 1.0, rows[k])
+            factors = [None] * TILE
             for i in range(k + 1, TILE):
-                factor = pivot[k][i] * inverse[k]
+                factors[i] = pivot[k][i] * inverse[k]
                 for c in range(i, TILE):
-                    pivot[i][c] = pivot[i][c] - factor * pivot[k][c]
-                rows[i] = jnp.where(lanes == base + k, 0.0, rows[i]) - factor * scaled
-        solved = [None] * TILE
-        for k in reversed(range(TILE)):
-            value = jnp.where(lanes == base + k, 1.0, rows[k])
-            value = jnp.where((lanes > base + k) & (lanes < base + TILE), 0.0, value)
-            for c in range(TILE - 1, k, -1):
-                value = value - pivot[k][c] * solved[c]
-            solved[k] = value * inverse[k]
-        wide = [jnp.broadcast_to(row, (TILE, ROWS)) for row in solved]
-        inside = (lane >= base) & (lane < base + TILE)
-        for t in range(at + 1, TILES):
+                    pivot[i][c] = pivot[i][c] - factors[i] * pivot[k][c]
+                rows[i] = jnp.where(lanes == base + k, 0.0, rows[i]) - factors[i] * scaled
+            if near:
+                lower = jnp.where((lanes > base + k) & (lanes < base + TILE), 0.0, scaled) * inverse[k]
+                after = after - columns[k] * lower
+                for i in range(k + 1, TILE):
+                    columns[i] = columns[i] - factors[i] * columns[k]
+        if at + 2 < TILES:
+            solved = [None] * TILE
+            for k in reversed(range(TILE)):
+                value = jnp.where(lanes == base + k, 1.0, rows[k])
+                value = jnp.where((lanes > base + k) & (lanes < base + TILE), 0.0, value)
+                for c in range(TILE - 1, k, -1):
+                    value = value - pivot[k][c] * solved[c]
+                solved[k] = value * inverse[k]
+            wide = [jnp.broadcast_to(row, (TILE, ROWS)) for row in solved]
+        for t in range(at + 2, TILES):
             value = jnp.where(inside, 0.0, tiles[t])
             for k in reversed(range(TILE)):
                 value = value - tiles[t][:, base + k:base + k + 1] * wide[k]
             tiles[t] = value
+        if near:
+            tiles[at + 1] = after
         done = None
         for r in range(TILE):
             row = jnp.where(lanes < base + r, rows[r], jnp.where(lanes == base + r, 1.0, 0.0))
@@ -129,7 +144,7 @@
 PART = 4
 
 
-def join_kernel(core_ref, mine_ref, theirs_ref, strip_ref, out_ref, theirs_held, held, arrived, left):
+def join_kernel(role_ref, mine_ref, theirs_ref, strip_ref, out_ref, theirs_held, held, arrived, left):
     def arrival(part):
         tiles = pl.ds(part * PART, PART)
         return pltpu.make_async_copy(theirs_ref.at[tiles], theirs_held.at[tiles], arrived.at[part])
@@ -142,7 +157,7 @@
         return pltpu.make_async_copy(held.at[TILES], out_ref.at[:, SAMP], left.at[TILES])
 
     def on_core(core, tiles, act):
-        @pl.when(core_ref[0] == core)
+        @pl.when(role_ref[0] == core)
         def _():
             for tile in tiles:
                 act(departure(tile, core))
@@ -163,7 +178,7 @@
     strips().wait()
 
 
-def join(core, mine, theirs, strip):
+def join(role, mine, theirs, strip):
     anywhere = pl.BlockSpec(memory_space=pl.ANY)
     return pl.pallas_call(
         join_kernel,
@@ -178,20 +193,20 @@
         ],
         compiler_params=pltpu.CompilerParams(vmem_limit_bytes=16 << 20),
         cost_estimate=pl.CostEstimate(flops=1 << 20, bytes_accessed=4 << 20, transcendentals=0),
-    )(core[None], mine, theirs, strip)
-
-
-def first_kernel(core_ref, block_ref, inverse_ref):
-    @pl.when(core_ref[0] == 0)
+    )(role[None], mine, theirs, strip)
+
+
+def first_kernel(role_ref, block_ref, inverse_ref):
+    @pl.when(role_ref[0] == 0)
     def _():
         inverse_ref[...] = jnp.zeros_like(inverse_ref)
 
-    @pl.when(core_ref[0] == 1)
+    @pl.when(role_ref[0] == 1)
     def _():
         inverse_ref[...] = inverse_factor(block_ref[...].reshape(ROWS, ROWS))
 
 
-def first_factor(core, block):
+def first_factor(role, block):
     return pl.pallas_call(
         first_kernel,
         out_shape=jax.ShapeDtypeStruct((ROWS, ROWS), jnp.float32),
@@ -199,7 +214,7 @@
         out_specs=VMEM,
         compiler_params=pltpu.CompilerParams(vmem_limit_bytes=16 << 20),
         cost_estimate=pl.CostEstimate(flops=20 << 20, bytes_accessed=1 << 20, transcendentals=0),
-    )(core[None], block)
+    )(role[None], block)
 
 
 def last_kernel(flags_ref, mine_ref, theirs_ref, shift_ref, inverse_ref, their_inverse_ref, out_ref):
@@ -242,10 +257,10 @@
 def per_device(samples, shift, panel_ids):
     here = lax.axis_index("samp")
     place = lax.axis_index("par")
-    core = lax.rem(place, 2)
+    role = 1 - lax.rem(place, 2)
     chip = lax.div(place, 2)
-    mine = jnp.where(core == 0, panel_ids[0], panel_ids[1])
-    theirs = jnp.where(core == 0, panel_ids[1], panel_ids[0])
+    mine = jnp.where(role == 0, panel_ids[0], panel_ids[1])
+    theirs = jnp.where(role == 0, panel_ids[1], panel_ids[0])
     axes = ("samp", "par")
 
     pieces = lax.all_to_all(cut(samples), "samp", 0, 0, tiled=True)
@@ -260,7 +275,7 @@
     pieces, strip = lax.optimization_barrier((pieces, strip))
 
     sent = flip(partial_gram(theirs, pieces), 1)
-    total = join(core, partial_gram(mine, pieces), sent, strip)
+    total = join(role, partial_gram(mine, pieces), sent, strip)
 
     total = lax.all_to_all(total, axes, 0, 0, axis_index_groups=CHIPS_THEN_SAMP, tiled=True)
     strips = total[:, SAMP]
@@ -269,21 +284,21 @@
     def pick(array, k):
         return lax.dynamic_index_in_dim(array, panel_ids[k], 0, keepdims=False)
 
-    second = jnp.where(core == 0, pick(total, 1), pick(strips, 0))
+    second = jnp.where(role == 0, pick(total, 1), pick(strips, 0))
     diagonal = pick(strips, 1)
     total = jnp.stack([total, jnp.broadcast_to(second, total.shape)], 1)
     total = lax.all_to_all(total, axes, 0, 0, axis_index_groups=SAMP_THEN_CHIPS, tiled=True)
     block = total[:, 1]
     total = total.sum(0)
-    total = jnp.stack([total[0], jnp.where(core == 0, total[1], diagonal)])
+    total = jnp.stack([total[0], jnp.where(role == 0, total[1], diagonal)])
 
     copies = jnp.broadcast_to(total[None], (CHIPS,) + total.shape)
     gathered = lax.all_to_all(copies, "par", 0, 0, axis_index_groups=CHIPS_BY_CORE, tiled=True)
-    inverse = first_factor(core, block)
+    inverse = first_factor(role, block)
     their_inverse = flip(inverse, 1)
     gathered, inverse, their_inverse = lax.optimization_barrier((gathered, inverse, their_inverse))
     flags = jnp.stack([
-        (panel_ids[0] == here).astype(jnp.int32), (panel_ids[1] == here).astype(jnp.int32), core
+        (panel_ids[0] == here).astype(jnp.int32), (panel_ids[1] == here).astype(jnp.int32), role
     ])
     return last_factor(flags, gathered, flip(gathered, 1), shift[None, :], inverse, their_inverse)
 

time: 142 us -> 139 us (0.979)
  starting transfers between devices: 55.9 us -> 61 us
  Pallas kernels: 16 us -> 11.4 us
  waiting for transfers between devices: 42.1 us -> 38.6 us
    pallas_call x1, Pallas kernels: 3.86 us -> 0.02 us  [first_factor(): pl.pallas_call(first_kernel, out_shape=jax.ShapeDtypeStruct((ROWS, ROWS),...]
    all_to_all x1, waiting for transfers between devices: 16.4 us -> 12.9 us  [per_device(): lax.all_to_all(total, axes, 0, 0, axis_index_groups=CHIPS_THEN_SAMP, tile...]
    all_to_all x1, starting transfers between devices: 3.71 us -> 6.97 us  [per_device(): lax.all_to_all(total, axes, 0, 0, axis_index_groups=CHIPS_THEN_SAMP, tile...]
  transfers between devices with their start and end apart: 11 -> 11, of which waited for: 10 -> 10; matrix products, arithmetic and copies ran while one was open for 3% -> 3% of each run, Pallas kernels for 3% -> 1%
where the time goes in v9:
time: 139 us; the launch traced here: 138 us
  starting transfers between devices  61 us (44%)
  waiting for transfers between devices  38.6 us (28%)
  blocking collectives  14.8 us (11%)
  Pallas kernels  11.4 us (8%)
  between operations  7.74 us (6%)
  matrix products  2.93 us (2%)
    ppermute x8, starting transfers between devices, flip(): return lax.ppermute(block, 'par', [(i, i ^ bit) for i in range(PAR)])  36.3 us
    all_to_all x1, waiting for transfers between devices, per_device(): pieces = lax.all_to_all(cut(samples), 'samp', 0, 0, tiled=True)  16 us
    all_to_all x1, blocking collectives, per_device(): lax.all_to_all(total, axes, 0, 0, axis_index_groups=SAMP_THEN_CHIPS, tile...  14.8 us
    all_to_all x1, starting transfers between devices, per_device(): pieces = lax.all_to_all(cut(samples), 'samp', 0, 0, tiled=True)  13.4 us
    all_to_all x1, waiting for transfers between devices, per_device(): lax.all_to_all(total, axes, 0, 0, axis_index_groups=CHIPS_THEN_SAMP, tile...  12.9 us
    ppermute x8, waiting for transfers between devices, flip(): return lax.ppermute(block, 'par', [(i, i ^ bit) for i in range(PAR)])  9.35 us
    all_to_all x1, starting transfers between devices, per_device(): lax.all_to_all(total, axes, 0, 0, axis_index_groups=CHIPS_THEN_SAMP, tile...  6.97 us
    pallas_call x1, Pallas kernels, last_factor(): pl.pallas_call(last_kernel, out_shape=jax.ShapeDtypeStruct((ROWS, 2 * ROW...  5.23 us
  transfers between devices with their start and end apart: 11, of which 10 were waited for; matrix products, arithmetic and copies ran while one was open for 3% of the time, Pallas kernels for 1%

profile of v9, /device:TPU:1, one launch (start us, length us, event | category | flops | bytes accessed | tf_op | source)
XLA Modules:
  0.0 138.2 jit_solution(10080575479657432350)
XLA Ops:
  0.0 2.6 %shard_map.37 = bf16[16,128,512]{2,1,0:T(8,128)(2,1)} custom-call(bf16[128,8192]{1,0:T(8,128)(2,1)} %samples_ref.1), custom_call_target="tpu_custom_call" | custom-call | bytes 4194304 | tf_op jit(solution)/shard_map/pallas_call | solution.py:107
  2.6 13.4 %all-to-all-start = ((bf16[16,128,512]{2,1,0:T(8,128)(2,1)}), bf16[16,128,512]{2,1,0:T(8,128)(2,1)S(1)}, u32[]{:S(2)}, u32[]{:S(2)}) async-start(bf16[16,128,512]{2,1,0:T(8,128)(2,1)} %shard_map.37), calls=%async_computation | async-start | bytes 4194304 | tf_op jit(solution)/shard_map/all_to_all | solution.py:266
  16.1 0.0 copy-start
  16.1 0.0 copy-start.1
  16.1 2.9 %fusion.3 = f32[128,128]{1,0:T(8,128)S(1)} fusion(bf16[128,8192]{1,0:T(8,128)(2,1)} %samples_ref.1), kind=kOutput, calls=%fused_computation.12 | convolution fusion | flops 268435456 | bytes 2162688 | tf_op jit(solution)/shard_map/dot_general | solution.py:268
  19.0 2.9 %collective-permute-start = (f32[128,128]{1,0:T(8,128)S(1)}, f32[128,128]{1,0:T(8,128)S(1)}, u32[]{:S(2)}, u32[]{:S(2)}) collective-permute-start(f32[128,128]{1,0:T(8,128)S(1)} %fusion.3), channel_id=1, source_target_pairs={{0,1},{1,0},{2,3},{3,2},{4,5},{5,4},{6,7},{7,6},{8,9},{9,8},{10,11... | collective-permute-start | bytes 196616 | tf_op jit(solution)/shard_map/ppermute | solution.py:254
  21.9 0.9 collective-permute-done
  22.8 2.2 %collective-permute-start.1 = (f32[128,128]{1,0:T(8,128)S(1)}, f32[128,128]{1,0:T(8,128)S(1)}, u32[]{:S(2)}, u32[]{:S(2)}) collective-permute-start(f32[128,128]{1,0:T(8,128)S(1)} %add.29), channel_id=1, source_target_pairs={{0,16},{1,17},{2,18},{3,19},{4,20},{5,21},{6,22},{7,23},{8,24},{9,... | collective-permute-start | bytes 196616 | tf_op jit(solution)/shard_map/ppermute | solution.py:254
  25.0 3.1 %collective-permute-done.1 = f32[128,128]{1,0:T(8,128)S(1)} collective-permute-done((f32[128,128]{1,0:T(8,128)S(1)}, f32[128,128]{1,0:T(8,128)S(1)}, u32[]{:S(2)}, u32[]{:S(2)}) %collective-permute-start.1) | collective-permute-done | bytes 65568 | tf_op jit(solution)/shard_map/ppermute | solution.py:254
  28.1 3.2 %collective-permute-start.2 = (f32[128,128]{1,0:T(8,128)S(1)}, f32[128,128]{1,0:T(8,128)S(1)}, u32[]{:S(2)}, u32[]{:S(2)}) collective-permute-start(f32[128,128]{1,0:T(8,128)S(1)} %add.30), channel_id=1, source_target_pairs={{0,2},{1,3},{2,0},{3,1},{4,6},{5,7},{6,4},{7,5},{8,10},{9,11},{10,... | collective-permute-start | bytes 196616 | tf_op jit(solution)/shard_map/ppermute | solution.py:254
  31.3 2.1 %collective-permute-done.2 = f32[128,128]{1,0:T(8,128)S(1)} collective-permute-done((f32[128,128]{1,0:T(8,128)S(1)}, f32[128,128]{1,0:T(8,128)S(1)}, u32[]{:S(2)}, u32[]{:S(2)}) %collective-permute-start.2) | collective-permute-done | bytes 65568 | tf_op jit(solution)/shard_map/ppermute | solution.py:254
  33.5 4.2 %collective-permute-start.3 = (f32[128,128]{1,0:T(8,128)S(1)}, f32[128,128]{1,0:T(8,128)S(1)}, u32[]{:S(2)}, u32[]{:S(2)}) collective-permute-start(f32[128,128]{1,0:T(8,128)S(1)} %add.31), channel_id=1, source_target_pairs={{0,4},{1,5},{2,6},{3,7},{4,0},{5,1},{6,2},{7,3},{8,12},{9,13},{10,... | collective-permute-start | bytes 196616 | tf_op jit(solution)/shard_map/ppermute | solution.py:254
  37.7 0.0 copy-done
  37.7 0.1 dynamic-slice.2
  37.8 1.9 %collective-permute-done.3 = f32[128,128]{1,0:T(8,128)S(1)} collective-permute-done((f32[128,128]{1,0:T(8,128)S(1)}, f32[128,128]{1,0:T(8,128)S(1)}, u32[]{:S(2)}, u32[]{:S(2)}) %collective-permute-start.3) | collective-permute-done | bytes 65568 | tf_op jit(solution)/shard_map/ppermute | solution.py:254
  39.7 8.2 %collective-permute-start.4 = (f32[128,128]{1,0:T(8,128)S(1)}, f32[128,128]{1,0:T(8,128)S(1)}, u32[]{:S(2)}, u32[]{:S(2)}) collective-permute-start(f32[128,128]{1,0:T(8,128)S(1)} %add.32), channel_id=1, source_target_pairs={{0,8},{1,9},{2,10},{3,11},{4,12},{5,13},{6,14},{7,15},{8,0},{9,1},... | collective-permute-start | bytes 196616 | tf_op jit(solution)/shard_map/ppermute | solution.py:254
  47.8 0.0 copy-done.1
  47.8 0.6 fusion.2
  49.7 0.1 collective-permute-done.4
  49.8 0.1 fusion.strip_ref
  49.8 16.0 %all-to-all-done.pieces_ref = bf16[16,128,512]{2,1,0:T(8,128)(2,1)S(1)} async-done(((bf16[16,128,512]{2,1,0:T(8,128)(2,1)}), bf16[16,128,512]{2,1,0:T(8,128)(2,1)S(1)}, u32[]{:S(2)}, u32[]{:S(2)}) %all-to-all-start) | async-done | bytes 2097184 | tf_op jit(solution)/shard_map/all_to_all | solution.py:266
  65.8 0.7 shard_map.39
  66.6 5.2 %collective-permute-start.5 = (f32[16,16,8,128]{3,2,1,0:T(8,128)S(1)}, f32[16,16,8,128]{3,2,1,0:T(8,128)}, u32[]{:S(2)}, u32[]{:S(2)}) collective-permute-start(f32[16,16,8,128]{3,2,1,0:T(8,128)S(1)} %shard_map.39), channel_id=1, source_target_pairs={{0,1},{1,0},{2,3},{3,2},{4,5},{5,4},{6,7},{7,6},{8,9},{9,8},{10,11... | collective-permute-start | bytes 3145736 | tf_op jit(solution)/shard_map/ppermute | solution.py:254
  73.0 0.7 shard_map.38.mine_ref
  73.7 0.4 collective-permute-done.5.theirs_ref
  74.1 2.2 %shard_map.40 = f32[16,17,8,128]{3,2,1,0:T(8,128)} custom-call(s32[1]{0:T(128)} %bitcast.4.role_ref, f32[16,16,8,128]{3,2,1,0:T(8,128)S(1)} %shard_map.38.mine_ref, f32[16,16,8,128]{3,2,1,0:T(8,128)} %collective-permute-done.5.theirs_ref, f32[8,128]{1,0:T(8,128)S(1)} %fusion.strip_ref), custom_call_target="tpu_custom_call" | custom-call | flops 1048576 | bytes 4194304 | tf_op jit(solution)/shard_map/pallas_call | solution.py:183
  76.3 7.0 %all-to-all-start.1 = ((f32[16,17,8,128]{3,2,1,0:T(8,128)}), f32[16,17,8,128]{3,2,1,0:T(8,128)S(1)}, u32[]{:S(2)}, u32[]{:S(2)}) async-start(f32[16,17,8,128]{3,2,1,0:T(8,128)} %shard_map.40), calls=%async_computation.1 | async-start | bytes 2228224 | tf_op jit(solution)/shard_map/all_to_all | solution.py:280
  87.0 12.9 %all-to-all-done.1 = f32[16,17,8,128]{3,2,1,0:T(8,128)S(1)} async-done(((f32[16,17,8,128]{3,2,1,0:T(8,128)}), f32[16,17,8,128]{3,2,1,0:T(8,128)S(1)}, u32[]{:S(2)}, u32[]{:S(2)}) %all-to-all-start.1) | async-done | bytes 1114144 | tf_op jit(solution)/shard_map/all_to_all | solution.py:280
  100.0 0.1 slice_reduce_fusion
  100.1 14.8 %all_to_all.20 = f32[16,2,8,128]{3,2,1,0:T(8,128)S(1)} all-to-all(f32[16,2,8,128]{3,2,1,0:T(8,128)S(1)} %pad_maximum_fusion), channel_id=1, replica_groups={{1,33,65,97,129,161,193,225,257,289,321,353,385,417,449,481},{3,35,67,9..., dimensions={0} | all-to-all | bytes 262144 | tf_op jit(solution)/shard_map/all_to_all | solution.py:290
  114.9 0.7 broadcast_in_dim.20
  115.6 4.2 %all-to-all-start.3 = ((f32[16,2,8,128]{3,2,1,0:T(8,128)}), f32[16,2,8,128]{3,2,1,0:T(8,128)S(1)}, u32[]{:S(2)}, u32[]{:S(2)}) async-start(f32[16,2,8,128]{3,2,1,0:T(8,128)} %broadcast_in_dim.20), calls=%async_computation.3 | async-start | bytes 262144 | tf_op jit(solution)/shard_map/all_to_all | solution.py:296
  119.9 6.3 %collective-permute-start.6 = (f32[128,128]{1,0:T(8,128)S(1)}, f32[128,128]{1,0:T(8,128)S(1)}, u32[]{:S(2)}, u32[]{:S(2)}) collective-permute-start(f32[128,128]{1,0:T(8,128)S(1)} %shard_map.41.inverse_ref), channel_id=1, source_target_pairs={{0,1},{1,0},{2,3},{3,2},{4,5},{5,4},{6,7},{7,6},{8,9},{9,8},{10,11... | collective-permute-start | bytes 196616 | tf_op jit(solution)/shard_map/ppermute | solution.py:254
  126.2 0.9 collective-permute-done.6.their_inverse_ref
  127.0 0.3 all-to-all-done.3.mine_ref
  127.4 4.2 %collective-permute-start.7 = (f32[16,2,8,128]{3,2,1,0:T(8,128)S(1)}, f32[16,2,8,128]{3,2,1,0:T(8,128)S(1)}, u32[]{:S(2)}, u32[]{:S(2)}) collective-permute-start(f32[16,2,8,128]{3,2,1,0:T(8,128)S(1)} %all-to-all-done.3.mine_ref), channel_id=1, source_target_pairs={{0,1},{1,0},{2,3},{3,2},{4,5},{5,4},{6,7},{7,6},{8,9},{9,8},{10,11... | collective-permute-start | bytes 393224 | tf_op jit(solution)/shard_map/ppermute | solution.py:254
  132.8 0.1 pad_add_fusion.flags_ref
  132.9 0.0 collective-permute-done.7.theirs_ref
  132.9 5.2 %shard_map.42 = f32[128,256]{1,0:T(8,128)} custom-call(s32[3]{0:T(128)S(1)} %pad_add_fusion.flags_ref, f32[16,2,8,128]{3,2,1,0:T(8,128)S(1)} %all-to-all-done.3.mine_ref, f32[16,2,8,128]{3,2,1,0:T(8,128)S(1)} %collective-permute-done.7.theirs_ref, f32[1,128]{1,0:T(1,128)S(1)} %bitcast.21, f32[128,128]{1,0:T(8,128)S(1)} %shard_map.41.inverse_ref, ...), custom_call_target="tpu_custom_call" | custom-call | flops 67108864 | bytes 1048576 | tf_op jit(solution)/shard_map/pallas_call | solution.py:243
  (13 shorter events, 0.1 us)
Async XLA Ops:
  2.6 63.2 %all-to-all-start = ((bf16[16,128,512]{2,1,0:T(8,128)(2,1)}), bf16[16,128,512]{2,1,0:T(8,128)(2,1)S(1)}, u32[]{:S(2)}, u32[]{:S(2)}) async-start(bf16[16,128,512]{2,1,0:T(8,128)(2,1)} %shard_map.37), calls=%async_computation | async-start | bytes 4194304 | tf_op jit(solution)/shard_map/all_to_all | solution.py:266
  16.1 21.6 %copy-start = (f32[128]{0:T(128)S(1)}, f32[128]{0:T(128)}, u32[]{:S(2)}) copy-start(f32[128]{0:T(128)} %param.4) | copy-start | bytes 1540
  16.1 31.7 %copy-start.1 = (s32[16]{0:T(128)S(1)}, s32[16]{0:T(128)}, u32[]{:S(2)}) copy-start(s32[16]{0:T(128)} %param.5) | copy-start | bytes 196
  19.0 3.8 %collective-permute-start = (f32[128,128]{1,0:T(8,128)S(1)}, f32[128,128]{1,0:T(8,128)S(1)}, u32[]{:S(2)}, u32[]{:S(2)}) collective-permute-start(f32[128,128]{1,0:T(8,128)S(1)} %fusion.3), channel_id=1, source_target_pairs={{0,1},{1,0},{2,3},{3,2},{4,5},{5,4},{6,7},{7,6},{8,9},{9,8},{10,11... | collective-permute-start | bytes 196616 | tf_op jit(solution)/shard_map/ppermute | solution.py:254
  22.8 5.3 %collective-permute-start.1 = (f32[128,128]{1,0:T(8,128)S(1)}, f32[128,128]{1,0:T(8,128)S(1)}, u32[]{:S(2)}, u32[]{:S(2)}) collective-permute-start(f32[128,128]{1,0:T(8,128)S(1)} %add.29), channel_id=1, source_target_pairs={{0,16},{1,17},{2,18},{3,19},{4,20},{5,21},{6,22},{7,23},{8,24},{9,... | collective-permute-start | bytes 196616 | tf_op jit(solution)/shard_map/ppermute | solution.py:254
  28.1 5.3 %collective-permute-start.2 = (f32[128,128]{1,0:T(8,128)S(1)}, f32[128,128]{1,0:T(8,128)S(1)}, u32[]{:S(2)}, u32[]{:S(2)}) collective-permute-start(f32[128,128]{1,0:T(8,128)S(1)} %add.30), channel_id=1, source_target_pairs={{0,2},{1,3},{2,0},{3,1},{4,6},{5,7},{6,4},{7,5},{8,10},{9,11},{10,... | collective-permute-start | bytes 196616 | tf_op jit(solution)/shard_map/ppermute | solution.py:254
  33.5 6.2 %collective-permute-start.3 = (f32[128,128]{1,0:T(8,128)S(1)}, f32[128,128]{1,0:T(8,128)S(1)}, u32[]{:S(2)}, u32[]{:S(2)}) collective-permute-start(f32[128,128]{1,0:T(8,128)S(1)} %add.31), channel_id=1, source_target_pairs={{0,4},{1,5},{2,6},{3,7},{4,0},{5,1},{6,2},{7,3},{8,12},{9,13},{10,... | collective-permute-start | bytes 196616 | tf_op jit(solution)/shard_map/ppermute | solution.py:254
  39.7 10.1 %collective-permute-start.4 = (f32[128,128]{1,0:T(8,128)S(1)}, f32[128,128]{1,0:T(8,128)S(1)}, u32[]{:S(2)}, u32[]{:S(2)}) collective-permute-start(f32[128,128]{1,0:T(8,128)S(1)} %add.32), channel_id=1, source_target_pairs={{0,8},{1,9},{2,10},{3,11},{4,12},{5,13},{6,14},{7,15},{8,0},{9,1},... | collective-permute-start | bytes 196616 | tf_op jit(solution)/shard_map/ppermute | solution.py:254
  66.6 7.6 %collective-permute-start.5 = (f32[16,16,8,128]{3,2,1,0:T(8,128)S(1)}, f32[16,16,8,128]{3,2,1,0:T(8,128)}, u32[]{:S(2)}, u32[]{:S(2)}) collective-permute-start(f32[16,16,8,128]{3,2,1,0:T(8,128)S(1)} %shard_map.39), channel_id=1, source_target_pairs={{0,1},{1,0},{2,3},{3,2},{4,5},{5,4},{6,7},{7,6},{8,9},{9,8},{10,11... | collective-permute-start | bytes 3145736 | tf_op jit(solution)/shard_map/ppermute | solution.py:254
  76.3 23.6 %all-to-all-start.1 = ((f32[16,17,8,128]{3,2,1,0:T(8,128)}), f32[16,17,8,128]{3,2,1,0:T(8,128)S(1)}, u32[]{:S(2)}, u32[]{:S(2)}) async-start(f32[16,17,8,128]{3,2,1,0:T(8,128)} %shard_map.40), calls=%async_computation.1 | async-start | bytes 2228224 | tf_op jit(solution)/shard_map/all_to_all | solution.py:280
  115.6 11.8 %all-to-all-start.3 = ((f32[16,2,8,128]{3,2,1,0:T(8,128)}), f32[16,2,8,128]{3,2,1,0:T(8,128)S(1)}, u32[]{:S(2)}, u32[]{:S(2)}) async-start(f32[16,2,8,128]{3,2,1,0:T(8,128)} %broadcast_in_dim.20), calls=%async_computation.3 | async-start | bytes 262144 | tf_op jit(solution)/shard_map/all_to_all | solution.py:296
  119.9 7.2 %collective-permute-start.6 = (f32[128,128]{1,0:T(8,128)S(1)}, f32[128,128]{1,0:T(8,128)S(1)}, u32[]{:S(2)}, u32[]{:S(2)}) collective-permute-start(f32[128,128]{1,0:T(8,128)S(1)} %shard_map.41.inverse_ref), channel_id=1, source_target_pairs={{0,1},{1,0},{2,3},{3,2},{4,5},{5,4},{6,7},{7,6},{8,9},{9,8},{10,11... | collective-permute-start | bytes 196616 | tf_op jit(solution)/shard_map/ppermute | solution.py:254
  127.4 5.6 %collective-permute-start.7 = (f32[16,2,8,128]{3,2,1,0:T(8,128)S(1)}, f32[16,2,8,128]{3,2,1,0:T(8,128)S(1)}, u32[]{:S(2)}, u32[]{:S(2)}) collective-permute-start(f32[16,2,8,128]{3,2,1,0:T(8,128)S(1)} %all-to-all-done.3.mine_ref), channel_id=1, source_target_pairs={{0,1},{1,0},{2,3},{3,2},{4,5},{5,4},{6,7},{7,6},{8,9},{9,8},{10,11... | collective-permute-start | bytes 393224 | tf_op jit(solution)/shard_map/ppermute | solution.py:254

commit v10 on v9

--- a/solution.py
+++ b/solution.py
@@ -138,57 +138,42 @@
         out_specs=VMEM,
         compiler_params=pltpu.CompilerParams(vmem_limit_bytes=16 << 20),
         cost_estimate=pl.CostEstimate(flops=1 << 28, bytes_accessed=4 << 20, transcendentals=0),
-    )(panel[None], pieces)
-
-
-PART = 4
-
-
-def join_kernel(role_ref, mine_ref, theirs_ref, strip_ref, out_ref, theirs_held, held, arrived, left):
-    def arrival(part):
-        tiles = pl.ds(part * PART, PART)
-        return pltpu.make_async_copy(theirs_ref.at[tiles], theirs_held.at[tiles], arrived.at[part])
-
-    def departure(tile, core):
-        place = out_ref.at[tile, pl.ds(0, SAMP)] if core == 0 else out_ref.at[:, tile]
+    )(panel, pieces)
+
+
+def join_kernel(role_ref, mine_ref, theirs_ref, strip_ref, out_ref, held, left):
+    def departure(tile, role):
+        place = out_ref.at[tile, pl.ds(0, SAMP)] if role == 0 else out_ref.at[:, tile]
         return pltpu.make_async_copy(held.at[tile], place, left.at[tile])
 
     def strips():
         return pltpu.make_async_copy(held.at[TILES], out_ref.at[:, SAMP], left.at[TILES])
 
-    def on_core(core, tiles, act):
-        @pl.when(role_ref[0] == core)
+    def in_role(role, tiles, act):
+        @pl.when(role_ref[0] == role)
         def _():
             for tile in tiles:
-                act(departure(tile, core))
-
-    for part in range(TILES // PART):
-        arrival(part).start()
+                act(departure(tile, role))
+
     held[TILES] = jnp.broadcast_to(strip_ref[...][None], (SAMP, TILE, ROWS))
     strips().start()
-    for part in range(TILES // PART):
-        arrival(part).wait()
-        tiles = range(part * PART, part * PART + PART)
-        for tile in tiles:
-            held[tile] = mine_ref[tile] + theirs_held[tile]
-        for core in range(2):
-            on_core(core, tiles, lambda copy: copy.start())
-    for core in range(2):
-        on_core(core, range(TILES), lambda copy: copy.wait())
+    for tile in range(TILES):
+        held[tile] = mine_ref[tile] + theirs_ref[tile]
+        for role in range(2):
+            in_role(role, [tile], lambda copy: copy.start())
+    for role in range(2):
+        in_role(role, range(TILES), lambda copy: copy.wait())
     strips().wait()
 
 
 def join(role, mine, theirs, strip):
-    anywhere = pl.BlockSpec(memory_space=pl.ANY)
     return pl.pallas_call(
         join_kernel,
         out_shape=jax.ShapeDtypeStruct((TILES, SAMP + 1, TILE, ROWS), jnp.float32),
-        in_specs=[SMEM, VMEM, anywhere, VMEM],
-        out_specs=anywhere,
+        in_specs=[SMEM, VMEM, VMEM, VMEM],
+        out_specs=pl.BlockSpec(memory_space=pl.ANY),
         scratch_shapes=[
-            pltpu.VMEM((TILES, SAMP, TILE, ROWS), jnp.float32),
             pltpu.VMEM((TILES + 1, SAMP, TILE, ROWS), jnp.float32),
-            pltpu.SemaphoreType.DMA((TILES // PART,)),
             pltpu.SemaphoreType.DMA((TILES + 1,)),
         ],
         compiler_params=pltpu.CompilerParams(vmem_limit_bytes=16 << 20),
@@ -272,7 +257,10 @@
         square = square + flip(square, bit)
     square = square + jnp.eye(ROWS, dtype=jnp.float32) * shift[:, None]
     strip = lax.dynamic_slice_in_dim(square, chip * TILE, TILE, 0)
-    pieces, strip = lax.optimization_barrier((pieces, strip))
+    flags = jnp.stack([
+        (panel_ids[0] == here).astype(jnp.int32), (panel_ids[1] == here).astype(jnp.int32), role
+    ])
+    pieces, strip, flags, mine, theirs = lax.optimization_barrier((pieces, strip, flags, mine[None], theirs[None]))
 
     sent = flip(partial_gram(theirs, pieces), 1)
     total = join(role, partial_gram(mine, pieces), sent, strip)
@@ -297,9 +285,6 @@
     inverse = first_factor(role, block)
     their_inverse = flip(inverse, 1)
     gathered, inverse, their_inverse = lax.optimization_barrier((gathered, inverse, their_inverse))
-    flags = jnp.stack([
-        (panel_ids[0] == here).astype(jnp.int32), (panel_ids[1] == here).astype(jnp.int32), role
-    ])
     return last_factor(flags, gathered, flip(gathered, 1), shift[None, :], inverse, their_inverse)
 
 

time: 139 us -> 137 us (0.986)
  starting transfers between devices: 61 us -> 58.5 us
  waiting for transfers between devices: 38.6 us -> 40.4 us
    ppermute x8, waiting for transfers between devices: 9.35 us -> 12.9 us  [flip(): return lax.ppermute(block, 'par', [(i, i ^ bit) for i in range(PAR)])]
    ppermute x8, starting transfers between devices: 36.3 us -> 33.8 us  [flip(): return lax.ppermute(block, 'par', [(i, i ^ bit) for i in range(PAR)])]
    all_to_all x1, waiting for transfers between devices: 16 us -> 14.3 us  [per_device(): pieces = lax.all_to_all(cut(samples), 'samp', 0, 0, tiled=True)]
where the time goes in v10:
time: 137 us
  starting transfers between devices  58.5 us (43%)
  waiting for transfers between devices  40.4 us (29%)
  blocking collectives  14.8 us (11%)
  Pallas kernels  10.4 us (8%)
  between operations  7.95 us (6%)
  matrix products  2.93 us (2%)
  local copies, waits for them, and re-layouts  1.38 us (1%)
    ppermute x8, starting transfers between devices, flip(): return lax.ppermute(block, 'par', [(i, i ^ bit) for i in range(PAR)])  33.8 us
    all_to_all x1, blocking collectives, per_device(): lax.all_to_all(total, axes, 0, 0, axis_index_groups=SAMP_THEN_CHIPS, tile...  14.8 us
    all_to_all x1, waiting for transfers between devices, per_device(): pieces = lax.all_to_all(cut(samples), 'samp', 0, 0, tiled=True)  14.3 us
    all_to_all x1, starting transfers between devices, per_device(): pieces = lax.all_to_all(cut(samples), 'samp', 0, 0, tiled=True)  13.4 us
    ppermute x8, waiting for transfers between devices, flip(): return lax.ppermute(block, 'par', [(i, i ^ bit) for i in range(PAR)])  12.9 us
    all_to_all x1, waiting for transfers between devices, per_device(): lax.all_to_all(total, axes, 0, 0, axis_index_groups=CHIPS_THEN_SAMP, tile...  12.8 us
    all_to_all x1, starting transfers between devices, per_device(): lax.all_to_all(total, axes, 0, 0, axis_index_groups=CHIPS_THEN_SAMP, tile...  6.97 us
    pallas_call x1, Pallas kernels, last_factor(): pl.pallas_call(last_kernel, out_shape=jax.ShapeDtypeStruct((ROWS, 2 * ROW...  5.23 us
  transfers between devices with their start and end apart: 11, of which 10 were waited for; matrix products, arithmetic and copies ran while one was open for 3% of the time, Pallas kernels for 1%

profile of v10, /device:TPU:1, one launch (start us, length us, event | category | flops | bytes accessed | tf_op | source)
XLA Modules:
  0.0 136.6 jit_solution(16222835181581595758)
XLA Ops:
  0.0 2.6 %shard_map.37 = bf16[16,128,512]{2,1,0:T(8,128)(2,1)} custom-call(bf16[128,8192]{1,0:T(8,128)(2,1)} %samples_ref.1), custom_call_target="tpu_custom_call" | custom-call | bytes 4194304 | tf_op jit(solution)/shard_map/pallas_call | solution.py:107
  2.6 13.4 %all-to-all-start = ((bf16[16,128,512]{2,1,0:T(8,128)(2,1)}), bf16[16,128,512]{2,1,0:T(8,128)(2,1)S(1)}, u32[]{:S(2)}, u32[]{:S(2)}) async-start(bf16[16,128,512]{2,1,0:T(8,128)(2,1)} %shard_map.37), calls=%async_computation | async-start | bytes 4194304 | tf_op jit(solution)/shard_map/all_to_all | solution.py:251
  16.1 0.0 copy-start.1
  16.1 0.0 copy-start
  16.1 2.9 %fusion.3 = f32[128,128]{1,0:T(8,128)S(1)} fusion(bf16[128,8192]{1,0:T(8,128)(2,1)} %samples_ref.1), kind=kOutput, calls=%fused_computation.12 | convolution fusion | flops 268435456 | bytes 2162688 | tf_op jit(solution)/shard_map/dot_general | solution.py:253
  19.0 2.9 %collective-permute-start = (f32[128,128]{1,0:T(8,128)S(1)}, f32[128,128]{1,0:T(8,128)S(1)}, u32[]{:S(2)}, u32[]{:S(2)}) collective-permute-start(f32[128,128]{1,0:T(8,128)S(1)} %fusion.3), channel_id=1, source_target_pairs={{0,1},{1,0},{2,3},{3,2},{4,5},{5,4},{6,7},{7,6},{8,9},{9,8},{10,11... | collective-permute-start | bytes 196616 | tf_op jit(solution)/shard_map/ppermute | solution.py:239
  21.9 0.9 collective-permute-done
  22.8 2.2 %collective-permute-start.1 = (f32[128,128]{1,0:T(8,128)S(1)}, f32[128,128]{1,0:T(8,128)S(1)}, u32[]{:S(2)}, u32[]{:S(2)}) collective-permute-start(f32[128,128]{1,0:T(8,128)S(1)} %add.29), channel_id=1, source_target_pairs={{0,16},{1,17},{2,18},{3,19},{4,20},{5,21},{6,22},{7,23},{8,24},{9,... | collective-permute-start | bytes 196616 | tf_op jit(solution)/shard_map/ppermute | solution.py:239
  25.0 3.1 %collective-permute-done.1 = f32[128,128]{1,0:T(8,128)S(1)} collective-permute-done((f32[128,128]{1,0:T(8,128)S(1)}, f32[128,128]{1,0:T(8,128)S(1)}, u32[]{:S(2)}, u32[]{:S(2)}) %collective-permute-start.1) | collective-permute-done | bytes 65568 | tf_op jit(solution)/shard_map/ppermute | solution.py:239
  28.1 3.2 %collective-permute-start.2 = (f32[128,128]{1,0:T(8,128)S(1)}, f32[128,128]{1,0:T(8,128)S(1)}, u32[]{:S(2)}, u32[]{:S(2)}) collective-permute-start(f32[128,128]{1,0:T(8,128)S(1)} %add.30), channel_id=1, source_target_pairs={{0,2},{1,3},{2,0},{3,1},{4,6},{5,7},{6,4},{7,5},{8,10},{9,11},{10,... | collective-permute-start | bytes 196616 | tf_op jit(solution)/shard_map/ppermute | solution.py:239
  31.3 2.1 %collective-permute-done.2 = f32[128,128]{1,0:T(8,128)S(1)} collective-permute-done((f32[128,128]{1,0:T(8,128)S(1)}, f32[128,128]{1,0:T(8,128)S(1)}, u32[]{:S(2)}, u32[]{:S(2)}) %collective-permute-start.2) | collective-permute-done | bytes 65568 | tf_op jit(solution)/shard_map/ppermute | solution.py:239
  33.5 4.2 %collective-permute-start.3 = (f32[128,128]{1,0:T(8,128)S(1)}, f32[128,128]{1,0:T(8,128)S(1)}, u32[]{:S(2)}, u32[]{:S(2)}) collective-permute-start(f32[128,128]{1,0:T(8,128)S(1)} %add.31), channel_id=1, source_target_pairs={{0,4},{1,5},{2,6},{3,7},{4,0},{5,1},{6,2},{7,3},{8,12},{9,13},{10,... | collective-permute-start | bytes 196616 | tf_op jit(solution)/shard_map/ppermute | solution.py:239
  37.7 0.0 copy-done.1
  37.7 0.6 fusion.2
  42.1 0.0 copy-done
  42.2 0.1 dynamic-slice.2
  42.2 0.0 collective-permute-done.3
  42.3 5.7 %collective-permute-start.4 = (f32[128,128]{1,0:T(8,128)S(1)}, f32[128,128]{1,0:T(8,128)S(1)}, u32[]{:S(2)}, u32[]{:S(2)}) collective-permute-start(f32[128,128]{1,0:T(8,128)S(1)} %add.32), channel_id=1, source_target_pairs={{0,8},{1,9},{2,10},{3,11},{4,12},{5,13},{6,14},{7,15},{8,0},{9,1},... | collective-permute-start | bytes 196616 | tf_op jit(solution)/shard_map/ppermute | solution.py:239
  47.9 0.1 pad_add_fusion.flags_ref
  48.0 3.5 %collective-permute-done.4 = f32[128,128]{1,0:T(8,128)S(1)} collective-permute-done((f32[128,128]{1,0:T(8,128)S(1)}, f32[128,128]{1,0:T(8,128)S(1)}, u32[]{:S(2)}, u32[]{:S(2)}) %collective-permute-start.4) | collective-permute-done | bytes 65568 | tf_op jit(solution)/shard_map/ppermute | solution.py:239
  51.5 0.1 fusion.strip_ref
  51.5 14.3 %all-to-all-done.pieces_ref = bf16[16,128,512]{2,1,0:T(8,128)(2,1)S(1)} async-done(((bf16[16,128,512]{2,1,0:T(8,128)(2,1)}), bf16[16,128,512]{2,1,0:T(8,128)(2,1)S(1)}, u32[]{:S(2)}, u32[]{:S(2)}) %all-to-all-start) | async-done | bytes 2097184 | tf_op jit(solution)/shard_map/all_to_all | solution.py:251
  65.8 0.7 shard_map.39
  66.6 5.2 %collective-permute-start.5 = (f32[16,16,8,128]{3,2,1,0:T(8,128)S(1)}, f32[16,16,8,128]{3,2,1,0:T(8,128)S(1)}, u32[]{:S(2)}, u32[]{:S(2)}) collective-permute-start(f32[16,16,8,128]{3,2,1,0:T(8,128)S(1)} %shard_map.39), channel_id=1, source_target_pairs={{0,1},{1,0},{2,3},{3,2},{4,5},{5,4},{6,7},{7,6},{8,9},{9,8},{10,11... | collective-permute-start | bytes 3145736 | tf_op jit(solution)/shard_map/ppermute | solution.py:239
  71.7 0.7 shard_map.38.mine_ref
  72.4 1.6 %collective-permute-done.5.theirs_ref = f32[16,16,8,128]{3,2,1,0:T(8,128)S(1)} collective-permute-done((f32[16,16,8,128]{3,2,1,0:T(8,128)S(1)}, f32[16,16,8,128]{3,2,1,0:T(8,128)S(1)}, u32[]{:S(2)}, u32[]{:S(2)}) %collective-permute-start.5) | collective-permute-done | bytes 1048608 | tf_op jit(solution)/shard_map/ppermute | solution.py:239
  74.0 1.2 shard_map.40
  75.2 7.0 %all-to-all-start.1 = ((f32[16,17,8,128]{3,2,1,0:T(8,128)}), f32[16,17,8,128]{3,2,1,0:T(8,128)S(1)}, u32[]{:S(2)}, u32[]{:S(2)}) async-start(f32[16,17,8,128]{3,2,1,0:T(8,128)} %shard_map.40), calls=%async_computation.1 | async-start | bytes 2228224 | tf_op jit(solution)/shard_map/all_to_all | solution.py:268
  86.0 12.8 %all-to-all-done.1 = f32[16,17,8,128]{3,2,1,0:T(8,128)S(1)} async-done(((f32[16,17,8,128]{3,2,1,0:T(8,128)}), f32[16,17,8,128]{3,2,1,0:T(8,128)S(1)}, u32[]{:S(2)}, u32[]{:S(2)}) %all-to-all-start.1) | async-done | bytes 1114144 | tf_op jit(solution)/shard_map/all_to_all | solution.py:268
  98.8 0.1 slice_reduce_fusion
  98.9 14.8 %all_to_all.20 = f32[16,2,8,128]{3,2,1,0:T(8,128)S(1)} all-to-all(f32[16,2,8,128]{3,2,1,0:T(8,128)S(1)} %pad_maximum_fusion), channel_id=1, replica_groups={{1,33,65,97,129,161,193,225,257,289,321,353,385,417,449,481},{3,35,67,9..., dimensions={0} | all-to-all | bytes 262144 | tf_op jit(solution)/shard_map/all_to_all | solution.py:278
  113.8 0.7 broadcast_in_dim.20
  114.4 4.2 %all-to-all-start.3 = ((f32[16,2,8,128]{3,2,1,0:T(8,128)}), f32[16,2,8,128]{3,2,1,0:T(8,128)S(1)}, u32[]{:S(2)}, u32[]{:S(2)}) async-start(f32[16,2,8,128]{3,2,1,0:T(8,128)} %broadcast_in_dim.20), calls=%async_computation.3 | async-start | bytes 262144 | tf_op jit(solution)/shard_map/all_to_all | solution.py:284
  118.7 6.3 %collective-permute-start.6 = (f32[128,128]{1,0:T(8,128)S(1)}, f32[128,128]{1,0:T(8,128)S(1)}, u32[]{:S(2)}, u32[]{:S(2)}) collective-permute-start(f32[128,128]{1,0:T(8,128)S(1)} %shard_map.41.inverse_ref), channel_id=1, source_target_pairs={{0,1},{1,0},{2,3},{3,2},{4,5},{5,4},{6,7},{7,6},{8,9},{9,8},{10,11... | collective-permute-start | bytes 196616 | tf_op jit(solution)/shard_map/ppermute | solution.py:239
  125.0 0.9 collective-permute-done.6.their_inverse_ref
  125.9 0.3 all-to-all-done.3.mine_ref
  126.2 4.2 %collective-permute-start.7 = (f32[16,2,8,128]{3,2,1,0:T(8,128)S(1)}, f32[16,2,8,128]{3,2,1,0:T(8,128)S(1)}, u32[]{:S(2)}, u32[]{:S(2)}) collective-permute-start(f32[16,2,8,128]{3,2,1,0:T(8,128)S(1)} %all-to-all-done.3.mine_ref), channel_id=1, source_target_pairs={{0,1},{1,0},{2,3},{3,2},{4,5},{5,4},{6,7},{7,6},{8,9},{9,8},{10,11... | collective-permute-start | bytes 393224 | tf_op jit(solution)/shard_map/ppermute | solution.py:239
  130.4 1.0 collective-permute-done.7.theirs_ref
  131.4 5.2 %shard_map.42 = f32[128,256]{1,0:T(8,128)} custom-call(s32[3]{0:T(128)S(1)} %pad_add_fusion.flags_ref, f32[16,2,8,128]{3,2,1,0:T(8,128)S(1)} %all-to-all-done.3.mine_ref, f32[16,2,8,128]{3,2,1,0:T(8,128)S(1)} %collective-permute-done.7.theirs_ref, f32[1,128]{1,0:T(1,128)S(1)} %bitcast.21, f32[128,128]{1,0:T(8,128)S(1)} %shard_map.41.inverse_ref, ...), custom_call_target="tpu_custom_call" | custom-call | flops 67108864 | bytes 1048576 | tf_op jit(solution)/shard_map/pallas_call | solution.py:228
  (13 shorter events, 0.1 us)
Async XLA Ops:
  2.6 63.2 %all-to-all-start = ((bf16[16,128,512]{2,1,0:T(8,128)(2,1)}), bf16[16,128,512]{2,1,0:T(8,128)(2,1)S(1)}, u32[]{:S(2)}, u32[]{:S(2)}) async-start(bf16[16,128,512]{2,1,0:T(8,128)(2,1)} %shard_map.37), calls=%async_computation | async-start | bytes 4194304 | tf_op jit(solution)/shard_map/all_to_all | solution.py:251
  16.1 21.6 %copy-start.1 = (s32[16]{0:T(128)S(1)}, s32[16]{0:T(128)}, u32[]{:S(2)}) copy-start(s32[16]{0:T(128)} %param.5) | copy-start | bytes 196
  16.1 26.1 %copy-start = (f32[128]{0:T(128)S(1)}, f32[128]{0:T(128)}, u32[]{:S(2)}) copy-start(f32[128]{0:T(128)} %param.4) | copy-start | bytes 1540
  19.0 3.8 %collective-permute-start = (f32[128,128]{1,0:T(8,128)S(1)}, f32[128,128]{1,0:T(8,128)S(1)}, u32[]{:S(2)}, u32[]{:S(2)}) collective-permute-start(f32[128,128]{1,0:T(8,128)S(1)} %fusion.3), channel_id=1, source_target_pairs={{0,1},{1,0},{2,3},{3,2},{4,5},{5,4},{6,7},{7,6},{8,9},{9,8},{10,11... | collective-permute-start | bytes 196616 | tf_op jit(solution)/shard_map/ppermute | solution.py:239
  22.8 5.3 %collective-permute-start.1 = (f32[128,128]{1,0:T(8,128)S(1)}, f32[128,128]{1,0:T(8,128)S(1)}, u32[]{:S(2)}, u32[]{:S(2)}) collective-permute-start(f32[128,128]{1,0:T(8,128)S(1)} %add.29), channel_id=1, source_target_pairs={{0,16},{1,17},{2,18},{3,19},{4,20},{5,21},{6,22},{7,23},{8,24},{9,... | collective-permute-start | bytes 196616 | tf_op jit(solution)/shard_map/ppermute | solution.py:239
  28.1 5.3 %collective-permute-start.2 = (f32[128,128]{1,0:T(8,128)S(1)}, f32[128,128]{1,0:T(8,128)S(1)}, u32[]{:S(2)}, u32[]{:S(2)}) collective-permute-start(f32[128,128]{1,0:T(8,128)S(1)} %add.30), channel_id=1, source_target_pairs={{0,2},{1,3},{2,0},{3,1},{4,6},{5,7},{6,4},{7,5},{8,10},{9,11},{10,... | collective-permute-start | bytes 196616 | tf_op jit(solution)/shard_map/ppermute | solution.py:239
  33.5 8.8 %collective-permute-start.3 = (f32[128,128]{1,0:T(8,128)S(1)}, f32[128,128]{1,0:T(8,128)S(1)}, u32[]{:S(2)}, u32[]{:S(2)}) collective-permute-start(f32[128,128]{1,0:T(8,128)S(1)} %add.31), channel_id=1, source_target_pairs={{0,4},{1,5},{2,6},{3,7},{4,0},{5,1},{6,2},{7,3},{8,12},{9,13},{10,... | collective-permute-start | bytes 196616 | tf_op jit(solution)/shard_map/ppermute | solution.py:239
  42.3 9.2 %collective-permute-start.4 = (f32[128,128]{1,0:T(8,128)S(1)}, f32[128,128]{1,0:T(8,128)S(1)}, u32[]{:S(2)}, u32[]{:S(2)}) collective-permute-start(f32[128,128]{1,0:T(8,128)S(1)} %add.32), channel_id=1, source_target_pairs={{0,8},{1,9},{2,10},{3,11},{4,12},{5,13},{6,14},{7,15},{8,0},{9,1},... | collective-permute-start | bytes 196616 | tf_op jit(solution)/shard_map/ppermute | solution.py:239
  66.6 7.4 %collective-permute-start.5 = (f32[16,16,8,128]{3,2,1,0:T(8,128)S(1)}, f32[16,16,8,128]{3,2,1,0:T(8,128)S(1)}, u32[]{:S(2)}, u32[]{:S(2)}) collective-permute-start(f32[16,16,8,128]{3,2,1,0:T(8,128)S(1)} %shard_map.39), channel_id=1, source_target_pairs={{0,1},{1,0},{2,3},{3,2},{4,5},{5,4},{6,7},{7,6},{8,9},{9,8},{10,11... | collective-permute-start | bytes 3145736 | tf_op jit(solution)/shard_map/ppermute | solution.py:239
  75.2 23.6 %all-to-all-start.1 = ((f32[16,17,8,128]{3,2,1,0:T(8,128)}), f32[16,17,8,128]{3,2,1,0:T(8,128)S(1)}, u32[]{:S(2)}, u32[]{:S(2)}) async-start(f32[16,17,8,128]{3,2,1,0:T(8,128)} %shard_map.40), calls=%async_computation.1 | async-start | bytes 2228224 | tf_op jit(solution)/shard_map/all_to_all | solution.py:268
  114.4 11.8 %all-to-all-start.3 = ((f32[16,2,8,128]{3,2,1,0:T(8,128)}), f32[16,2,8,128]{3,2,1,0:T(8,128)S(1)}, u32[]{:S(2)}, u32[]{:S(2)}) async-start(f32[16,2,8,128]{3,2,1,0:T(8,128)} %broadcast_in_dim.20), calls=%async_computation.3 | async-start | bytes 262144 | tf_op jit(solution)/shard_map/all_to_all | solution.py:284
  118.7 7.2 %collective-permute-start.6 = (f32[128,128]{1,0:T(8,128)S(1)}, f32[128,128]{1,0:T(8,128)S(1)}, u32[]{:S(2)}, u32[]{:S(2)}) collective-permute-start(f32[128,128]{1,0:T(8,128)S(1)} %shard_map.41.inverse_ref), channel_id=1, source_target_pairs={{0,1},{1,0},{2,3},{3,2},{4,5},{5,4},{6,7},{7,6},{8,9},{9,8},{10,11... | collective-permute-start | bytes 196616 | tf_op jit(solution)/shard_map/ppermute | solution.py:239
  126.2 5.2 %collective-permute-start.7 = (f32[16,2,8,128]{3,2,1,0:T(8,128)S(1)}, f32[16,2,8,128]{3,2,1,0:T(8,128)S(1)}, u32[]{:S(2)}, u32[]{:S(2)}) collective-permute-start(f32[16,2,8,128]{3,2,1,0:T(8,128)S(1)} %all-to-all-done.3.mine_ref), channel_id=1, source_target_pairs={{0,1},{1,0},{2,3},{3,2},{4,5},{5,4},{6,7},{7,6},{8,9},{9,8},{10,11... | collective-permute-start | bytes 393224 | tf_op jit(solution)/shard_map/ppermute | solution.py:239

commit v11 on v10

--- a/solution.py
+++ b/solution.py
@@ -149,20 +149,19 @@
     def strips():
         return pltpu.make_async_copy(held.at[TILES], out_ref.at[:, SAMP], left.at[TILES])
 
-    def in_role(role, tiles, act):
+    def send(role):
         @pl.when(role_ref[0] == role)
         def _():
-            for tile in tiles:
-                act(departure(tile, role))
+            for tile in range(TILES):
+                held[tile] = mine_ref[tile] + theirs_ref[tile]
+                departure(tile, role).start()
+            for tile in range(TILES):
+                departure(tile, role).wait()
 
     held[TILES] = jnp.broadcast_to(strip_ref[...][None], (SAMP, TILE, ROWS))
     strips().start()
-    for tile in range(TILES):
-        held[tile] = mine_ref[tile] + theirs_ref[tile]
-        for role in range(2):
-            in_role(role, [tile], lambda copy: copy.start())
-    for role in range(2):
-        in_role(role, range(TILES), lambda copy: copy.wait())
+    send(0)
+    send(1)
     strips().wait()
 
 
@@ -217,10 +216,10 @@
 
     inverse = jnp.where(flags_ref[2] == 1, inverse_ref[...], their_inverse_ref[...])
     remote = exact(inverse, item(0, 1), ((1,), (0,)))
-    second = inverse_factor(item(1, 1) - exact(remote, remote, ((0,), (0,))))
     zero = exact(inverse, own(0), ((1,), (0,)))
     rest = own(1) - exact(remote, zero, ((0,), (0,)))
     out_ref[:, :ROWS] = zero.T
+    second = inverse_factor(item(1, 1) - exact(remote, remote, ((0,), (0,))))
     out_ref[:, ROWS:] = exact(second, rest, ((1,), (0,))).T
 
 

time: 137 us -> 137 us (level)
  no operation moved by 1% of the time
where the time goes in v11:
time: 137 us
  starting transfers between devices  58.5 us (43%)
  waiting for transfers between devices  40.4 us (29%)
  blocking collectives  14.8 us (11%)
  Pallas kernels  10.4 us (8%)
  between operations  7.95 us (6%)
  matrix products  2.93 us (2%)
  local copies, waits for them, and re-layouts  1.38 us (1%)
    ppermute x8, starting transfers between devices, flip(): return lax.ppermute(block, 'par', [(i, i ^ bit) for i in range(PAR)])  33.8 us
    all_to_all x1, blocking collectives, per_device(): lax.all_to_all(total, axes, 0, 0, axis_index_groups=SAMP_THEN_CHIPS, tile...  14.8 us
    all_to_all x1, waiting for transfers between devices, per_device(): pieces = lax.all_to_all(cut(samples), 'samp', 0, 0, tiled=True)  14.3 us
    all_to_all x1, starting transfers between devices, per_device(): pieces = lax.all_to_all(cut(samples), 'samp', 0, 0, tiled=True)  13.4 us
    ppermute x8, waiting for transfers between devices, flip(): return lax.ppermute(block, 'par', [(i, i ^ bit) for i in range(PAR)])  12.9 us
    all_to_all x1, waiting for transfers between devices, per_device(): lax.all_to_all(total, axes, 0, 0, axis_index_groups=CHIPS_THEN_SAMP, tile...  12.8 us
    all_to_all x1, starting transfers between devices, per_device(): lax.all_to_all(total, axes, 0, 0, axis_index_groups=CHIPS_THEN_SAMP, tile...  6.97 us
    pallas_call x1, Pallas kernels, last_factor(): pl.pallas_call(last_kernel, out_shape=jax.ShapeDtypeStruct((ROWS, 2 * ROW...  5.18 us
  transfers between devices with their start and end apart: 11, of which 10 were waited for; matrix products, arithmetic and copies ran while one was open for 3% of the time, Pallas kernels for 1%

profile of v11, /device:TPU:1, one launch (start us, length us, event | category | flops | bytes accessed | tf_op | source)
XLA Modules:
  0.0 136.6 jit_solution(14952595146555360383)
XLA Ops:
  0.0 2.6 %shard_map.37 = bf16[16,128,512]{2,1,0:T(8,128)(2,1)} custom-call(bf16[128,8192]{1,0:T(8,128)(2,1)} %samples_ref.1), custom_call_target="tpu_custom_call" | custom-call | bytes 4194304 | tf_op jit(solution)/shard_map/pallas_call | solution.py:107
  2.6 13.4 %all-to-all-start = ((bf16[16,128,512]{2,1,0:T(8,128)(2,1)}), bf16[16,128,512]{2,1,0:T(8,128)(2,1)S(1)}, u32[]{:S(2)}, u32[]{:S(2)}) async-start(bf16[16,128,512]{2,1,0:T(8,128)(2,1)} %shard_map.37), calls=%async_computation | async-start | bytes 4194304 | tf_op jit(solution)/shard_map/all_to_all | solution.py:250
  16.1 0.0 copy-start.1
  16.1 0.0 copy-start
  16.1 2.9 %fusion.3 = f32[128,128]{1,0:T(8,128)S(1)} fusion(bf16[128,8192]{1,0:T(8,128)(2,1)} %samples_ref.1), kind=kOutput, calls=%fused_computation.12 | convolution fusion | flops 268435456 | bytes 2162688 | tf_op jit(solution)/shard_map/dot_general | solution.py:252
  19.0 2.9 %collective-permute-start = (f32[128,128]{1,0:T(8,128)S(1)}, f32[128,128]{1,0:T(8,128)S(1)}, u32[]{:S(2)}, u32[]{:S(2)}) collective-permute-start(f32[128,128]{1,0:T(8,128)S(1)} %fusion.3), channel_id=1, source_target_pairs={{0,1},{1,0},{2,3},{3,2},{4,5},{5,4},{6,7},{7,6},{8,9},{9,8},{10,11... | collective-permute-start | bytes 196616 | tf_op jit(solution)/shard_map/ppermute | solution.py:238
  21.9 0.9 collective-permute-done
  22.8 2.2 %collective-permute-start.1 = (f32[128,128]{1,0:T(8,128)S(1)}, f32[128,128]{1,0:T(8,128)S(1)}, u32[]{:S(2)}, u32[]{:S(2)}) collective-permute-start(f32[128,128]{1,0:T(8,128)S(1)} %add.29), channel_id=1, source_target_pairs={{0,16},{1,17},{2,18},{3,19},{4,20},{5,21},{6,22},{7,23},{8,24},{9,... | collective-permute-start | bytes 196616 | tf_op jit(solution)/shard_map/ppermute | solution.py:238
  25.0 3.1 %collective-permute-done.1 = f32[128,128]{1,0:T(8,128)S(1)} collective-permute-done((f32[128,128]{1,0:T(8,128)S(1)}, f32[128,128]{1,0:T(8,128)S(1)}, u32[]{:S(2)}, u32[]{:S(2)}) %collective-permute-start.1) | collective-permute-done | bytes 65568 | tf_op jit(solution)/shard_map/ppermute | solution.py:238
  28.1 3.2 %collective-permute-start.2 = (f32[128,128]{1,0:T(8,128)S(1)}, f32[128,128]{1,0:T(8,128)S(1)}, u32[]{:S(2)}, u32[]{:S(2)}) collective-permute-start(f32[128,128]{1,0:T(8,128)S(1)} %add.30), channel_id=1, source_target_pairs={{0,2},{1,3},{2,0},{3,1},{4,6},{5,7},{6,4},{7,5},{8,10},{9,11},{10,... | collective-permute-start | bytes 196616 | tf_op jit(solution)/shard_map/ppermute | solution.py:238
  31.3 2.1 %collective-permute-done.2 = f32[128,128]{1,0:T(8,128)S(1)} collective-permute-done((f32[128,128]{1,0:T(8,128)S(1)}, f32[128,128]{1,0:T(8,128)S(1)}, u32[]{:S(2)}, u32[]{:S(2)}) %collective-permute-start.2) | collective-permute-done | bytes 65568 | tf_op jit(solution)/shard_map/ppermute | solution.py:238
  33.5 4.2 %collective-permute-start.3 = (f32[128,128]{1,0:T(8,128)S(1)}, f32[128,128]{1,0:T(8,128)S(1)}, u32[]{:S(2)}, u32[]{:S(2)}) collective-permute-start(f32[128,128]{1,0:T(8,128)S(1)} %add.31), channel_id=1, source_target_pairs={{0,4},{1,5},{2,6},{3,7},{4,0},{5,1},{6,2},{7,3},{8,12},{9,13},{10,... | collective-permute-start | bytes 196616 | tf_op jit(solution)/shard_map/ppermute | solution.py:238
  37.7 0.0 copy-done.1
  37.7 0.6 fusion.2
  42.1 0.0 copy-done
  42.2 0.1 dynamic-slice.2
  42.2 0.0 collective-permute-done.3
  42.3 5.7 %collective-permute-start.4 = (f32[128,128]{1,0:T(8,128)S(1)}, f32[128,128]{1,0:T(8,128)S(1)}, u32[]{:S(2)}, u32[]{:S(2)}) collective-permute-start(f32[128,128]{1,0:T(8,128)S(1)} %add.32), channel_id=1, source_target_pairs={{0,8},{1,9},{2,10},{3,11},{4,12},{5,13},{6,14},{7,15},{8,0},{9,1},... | collective-permute-start | bytes 196616 | tf_op jit(solution)/shard_map/ppermute | solution.py:238
  47.9 0.1 pad_add_fusion.flags_ref
  48.0 3.5 %collective-permute-done.4 = f32[128,128]{1,0:T(8,128)S(1)} collective-permute-done((f32[128,128]{1,0:T(8,128)S(1)}, f32[128,128]{1,0:T(8,128)S(1)}, u32[]{:S(2)}, u32[]{:S(2)}) %collective-permute-start.4) | collective-permute-done | bytes 65568 | tf_op jit(solution)/shard_map/ppermute | solution.py:238
  51.5 0.1 fusion.strip_ref
  51.5 14.3 %all-to-all-done.pieces_ref = bf16[16,128,512]{2,1,0:T(8,128)(2,1)S(1)} async-done(((bf16[16,128,512]{2,1,0:T(8,128)(2,1)}), bf16[16,128,512]{2,1,0:T(8,128)(2,1)S(1)}, u32[]{:S(2)}, u32[]{:S(2)}) %all-to-all-start) | async-done | bytes 2097184 | tf_op jit(solution)/shard_map/all_to_all | solution.py:250
  65.8 0.7 shard_map.39
  66.6 5.2 %collective-permute-start.5 = (f32[16,16,8,128]{3,2,1,0:T(8,128)S(1)}, f32[16,16,8,128]{3,2,1,0:T(8,128)S(1)}, u32[]{:S(2)}, u32[]{:S(2)}) collective-permute-start(f32[16,16,8,128]{3,2,1,0:T(8,128)S(1)} %shard_map.39), channel_id=1, source_target_pairs={{0,1},{1,0},{2,3},{3,2},{4,5},{5,4},{6,7},{7,6},{8,9},{9,8},{10,11... | collective-permute-start | bytes 3145736 | tf_op jit(solution)/shard_map/ppermute | solution.py:238
  71.7 0.7 shard_map.38.mine_ref
  72.4 1.6 %collective-permute-done.5.theirs_ref = f32[16,16,8,128]{3,2,1,0:T(8,128)S(1)} collective-permute-done((f32[16,16,8,128]{3,2,1,0:T(8,128)S(1)}, f32[16,16,8,128]{3,2,1,0:T(8,128)S(1)}, u32[]{:S(2)}, u32[]{:S(2)}) %collective-permute-start.5) | collective-permute-done | bytes 1048608 | tf_op jit(solution)/shard_map/ppermute | solution.py:238
  74.0 1.2 shard_map.40
  75.2 7.0 %all-to-all-start.1 = ((f32[16,17,8,128]{3,2,1,0:T(8,128)}), f32[16,17,8,128]{3,2,1,0:T(8,128)S(1)}, u32[]{:S(2)}, u32[]{:S(2)}) async-start(f32[16,17,8,128]{3,2,1,0:T(8,128)} %shard_map.40), calls=%async_computation.1 | async-start | bytes 2228224 | tf_op jit(solution)/shard_map/all_to_all | solution.py:267
  86.0 12.8 %all-to-all-done.1 = f32[16,17,8,128]{3,2,1,0:T(8,128)S(1)} async-done(((f32[16,17,8,128]{3,2,1,0:T(8,128)}), f32[16,17,8,128]{3,2,1,0:T(8,128)S(1)}, u32[]{:S(2)}, u32[]{:S(2)}) %all-to-all-start.1) | async-done | bytes 1114144 | tf_op jit(solution)/shard_map/all_to_all | solution.py:267
  98.8 0.1 slice_reduce_fusion
  98.9 14.8 %all_to_all.20 = f32[16,2,8,128]{3,2,1,0:T(8,128)S(1)} all-to-all(f32[16,2,8,128]{3,2,1,0:T(8,128)S(1)} %pad_maximum_fusion), channel_id=1, replica_groups={{1,33,65,97,129,161,193,225,257,289,321,353,385,417,449,481},{3,35,67,9..., dimensions={0} | all-to-all | bytes 262144 | tf_op jit(solution)/shard_map/all_to_all | solution.py:277
  113.8 0.7 broadcast_in_dim.20
  114.4 4.2 %all-to-all-start.3 = ((f32[16,2,8,128]{3,2,1,0:T(8,128)}), f32[16,2,8,128]{3,2,1,0:T(8,128)S(1)}, u32[]{:S(2)}, u32[]{:S(2)}) async-start(f32[16,2,8,128]{3,2,1,0:T(8,128)} %broadcast_in_dim.20), calls=%async_computation.3 | async-start | bytes 262144 | tf_op jit(solution)/shard_map/all_to_all | solution.py:283
  118.7 6.3 %collective-permute-start.6 = (f32[128,128]{1,0:T(8,128)S(1)}, f32[128,128]{1,0:T(8,128)S(1)}, u32[]{:S(2)}, u32[]{:S(2)}) collective-permute-start(f32[128,128]{1,0:T(8,128)S(1)} %shard_map.41.inverse_ref), channel_id=1, source_target_pairs={{0,1},{1,0},{2,3},{3,2},{4,5},{5,4},{6,7},{7,6},{8,9},{9,8},{10,11... | collective-permute-start | bytes 196616 | tf_op jit(solution)/shard_map/ppermute | solution.py:238
  125.0 0.9 collective-permute-done.6.their_inverse_ref
  125.9 0.3 all-to-all-done.3.mine_ref
  126.2 4.2 %collective-permute-start.7 = (f32[16,2,8,128]{3,2,1,0:T(8,128)S(1)}, f32[16,2,8,128]{3,2,1,0:T(8,128)S(1)}, u32[]{:S(2)}, u32[]{:S(2)}) collective-permute-start(f32[16,2,8,128]{3,2,1,0:T(8,128)S(1)} %all-to-all-done.3.mine_ref), channel_id=1, source_target_pairs={{0,1},{1,0},{2,3},{3,2},{4,5},{5,4},{6,7},{7,6},{8,9},{9,8},{10,11... | collective-permute-start | bytes 393224 | tf_op jit(solution)/shard_map/ppermute | solution.py:238
  130.4 1.0 collective-permute-done.7.theirs_ref
  131.4 5.2 %shard_map.42 = f32[128,256]{1,0:T(8,128)} custom-call(s32[3]{0:T(128)S(1)} %pad_add_fusion.flags_ref, f32[16,2,8,128]{3,2,1,0:T(8,128)S(1)} %all-to-all-done.3.mine_ref, f32[16,2,8,128]{3,2,1,0:T(8,128)S(1)} %collective-permute-done.7.theirs_ref, f32[1,128]{1,0:T(1,128)S(1)} %bitcast.21, f32[128,128]{1,0:T(8,128)S(1)} %shard_map.41.inverse_ref, ...), custom_call_target="tpu_custom_call" | custom-call | flops 67108864 | bytes 1048576 | tf_op jit(solution)/shard_map/pallas_call | solution.py:227
  (13 shorter events, 0.1 us)
Async XLA Ops:
  2.6 63.2 %all-to-all-start = ((bf16[16,128,512]{2,1,0:T(8,128)(2,1)}), bf16[16,128,512]{2,1,0:T(8,128)(2,1)S(1)}, u32[]{:S(2)}, u32[]{:S(2)}) async-start(bf16[16,128,512]{2,1,0:T(8,128)(2,1)} %shard_map.37), calls=%async_computation | async-start | bytes 4194304 | tf_op jit(solution)/shard_map/all_to_all | solution.py:250
  16.1 21.6 %copy-start.1 = (s32[16]{0:T(128)S(1)}, s32[16]{0:T(128)}, u32[]{:S(2)}) copy-start(s32[16]{0:T(128)} %param.5) | copy-start | bytes 196
  16.1 26.1 %copy-start = (f32[128]{0:T(128)S(1)}, f32[128]{0:T(128)}, u32[]{:S(2)}) copy-start(f32[128]{0:T(128)} %param.4) | copy-start | bytes 1540
  19.0 3.8 %collective-permute-start = (f32[128,128]{1,0:T(8,128)S(1)}, f32[128,128]{1,0:T(8,128)S(1)}, u32[]{:S(2)}, u32[]{:S(2)}) collective-permute-start(f32[128,128]{1,0:T(8,128)S(1)} %fusion.3), channel_id=1, source_target_pairs={{0,1},{1,0},{2,3},{3,2},{4,5},{5,4},{6,7},{7,6},{8,9},{9,8},{10,11... | collective-permute-start | bytes 196616 | tf_op jit(solution)/shard_map/ppermute | solution.py:238
  22.8 5.3 %collective-permute-start.1 = (f32[128,128]{1,0:T(8,128)S(1)}, f32[128,128]{1,0:T(8,128)S(1)}, u32[]{:S(2)}, u32[]{:S(2)}) collective-permute-start(f32[128,128]{1,0:T(8,128)S(1)} %add.29), channel_id=1, source_target_pairs={{0,16},{1,17},{2,18},{3,19},{4,20},{5,21},{6,22},{7,23},{8,24},{9,... | collective-permute-start | bytes 196616 | tf_op jit(solution)/shard_map/ppermute | solution.py:238
  28.1 5.3 %collective-permute-start.2 = (f32[128,128]{1,0:T(8,128)S(1)}, f32[128,128]{1,0:T(8,128)S(1)}, u32[]{:S(2)}, u32[]{:S(2)}) collective-permute-start(f32[128,128]{1,0:T(8,128)S(1)} %add.30), channel_id=1, source_target_pairs={{0,2},{1,3},{2,0},{3,1},{4,6},{5,7},{6,4},{7,5},{8,10},{9,11},{10,... | collective-permute-start | bytes 196616 | tf_op jit(solution)/shard_map/ppermute | solution.py:238
  33.5 8.8 %collective-permute-start.3 = (f32[128,128]{1,0:T(8,128)S(1)}, f32[128,128]{1,0:T(8,128)S(1)}, u32[]{:S(2)}, u32[]{:S(2)}) collective-permute-start(f32[128,128]{1,0:T(8,128)S(1)} %add.31), channel_id=1, source_target_pairs={{0,4},{1,5},{2,6},{3,7},{4,0},{5,1},{6,2},{7,3},{8,12},{9,13},{10,... | collective-permute-start | bytes 196616 | tf_op jit(solution)/shard_map/ppermute | solution.py:238
  42.3 9.2 %collective-permute-start.4 = (f32[128,128]{1,0:T(8,128)S(1)}, f32[128,128]{1,0:T(8,128)S(1)}, u32[]{:S(2)}, u32[]{:S(2)}) collective-permute-start(f32[128,128]{1,0:T(8,128)S(1)} %add.32), channel_id=1, source_target_pairs={{0,8},{1,9},{2,10},{3,11},{4,12},{5,13},{6,14},{7,15},{8,0},{9,1},... | collective-permute-start | bytes 196616 | tf_op jit(solution)/shard_map/ppermute | solution.py:238
  66.6 7.4 %collective-permute-start.5 = (f32[16,16,8,128]{3,2,1,0:T(8,128)S(1)}, f32[16,16,8,128]{3,2,1,0:T(8,128)S(1)}, u32[]{:S(2)}, u32[]{:S(2)}) collective-permute-start(f32[16,16,8,128]{3,2,1,0:T(8,128)S(1)} %shard_map.39), channel_id=1, source_target_pairs={{0,1},{1,0},{2,3},{3,2},{4,5},{5,4},{6,7},{7,6},{8,9},{9,8},{10,11... | collective-permute-start | bytes 3145736 | tf_op jit(solution)/shard_map/ppermute | solution.py:238
  75.2 23.6 %all-to-all-start.1 = ((f32[16,17,8,128]{3,2,1,0:T(8,128)}), f32[16,17,8,128]{3,2,1,0:T(8,128)S(1)}, u32[]{:S(2)}, u32[]{:S(2)}) async-start(f32[16,17,8,128]{3,2,1,0:T(8,128)} %shard_map.40), calls=%async_computation.1 | async-start | bytes 2228224 | tf_op jit(solution)/shard_map/all_to_all | solution.py:267
  114.4 11.8 %all-to-all-start.3 = ((f32[16,2,8,128]{3,2,1,0:T(8,128)}), f32[16,2,8,128]{3,2,1,0:T(8,128)S(1)}, u32[]{:S(2)}, u32[]{:S(2)}) async-start(f32[16,2,8,128]{3,2,1,0:T(8,128)} %broadcast_in_dim.20), calls=%async_computation.3 | async-start | bytes 262144 | tf_op jit(solution)/shard_map/all_to_all | solution.py:283
  118.7 7.2 %collective-permute-start.6 = (f32[128,128]{1,0:T(8,128)S(1)}, f32[128,128]{1,0:T(8,128)S(1)}, u32[]{:S(2)}, u32[]{:S(2)}) collective-permute-start(f32[128,128]{1,0:T(8,128)S(1)} %shard_map.41.inverse_ref), channel_id=1, source_target_pairs={{0,1},{1,0},{2,3},{3,2},{4,5},{5,4},{6,7},{7,6},{8,9},{9,8},{10,11... | collective-permute-start | bytes 196616 | tf_op jit(solution)/shard_map/ppermute | solution.py:238
  126.2 5.2 %collective-permute-start.7 = (f32[16,2,8,128]{3,2,1,0:T(8,128)S(1)}, f32[16,2,8,128]{3,2,1,0:T(8,128)S(1)}, u32[]{:S(2)}, u32[]{:S(2)}) collective-permute-start(f32[16,2,8,128]{3,2,1,0:T(8,128)S(1)} %all-to-all-done.3.mine_ref), channel_id=1, source_target_pairs={{0,1},{1,0},{2,3},{3,2},{4,5},{5,4},{6,7},{7,6},{8,9},{9,8},{10,11... | collective-permute-start | bytes 393224 | tf_op jit(solution)/shard_map/ppermute | solution.py:238

commit v12 on v11

--- a/solution.py
+++ b/solution.py
@@ -252,7 +252,7 @@
     square = lax.dot_general(
         samples, samples, (((1,), (1,)), ((), ())), preferred_element_type=jnp.float32
     )
-    for bit in (1, 16, 2, 4, 8):
+    for bit in (1, 16, 2, 6, 14):
         square = square + flip(square, bit)
     square = square + jnp.eye(ROWS, dtype=jnp.float32) * shift[:, None]
     strip = lax.dynamic_slice_in_dim(square, chip * TILE, TILE, 0)

time: 137 us -> 137 us (level)
  no operation moved by 1% of the time
where the time goes in v12:
time: 137 us
  starting transfers between devices  58.2 us (42%)
  waiting for transfers between devices  40.6 us (30%)
  blocking collectives  14.8 us (11%)
  Pallas kernels  10.4 us (8%)
  between operations  7.95 us (6%)
  matrix products  2.93 us (2%)
  local copies, waits for them, and re-layouts  1.38 us (1%)
    ppermute x8, starting transfers between devices, flip(): return lax.ppermute(block, 'par', [(i, i ^ bit) for i in range(PAR)])  33.6 us
    all_to_all x1, waiting for transfers between devices, per_device(): pieces = lax.all_to_all(cut(samples), 'samp', 0, 0, tiled=True)  15.4 us
    all_to_all x1, blocking collectives, per_device(): lax.all_to_all(total, axes, 0, 0, axis_index_groups=SAMP_THEN_CHIPS, tile...  14.8 us
    all_to_all x1, starting transfers between devices, per_device(): pieces = lax.all_to_all(cut(samples), 'samp', 0, 0, tiled=True)  13.4 us
    all_to_all x1, waiting for transfers between devices, per_device(): lax.all_to_all(total, axes, 0, 0, axis_index_groups=CHIPS_THEN_SAMP, tile...  12.8 us
    ppermute x8, waiting for transfers between devices, flip(): return lax.ppermute(block, 'par', [(i, i ^ bit) for i in range(PAR)])  12.1 us
    all_to_all x1, starting transfers between devices, per_device(): lax.all_to_all(total, axes, 0, 0, axis_index_groups=CHIPS_THEN_SAMP, tile...  6.97 us
    pallas_call x1, Pallas kernels, last_factor(): pl.pallas_call(last_kernel, out_shape=jax.ShapeDtypeStruct((ROWS, 2 * ROW...  5.18 us
  transfers between devices with their start and end apart: 11, of which 10 were waited for; matrix products, arithmetic and copies ran while one was open for 3% of the time, Pallas kernels for 1%

profile of v12, /device:TPU:1, one launch (start us, length us, event | category | flops | bytes accessed | tf_op | source)
XLA Modules:
  0.0 136.6 jit_solution(7826435903201083554)
XLA Ops:
  0.0 2.6 %shard_map.37 = bf16[16,128,512]{2,1,0:T(8,128)(2,1)} custom-call(bf16[128,8192]{1,0:T(8,128)(2,1)} %samples_ref.1), custom_call_target="tpu_custom_call" | custom-call | bytes 4194304 | tf_op jit(solution)/shard_map/pallas_call | solution.py:107
  2.6 13.4 %all-to-all-start = ((bf16[16,128,512]{2,1,0:T(8,128)(2,1)}), bf16[16,128,512]{2,1,0:T(8,128)(2,1)S(1)}, u32[]{:S(2)}, u32[]{:S(2)}) async-start(bf16[16,128,512]{2,1,0:T(8,128)(2,1)} %shard_map.37), calls=%async_computation | async-start | bytes 4194304 | tf_op jit(solution)/shard_map/all_to_all | solution.py:250
  16.1 0.0 copy-start.1
  16.1 0.0 copy-start
  16.1 2.9 %fusion.3 = f32[128,128]{1,0:T(8,128)S(1)} fusion(bf16[128,8192]{1,0:T(8,128)(2,1)} %samples_ref.1), kind=kOutput, calls=%fused_computation.12 | convolution fusion | flops 268435456 | bytes 2162688 | tf_op jit(solution)/shard_map/dot_general | solution.py:252
  19.0 2.9 %collective-permute-start = (f32[128,128]{1,0:T(8,128)S(1)}, f32[128,128]{1,0:T(8,128)S(1)}, u32[]{:S(2)}, u32[]{:S(2)}) collective-permute-start(f32[128,128]{1,0:T(8,128)S(1)} %fusion.3), channel_id=1, source_target_pairs={{0,1},{1,0},{2,3},{3,2},{4,5},{5,4},{6,7},{7,6},{8,9},{9,8},{10,11... | collective-permute-start | bytes 196616 | tf_op jit(solution)/shard_map/ppermute | solution.py:238
  21.9 0.9 collective-permute-done
  22.8 2.2 %collective-permute-start.1 = (f32[128,128]{1,0:T(8,128)S(1)}, f32[128,128]{1,0:T(8,128)S(1)}, u32[]{:S(2)}, u32[]{:S(2)}) collective-permute-start(f32[128,128]{1,0:T(8,128)S(1)} %add.29), channel_id=1, source_target_pairs={{0,16},{1,17},{2,18},{3,19},{4,20},{5,21},{6,22},{7,23},{8,24},{9,... | collective-permute-start | bytes 196616 | tf_op jit(solution)/shard_map/ppermute | solution.py:238
  25.0 3.1 %collective-permute-done.1 = f32[128,128]{1,0:T(8,128)S(1)} collective-permute-done((f32[128,128]{1,0:T(8,128)S(1)}, f32[128,128]{1,0:T(8,128)S(1)}, u32[]{:S(2)}, u32[]{:S(2)}) %collective-permute-start.1) | collective-permute-done | bytes 65568 | tf_op jit(solution)/shard_map/ppermute | solution.py:238
  28.1 3.2 %collective-permute-start.2 = (f32[128,128]{1,0:T(8,128)S(1)}, f32[128,128]{1,0:T(8,128)S(1)}, u32[]{:S(2)}, u32[]{:S(2)}) collective-permute-start(f32[128,128]{1,0:T(8,128)S(1)} %add.30), channel_id=1, source_target_pairs={{0,2},{1,3},{2,0},{3,1},{4,6},{5,7},{6,4},{7,5},{8,10},{9,11},{10,... | collective-permute-start | bytes 196616 | tf_op jit(solution)/shard_map/ppermute | solution.py:238
  31.3 2.1 %collective-permute-done.2 = f32[128,128]{1,0:T(8,128)S(1)} collective-permute-done((f32[128,128]{1,0:T(8,128)S(1)}, f32[128,128]{1,0:T(8,128)S(1)}, u32[]{:S(2)}, u32[]{:S(2)}) %collective-permute-start.2) | collective-permute-done | bytes 65568 | tf_op jit(solution)/shard_map/ppermute | solution.py:238
  33.5 5.2 %collective-permute-start.3 = (f32[128,128]{1,0:T(8,128)S(1)}, f32[128,128]{1,0:T(8,128)S(1)}, u32[]{:S(2)}, u32[]{:S(2)}) collective-permute-start(f32[128,128]{1,0:T(8,128)S(1)} %add.31), channel_id=1, source_target_pairs={{0,6},{1,7},{2,4},{3,5},{4,2},{5,3},{6,0},{7,1},{8,14},{9,15},{10,... | collective-permute-start | bytes 196616 | tf_op jit(solution)/shard_map/ppermute | solution.py:238
  38.7 0.0 copy-done.1
  38.7 0.6 fusion.2
  43.2 0.0 copy-done
  43.2 0.1 dynamic-slice.2
  43.2 0.0 collective-permute-done.3
  43.3 4.4 %collective-permute-start.4 = (f32[128,128]{1,0:T(8,128)S(1)}, f32[128,128]{1,0:T(8,128)S(1)}, u32[]{:S(2)}, u32[]{:S(2)}) collective-permute-start(f32[128,128]{1,0:T(8,128)S(1)} %add.32), channel_id=1, source_target_pairs={{0,14},{1,15},{2,12},{3,13},{4,10},{5,11},{6,8},{7,9},{8,6},{9,7},... | collective-permute-start | bytes 196616 | tf_op jit(solution)/shard_map/ppermute | solution.py:238
  47.7 0.1 pad_add_fusion.flags_ref
  47.8 2.6 %collective-permute-done.4 = f32[128,128]{1,0:T(8,128)S(1)} collective-permute-done((f32[128,128]{1,0:T(8,128)S(1)}, f32[128,128]{1,0:T(8,128)S(1)}, u32[]{:S(2)}, u32[]{:S(2)}) %collective-permute-start.4) | collective-permute-done | bytes 65568 | tf_op jit(solution)/shard_map/ppermute | solution.py:238
  50.4 0.1 fusion.strip_ref
  50.4 15.4 %all-to-all-done.pieces_ref = bf16[16,128,512]{2,1,0:T(8,128)(2,1)S(1)} async-done(((bf16[16,128,512]{2,1,0:T(8,128)(2,1)}), bf16[16,128,512]{2,1,0:T(8,128)(2,1)S(1)}, u32[]{:S(2)}, u32[]{:S(2)}) %all-to-all-start) | async-done | bytes 2097184 | tf_op jit(solution)/shard_map/all_to_all | solution.py:250
  65.8 0.7 shard_map.39
  66.6 5.2 %collective-permute-start.5 = (f32[16,16,8,128]{3,2,1,0:T(8,128)S(1)}, f32[16,16,8,128]{3,2,1,0:T(8,128)S(1)}, u32[]{:S(2)}, u32[]{:S(2)}) collective-permute-start(f32[16,16,8,128]{3,2,1,0:T(8,128)S(1)} %shard_map.39), channel_id=1, source_target_pairs={{0,1},{1,0},{2,3},{3,2},{4,5},{5,4},{6,7},{7,6},{8,9},{9,8},{10,11... | collective-permute-start | bytes 3145736 | tf_op jit(solution)/shard_map/ppermute | solution.py:238
  71.7 0.7 shard_map.38.mine_ref
  72.4 1.6 %collective-permute-done.5.theirs_ref = f32[16,16,8,128]{3,2,1,0:T(8,128)S(1)} collective-permute-done((f32[16,16,8,128]{3,2,1,0:T(8,128)S(1)}, f32[16,16,8,128]{3,2,1,0:T(8,128)S(1)}, u32[]{:S(2)}, u32[]{:S(2)}) %collective-permute-start.5) | collective-permute-done | bytes 1048608 | tf_op jit(solution)/shard_map/ppermute | solution.py:238
  74.0 1.2 shard_map.40
  75.2 7.0 %all-to-all-start.1 = ((f32[16,17,8,128]{3,2,1,0:T(8,128)}), f32[16,17,8,128]{3,2,1,0:T(8,128)S(1)}, u32[]{:S(2)}, u32[]{:S(2)}) async-start(f32[16,17,8,128]{3,2,1,0:T(8,128)} %shard_map.40), calls=%async_computation.1 | async-start | bytes 2228224 | tf_op jit(solution)/shard_map/all_to_all | solution.py:267
  86.0 12.8 %all-to-all-done.1 = f32[16,17,8,128]{3,2,1,0:T(8,128)S(1)} async-done(((f32[16,17,8,128]{3,2,1,0:T(8,128)}), f32[16,17,8,128]{3,2,1,0:T(8,128)S(1)}, u32[]{:S(2)}, u32[]{:S(2)}) %all-to-all-start.1) | async-done | bytes 1114144 | tf_op jit(solution)/shard_map/all_to_all | solution.py:267
  98.8 0.1 slice_reduce_fusion
  98.9 14.8 %all_to_all.20 = f32[16,2,8,128]{3,2,1,0:T(8,128)S(1)} all-to-all(f32[16,2,8,128]{3,2,1,0:T(8,128)S(1)} %pad_maximum_fusion), channel_id=1, replica_groups={{1,33,65,97,129,161,193,225,257,289,321,353,385,417,449,481},{3,35,67,9..., dimensions={0} | all-to-all | bytes 262144 | tf_op jit(solution)/shard_map/all_to_all | solution.py:277
  113.8 0.7 broadcast_in_dim.20
  114.4 4.2 %all-to-all-start.3 = ((f32[16,2,8,128]{3,2,1,0:T(8,128)}), f32[16,2,8,128]{3,2,1,0:T(8,128)S(1)}, u32[]{:S(2)}, u32[]{:S(2)}) async-start(f32[16,2,8,128]{3,2,1,0:T(8,128)} %broadcast_in_dim.20), calls=%async_computation.3 | async-start | bytes 262144 | tf_op jit(solution)/shard_map/all_to_all | solution.py:283
  118.7 6.3 %collective-permute-start.6 = (f32[128,128]{1,0:T(8,128)S(1)}, f32[128,128]{1,0:T(8,128)S(1)}, u32[]{:S(2)}, u32[]{:S(2)}) collective-permute-start(f32[128,128]{1,0:T(8,128)S(1)} %shard_map.41.inverse_ref), channel_id=1, source_target_pairs={{0,1},{1,0},{2,3},{3,2},{4,5},{5,4},{6,7},{7,6},{8,9},{9,8},{10,11... | collective-permute-start | bytes 196616 | tf_op jit(solution)/shard_map/ppermute | solution.py:238
  125.0 0.9 collective-permute-done.6.their_inverse_ref
  125.9 0.3 all-to-all-done.3.mine_ref
  126.2 4.2 %collective-permute-start.7 = (f32[16,2,8,128]{3,2,1,0:T(8,128)S(1)}, f32[16,2,8,128]{3,2,1,0:T(8,128)S(1)}, u32[]{:S(2)}, u32[]{:S(2)}) collective-permute-start(f32[16,2,8,128]{3,2,1,0:T(8,128)S(1)} %all-to-all-done.3.mine_ref), channel_id=1, source_target_pairs={{0,1},{1,0},{2,3},{3,2},{4,5},{5,4},{6,7},{7,6},{8,9},{9,8},{10,11... | collective-permute-start | bytes 393224 | tf_op jit(solution)/shard_map/ppermute | solution.py:238
  130.4 1.0 collective-permute-done.7.theirs_ref
  131.4 5.2 %shard_map.42 = f32[128,256]{1,0:T(8,128)} custom-call(s32[3]{0:T(128)S(1)} %pad_add_fusion.flags_ref, f32[16,2,8,128]{3,2,1,0:T(8,128)S(1)} %all-to-all-done.3.mine_ref, f32[16,2,8,128]{3,2,1,0:T(8,128)S(1)} %collective-permute-done.7.theirs_ref, f32[1,128]{1,0:T(1,128)S(1)} %bitcast.21, f32[128,128]{1,0:T(8,128)S(1)} %shard_map.41.inverse_ref, ...), custom_call_target="tpu_custom_call" | custom-call | flops 67108864 | bytes 1048576 | tf_op jit(solution)/shard_map/pallas_call | solution.py:227
  (13 shorter events, 0.1 us)
Async XLA Ops:
  2.6 63.2 %all-to-all-start = ((bf16[16,128,512]{2,1,0:T(8,128)(2,1)}), bf16[16,128,512]{2,1,0:T(8,128)(2,1)S(1)}, u32[]{:S(2)}, u32[]{:S(2)}) async-start(bf16[16,128,512]{2,1,0:T(8,128)(2,1)} %shard_map.37), calls=%async_computation | async-start | bytes 4194304 | tf_op jit(solution)/shard_map/all_to_all | solution.py:250
  16.1 22.6 %copy-start.1 = (s32[16]{0:T(128)S(1)}, s32[16]{0:T(128)}, u32[]{:S(2)}) copy-start(s32[16]{0:T(128)} %param.5) | copy-start | bytes 196
  16.1 27.1 %copy-start = (f32[128]{0:T(128)S(1)}, f32[128]{0:T(128)}, u32[]{:S(2)}) copy-start(f32[128]{0:T(128)} %param.4) | copy-start | bytes 1540
  19.0 3.8 %collective-permute-start = (f32[128,128]{1,0:T(8,128)S(1)}, f32[128,128]{1,0:T(8,128)S(1)}, u32[]{:S(2)}, u32[]{:S(2)}) collective-permute-start(f32[128,128]{1,0:T(8,128)S(1)} %fusion.3), channel_id=1, source_target_pairs={{0,1},{1,0},{2,3},{3,2},{4,5},{5,4},{6,7},{7,6},{8,9},{9,8},{10,11... | collective-permute-start | bytes 196616 | tf_op jit(solution)/shard_map/ppermute | solution.py:238
  22.8 5.3 %collective-permute-start.1 = (f32[128,128]{1,0:T(8,128)S(1)}, f32[128,128]{1,0:T(8,128)S(1)}, u32[]{:S(2)}, u32[]{:S(2)}) collective-permute-start(f32[128,128]{1,0:T(8,128)S(1)} %add.29), channel_id=1, source_target_pairs={{0,16},{1,17},{2,18},{3,19},{4,20},{5,21},{6,22},{7,23},{8,24},{9,... | collective-permute-start | bytes 196616 | tf_op jit(solution)/shard_map/ppermute | solution.py:238
  28.1 5.3 %collective-permute-start.2 = (f32[128,128]{1,0:T(8,128)S(1)}, f32[128,128]{1,0:T(8,128)S(1)}, u32[]{:S(2)}, u32[]{:S(2)}) collective-permute-start(f32[128,128]{1,0:T(8,128)S(1)} %add.30), channel_id=1, source_target_pairs={{0,2},{1,3},{2,0},{3,1},{4,6},{5,7},{6,4},{7,5},{8,10},{9,11},{10,... | collective-permute-start | bytes 196616 | tf_op jit(solution)/shard_map/ppermute | solution.py:238
  33.5 9.8 %collective-permute-start.3 = (f32[128,128]{1,0:T(8,128)S(1)}, f32[128,128]{1,0:T(8,128)S(1)}, u32[]{:S(2)}, u32[]{:S(2)}) collective-permute-start(f32[128,128]{1,0:T(8,128)S(1)} %add.31), channel_id=1, source_target_pairs={{0,6},{1,7},{2,4},{3,5},{4,2},{5,3},{6,0},{7,1},{8,14},{9,15},{10,... | collective-permute-start | bytes 196616 | tf_op jit(solution)/shard_map/ppermute | solution.py:238
  43.3 7.1 %collective-permute-start.4 = (f32[128,128]{1,0:T(8,128)S(1)}, f32[128,128]{1,0:T(8,128)S(1)}, u32[]{:S(2)}, u32[]{:S(2)}) collective-permute-start(f32[128,128]{1,0:T(8,128)S(1)} %add.32), channel_id=1, source_target_pairs={{0,14},{1,15},{2,12},{3,13},{4,10},{5,11},{6,8},{7,9},{8,6},{9,7},... | collective-permute-start | bytes 196616 | tf_op jit(solution)/shard_map/ppermute | solution.py:238
  66.6 7.4 %collective-permute-start.5 = (f32[16,16,8,128]{3,2,1,0:T(8,128)S(1)}, f32[16,16,8,128]{3,2,1,0:T(8,128)S(1)}, u32[]{:S(2)}, u32[]{:S(2)}) collective-permute-start(f32[16,16,8,128]{3,2,1,0:T(8,128)S(1)} %shard_map.39), channel_id=1, source_target_pairs={{0,1},{1,0},{2,3},{3,2},{4,5},{5,4},{6,7},{7,6},{8,9},{9,8},{10,11... | collective-permute-start | bytes 3145736 | tf_op jit(solution)/shard_map/ppermute | solution.py:238
  75.2 23.6 %all-to-all-start.1 = ((f32[16,17,8,128]{3,2,1,0:T(8,128)}), f32[16,17,8,128]{3,2,1,0:T(8,128)S(1)}, u32[]{:S(2)}, u32[]{:S(2)}) async-start(f32[16,17,8,128]{3,2,1,0:T(8,128)} %shard_map.40), calls=%async_computation.1 | async-start | bytes 2228224 | tf_op jit(solution)/shard_map/all_to_all | solution.py:267
  114.4 11.8 %all-to-all-start.3 = ((f32[16,2,8,128]{3,2,1,0:T(8,128)}), f32[16,2,8,128]{3,2,1,0:T(8,128)S(1)}, u32[]{:S(2)}, u32[]{:S(2)}) async-start(f32[16,2,8,128]{3,2,1,0:T(8,128)} %broadcast_in_dim.20), calls=%async_computation.3 | async-start | bytes 262144 | tf_op jit(solution)/shard_map/all_to_all | solution.py:283
  118.7 7.2 %collective-permute-start.6 = (f32[128,128]{1,0:T(8,128)S(1)}, f32[128,128]{1,0:T(8,128)S(1)}, u32[]{:S(2)}, u32[]{:S(2)}) collective-permute-start(f32[128,128]{1,0:T(8,128)S(1)} %shard_map.41.inverse_ref), channel_id=1, source_target_pairs={{0,1},{1,0},{2,3},{3,2},{4,5},{5,4},{6,7},{7,6},{8,9},{9,8},{10,11... | collective-permute-start | bytes 196616 | tf_op jit(solution)/shard_map/ppermute | solution.py:238
  126.2 5.2 %collective-permute-start.7 = (f32[16,2,8,128]{3,2,1,0:T(8,128)S(1)}, f32[16,2,8,128]{3,2,1,0:T(8,128)S(1)}, u32[]{:S(2)}, u32[]{:S(2)}) collective-permute-start(f32[16,2,8,128]{3,2,1,0:T(8,128)S(1)} %all-to-all-done.3.mine_ref), channel_id=1, source_target_pairs={{0,1},{1,0},{2,3},{3,2},{4,5},{5,4},{6,7},{7,6},{8,9},{9,8},{10,11... | collective-permute-start | bytes 393224 | tf_op jit(solution)/shard_map/ppermute | solution.py:238
